TPU v7x, 32 devices: a whole 2x2x4 slice. The times are simulated.
32 devices in a mesh: group: 2 (over y), tm: 4 (over z), space: 2 (over x), layer: 2 (over core).
Axes of the slice: x: 2, y: 2, z: 4, core: 2. Of those that a mesh axis runs over, the one named last changes fastest.
Arguments:
- state_guess: float32 [16, 64, 16, 128], P('tm', ('group', 'layer'), 'space'), parts along dimension 1, may hold values from -2.5 to 2.5
- start_state: float32 [64, 16, 128], P(('group', 'layer'), 'space'), parts along dimension 0, may hold values from -2.5 to 2.5
- reaction: float32 [64, 16, 128], P(('group', 'layer'), 'space'), parts along dimension 0, may hold values from 0.02 to 0.2
- source: float32 [64, 16, 128], P(('group', 'layer'), 'space'), parts along dimension 0, may hold values from -4 to 4
- self_diag: float32 [16, 128], P('space'), may hold values from 1 to 3
- tiles: bfloat16 [16, 7, 128, 128], P('space'), may hold values from -0.125 to 0.125
- neighbors: int32 [16, 4], P('space'), may hold values from 0 to 15, as said below
Outputs:
- new_state: float32 [16, 64, 16, 128], P('tm', ('group', 'layer'), 'space'), parts along dimension 1
There are 2 independent parts, one for each index of `group`. A program takes and returns all parts, laid end to end along the dimension named above; an argument that names none is the same for every part. Nothing has to cross between parts.
Inputs may be any that keep to these rules, and one draw needn't show every extreme that they name: `neighbors`: row e holds the four elements e - 2, e - 1, e + 1 and e + 2 modulo 16, in an order drawn for each row.
All inputs are finite; a program needn't handle non-finite values.
Results may differ from a plain program's by a relative error of at most 0.0063.
Values may be sent and summed in bfloat16 or wider, within the bound.
No kernel may reach another device: no remote copies, remote signals or barrier semaphores. Data moves between devices by JAX's collectives and lax.ppermute only.
A program may use at most 64 MiB of HBM per device.

v0:
```python
import math

import jax
import jax.numpy as jnp
from jax import lax
from jax.sharding import PartitionSpec as P

HALO = 2
NEWTON = 2


corner_weight = 0.25


def padded(block, sides, width, periodic):
    for axis, dim in sides:
        count = lax.axis_size(axis)
        forward = [(i, i + 1) for i in range(count - 1)]
        if periodic:
            forward.append((count - 1, 0))
        backward = [(target, source) for source, target in forward]
        low = lax.ppermute(
            lax.slice_in_dim(block, block.shape[dim] - width, None, axis=dim), axis, forward
        )
        high = lax.ppermute(lax.slice_in_dim(block, 0, width, axis=dim), axis, backward)
        block = jnp.concatenate([low, block, high], axis=dim)
    return block


def passed_along(array, axis, by):
    devices = lax.axis_size(axis)
    pairs = [(i, i + by) for i in range(devices) if 0 <= i + by < devices]
    return lax.ppermute(array, axis, pairs)


def transform_tables(steps):
    beta = corner_weight ** (1.0 / steps)
    counter = jnp.arange(steps, dtype=jnp.int32)
    product = counter[:, None] * counter[None, :] % steps
    angle = product.astype(jnp.float32) * (2.0 * math.pi / steps)
    times = counter.astype(jnp.float32)
    rising = jnp.power(jnp.float32(beta), times)
    falling = jnp.power(jnp.float32(beta), -times) / steps
    fwd_re = (jnp.cos(angle) * rising[None, :]).astype(jnp.bfloat16)
    fwd_im = (-jnp.sin(angle) * rising[None, :]).astype(jnp.bfloat16)
    back_re = (jnp.cos(angle) * falling[:, None]).astype(jnp.bfloat16)
    back_im = (-jnp.sin(angle) * falling[:, None]).astype(jnp.bfloat16)
    phase = times * (2.0 * math.pi / steps)
    eigen_re = 1.0 - beta * jnp.cos(phase)
    eigen_im = beta * jnp.sin(phase)
    return (fwd_re, fwd_im, back_re, back_im, eigen_re, eigen_im)


def tile_part(rounded, tiles, place, layer_pair):
    wide = padded(rounded, (("space", 2),), HALO, True)
    below, above = layer_pair(rounded)
    picked = [rounded]
    for slot in range(4):
        picked.append(jnp.take(wide, place[:, slot], axis=2))
    picked.append(below)
    picked.append(above)
    stacked = jnp.stack(picked, axis=3)
    return jnp.einsum("rlejp,ejpq->rleq", stacked, tiles, preferred_element_type=jnp.float32)


def layer_rims(rounded):
    wide = padded(rounded, (("layer", 1),), 1, False)
    return (wide[:, :-2], wide[:, 2:])


def divide(num_re, num_im, inverse_re, inverse_im):
    return (inverse_re * num_re - inverse_im * num_im, inverse_im * num_re + inverse_re * num_im)


def inverse_parts(eigen_re, eigen_im, self_diag, jacobian):
    diag_re = eigen_re[:, None, None, None] + self_diag[None, None] + jacobian[None]
    square_im = (eigen_im * eigen_im)[:, None, None, None]
    denom = diag_re * diag_re + square_im
    return (diag_re / denom, -eigen_im[:, None, None, None] / denom)


def shards(state_guess, start_state, reaction, source, self_diag, tiles, neighbors):
    local_steps = state_guess.shape[0]
    local_layers = state_guess.shape[1]
    local_elems = state_guess.shape[2]
    width = state_guess.shape[3]
    time_devices = lax.axis_size("tm")
    time_index = lax.axis_index("tm")
    steps = local_steps * time_devices
    all_elems = local_elems * lax.axis_size("space")
    global_ids = lax.axis_index("space") * local_elems + jnp.arange(local_elems, dtype=jnp.int32)
    half_elems = all_elems // 2
    offsets = (neighbors - global_ids[:, None] + half_elems + all_elems) % all_elems - half_elems
    place = jnp.arange(local_elems, dtype=jnp.int32)[:, None] + offsets + HALO
    fwd_re, fwd_im, back_re, back_im, eigen_re, eigen_im = transform_tables(steps)
    jacobian = 3.0 * reaction * start_state * start_state
    own_re = lax.dynamic_slice_in_dim(eigen_re, time_index * local_steps, local_steps, 0)
    own_im = lax.dynamic_slice_in_dim(eigen_im, time_index * local_steps, local_steps, 0)
    inverse_re, inverse_im = inverse_parts(own_re, own_im, self_diag, jacobian)
    state = state_guess
    for newton_step in range(NEWTON):
        prior = passed_along(state[-1:], "tm", 1)
        first = jnp.where(time_index == 0, start_state[None], prior)
        previous = jnp.concatenate([first, state[:-1]], 0)
        rounded = state.astype(jnp.bfloat16)
        image = self_diag * state + tile_part(rounded, tiles, place, layer_rims)
        residual = state - previous + image + reaction * state * state * state - source
        neg_rhs = (-residual).astype(jnp.bfloat16)
        forward_piece = lax.all_to_all(neg_rhs, "tm", split_axis=1, concat_axis=0, tiled=True)
        part_re = jnp.einsum(
            "kt,tlep->klep", fwd_re, forward_piece, preferred_element_type=jnp.float32
        )
        part_im = jnp.einsum(
            "kt,tlep->klep", fwd_im, forward_piece, preferred_element_type=jnp.float32
        )
        spectrum = lax.all_to_all(
            jnp.stack([part_re.astype(jnp.bfloat16), part_im.astype(jnp.bfloat16)], 1),
            "tm",
            split_axis=0,
            concat_axis=2,
            tiled=True,
        )
        rows, layers_here, linker = (local_steps, local_layers, layer_rims)
        spec_re = spectrum[:, 0].astype(jnp.float32)
        spec_im = spectrum[:, 1].astype(jnp.float32)
        sol_re, sol_im = divide(spec_re, spec_im, inverse_re, inverse_im)
        packed = jnp.stack([sol_re.astype(jnp.bfloat16), sol_im.astype(jnp.bfloat16)], 1)
        flat = packed.reshape(2 * rows, layers_here, local_elems, width)
        applied = tile_part(flat, tiles, place, linker).reshape(
            rows, 2, layers_here, local_elems, width
        )
        sol_re, sol_im = divide(
            spec_re - applied[:, 0], spec_im - applied[:, 1], inverse_re, inverse_im
        )
        final = jnp.stack([sol_re.astype(jnp.bfloat16), sol_im.astype(jnp.bfloat16)], 1)
        piece = lax.all_to_all(final, "tm", split_axis=2, concat_axis=0, tiled=True)
        moved = jnp.einsum(
            "tk,klep->tlep", back_re, piece[:, 0], preferred_element_type=jnp.float32
        )
        moved = moved + jnp.einsum(
            "tk,klep->tlep", back_im, piece[:, 1], preferred_element_type=jnp.float32
        )
        delta = lax.all_to_all(
            moved.astype(jnp.bfloat16), "tm", split_axis=0, concat_axis=1, tiled=True
        )
        state = state + delta.astype(jnp.float32)
    return state


def solution(mesh):
    in_specs = (
        P("tm", ("group", "layer"), "space", None),
        P(("group", "layer"), "space", None),
        P(("group", "layer"), "space", None),
        P(("group", "layer"), "space", None),
        P("space", None),
        P("space", None, None, None),
        P("space", None),
    )
    out_specs = P("tm", ("group", "layer"), "space", None)
    return jax.shard_map(shards, mesh=mesh, in_specs=in_specs, out_specs=out_specs, check_vma=False)
```

profile of v0, /device:TPU:1, one launch (start us, length us, event | category | flops | bytes accessed | tf_op | source)
XLA Modules:
  0.0 184.7 jit_solution(9640470891438229148)
XLA Ops:
  0.0 1.8 bitcast_dynamic-update-slice_fusion.16
  1.8 2.0 %collective-permute-start.1 = (bf16[4,16,2,128]{3,1,0,2:T(8,128)(2,1)S(1)}, bf16[4,16,2,128]{3,1,0,2:T(8,128)(2,1)S(1)}, u32[]{:S(2)}, u32[]{:S(2)}) collective-permute-start(bf16[4,16,2,128]{3,1,0,2:T(8,128)(2,1)S(1)} %get-tuple-element.46), channel_id=1, source_target_pairs={{0,2},{2,0},{1,3},{3,1},{4,6},{6,4},{5,7},{7,5},{8,10},{10,8},{9,1... | collective-permute-start | bytes 98312 | tf_op jit(solution)/shard_map/ppermute | solution.py:22
  4.0 1.3 collective-permute-start.3
  5.3 3.0 %collective-permute-start.4 = (bf16[4,1,8,128]{3,1,0,2:T(2,128)(2,1)S(1)}, bf16[4,1,8,128]{3,1,0,2:T(2,128)(2,1)S(1)}, u32[]{:S(2)}, u32[]{:S(2)}) collective-permute-start(bf16[4,1,8,128]{3,1,0,2:T(2,128)(2,1)S(1)} %get-tuple-element.44), channel_id=1, source_target_pairs={{1,0},{3,2},{5,4},{7,6},{9,8},{11,10},{13,12},{15,14},{17,16},{19,... | collective-permute-start | bytes 24584 | tf_op jit(solution)/shard_map/ppermute | solution.py:25
  9.2 3.5 %collective-permute-start = (f32[1,16,8,128]{3,1,0,2:T(8,128)S(1)}, f32[1,16,8,128]{3,1,0,2:T(8,128)S(1)}, u32[]{:S(2)}, u32[]{:S(2)}) collective-permute-start(f32[1,16,8,128]{3,1,0,2:T(8,128)S(1)} %copy.251), channel_id=1, source_target_pairs={{0,4},{4,8},{8,12},{1,5},{5,9},{9,13},{2,6},{6,10},{10,14},{3,7},{... | collective-permute-start | bytes 196616 | tf_op jit(solution)/shard_map/ppermute | solution.py:33
  16.1 0.9 copy.163
  20.2 1.4 bitcast_dynamic-update-slice_fusion.15
  25.5 1.7 fusion.29
  27.9 3.6 %all-to-all-start = ((bf16[4,16,8,128]{3,0,2,1:T(4,128)(2,1)}), bf16[4,16,8,128]{3,0,2,1:T(4,128)(2,1)S(1)}, u32[]{:S(2)}, u32[]{:S(2)}) async-start(bf16[4,16,8,128]{3,0,2,1:T(4,128)(2,1)} %copy.164), calls=%async_computation | async-start | bytes 262144 | tf_op jit(solution)/shard_map/all_to_all | solution.py:109
  31.6 5.4 %all-to-all-done = bf16[4,16,8,128]{3,0,2,1:T(4,128)(2,1)S(1)} async-done(((bf16[4,16,8,128]{3,0,2,1:T(4,128)(2,1)}), bf16[4,16,8,128]{3,0,2,1:T(4,128)(2,1)S(1)}, u32[]{:S(2)}, u32[]{:S(2)}) %all-to-all-start) | async-done | bytes 131104 | tf_op jit(solution)/shard_map/all_to_all | solution.py:109
  38.3 3.4 %all-to-all-start.1 = ((bf16[16,2,4,8,128]{4,3,2,1,0:T(8,128)(2,1)}), bf16[16,2,4,8,128]{4,3,2,1,0:T(8,128)(2,1)S(1)}, u32[]{:S(2)}, u32[]{:S(2)}) async-start(bf16[16,2,4,8,128]{4,3,2,1,0:T(8,128)(2,1)} %copy.166), calls=%async_computation.1 | async-start | bytes 524288 | tf_op jit(solution)/shard_map/all_to_all | solution.py:116
  41.8 7.4 %all-to-all-done.1 = bf16[16,2,4,8,128]{4,3,2,1,0:T(8,128)(2,1)S(1)} async-done(((bf16[16,2,4,8,128]{4,3,2,1,0:T(8,128)(2,1)}), bf16[16,2,4,8,128]{4,3,2,1,0:T(8,128)(2,1)S(1)}, u32[]{:S(2)}, u32[]{:S(2)}) %all-to-all-start.1) | async-done | bytes 262176 | tf_op jit(solution)/shard_map/all_to_all | solution.py:116
  50.3 1.2 collective-permute-start.5
  51.7 1.3 collective-permute-start.7
  53.0 6.0 %collective-permute-start.8 = (bf16[8,1,8,128]{3,1,0,2:T(2,128)(2,1)}, bf16[8,1,8,128]{3,1,0,2:T(2,128)(2,1)}, u32[]{:S(2)}, u32[]{:S(2)}) collective-permute-start(bf16[8,1,8,128]{3,1,0,2:T(2,128)(2,1)} %get-tuple-element.36), channel_id=1, source_target_pairs={{1,0},{3,2},{5,4},{7,6},{9,8},{11,10},{13,12},{15,14},{17,16},{19,... | collective-permute-start | bytes 49160 | tf_op jit(solution)/shard_map/ppermute | solution.py:25
  59.9 1.4 gather_fusion.4
  61.3 1.4 gather_fusion.5
  62.7 1.4 gather_fusion.6
  64.8 1.8 bitcast_dynamic-update-slice_fusion.7
  66.6 1.8 bitcast_dynamic-update-slice_fusion.6
  68.4 1.8 bitcast_dynamic-update-slice_fusion.5
  71.1 1.6 fusion.49
  72.7 1.6 fusion.47
  74.3 2.1 %fusion.4 = f32[8,8,16,128,1]{3,2,4,1,0:T(8,128)S(1)} fusion(bf16[8,16,8,7,128]{4,1,3,0,2:T(8,128)(2,1)} %fusion.47, bf16[8,7,128,128]{3,2,1,0:T(8,128)(2,1)S(1)} %copy-done), kind=kOutput, calls=%fused_computation.20 | convolution fusion | flops 234881024 | bytes 4194304 | tf_op jit(solution)/shard_map/rlejp,ejpq->rleq/dot_general | solution.py:63
  77.7 3.4 %all-to-all-start.2 = ((bf16[4,2,16,8,128]{4,3,1,0,2:T(8,128)(2,1)}), bf16[4,2,16,8,128]{4,3,1,0,2:T(8,128)(2,1)S(1)}, u32[]{:S(2)}, u32[]{:S(2)}) async-start(bf16[4,2,16,8,128]{4,3,1,0,2:T(8,128)(2,1)} %copy.177), calls=%async_computation.2 | async-start | bytes 524288 | tf_op jit(solution)/shard_map/all_to_all | solution.py:136
  81.1 8.3 %all-to-all-done.2 = bf16[4,2,16,8,128]{4,3,1,0,2:T(8,128)(2,1)S(1)} async-done(((bf16[4,2,16,8,128]{4,3,1,0,2:T(8,128)(2,1)}), bf16[4,2,16,8,128]{4,3,1,0,2:T(8,128)(2,1)S(1)}, u32[]{:S(2)}, u32[]{:S(2)}) %all-to-all-start.2) | async-done | bytes 262176 | tf_op jit(solution)/shard_map/all_to_all | solution.py:136
  90.1 7.2 %all_to_all.126 = bf16[16,4,8,128]{3,2,1,0:T(8,128)(2,1)S(1)} all-to-all(bf16[16,4,8,128]{3,2,1,0:T(8,128)(2,1)S(1)} %copy.179), channel_id=1, replica_groups=mesh['group'=2,'tm'=4,'space'=2,'layer'=2] {'tm'}, dimensions={0} | all-to-all | bytes 262144 | tf_op jit(solution)/shard_map/all_to_all | solution.py:143
  98.1 1.2 collective-permute-start.10
  100.3 1.3 collective-permute-start.12
  101.6 4.5 %collective-permute-start.13 = (bf16[4,1,8,128]{3,1,0,2:T(2,128)(2,1)S(1)}, bf16[4,1,8,128]{3,1,0,2:T(2,128)(2,1)S(1)}, u32[]{:S(2)}, u32[]{:S(2)}) collective-permute-start(bf16[4,1,8,128]{3,1,0,2:T(2,128)(2,1)S(1)} %get-tuple-element.40), channel_id=1, source_target_pairs={{1,0},{3,2},{5,4},{7,6},{9,8},{11,10},{13,12},{15,14},{17,16},{19,... | collective-permute-start | bytes 24584 | tf_op jit(solution)/shard_map/ppermute | solution.py:25
  106.1 2.5 %collective-permute-start.9 = (f32[1,16,8,128]{3,1,0,2:T(8,128)}, f32[1,16,8,128]{3,1,0,2:T(8,128)S(1)}, u32[]{:S(2)}, u32[]{:S(2)}) collective-permute-start(f32[1,16,8,128]{3,1,0,2:T(8,128)} %slice.244), channel_id=1, source_target_pairs={{0,4},{4,8},{8,12},{1,5},{5,9},{9,13},{2,6},{6,10},{10,14},{3,7},{... | collective-permute-start | bytes 196616 | tf_op jit(solution)/shard_map/ppermute | solution.py:33
  116.0 1.7 fusion.11
  117.9 8.2 %all_to_all.127 = bf16[4,16,8,128]{3,0,2,1:T(4,128)(2,1)S(1)} all-to-all(bf16[4,16,8,128]{3,0,2,1:T(4,128)(2,1)S(1)} %copy.185), channel_id=1, replica_groups=mesh['group'=2,'tm'=4,'space'=2,'layer'=2] {'tm'}, dimensions={1} | all-to-all | bytes 262144 | tf_op jit(solution)/shard_map/all_to_all | solution.py:109
  126.8 10.0 %all_to_all.128 = bf16[16,2,4,8,128]{4,3,2,1,0:T(8,128)(2,1)S(1)} all-to-all(bf16[16,2,4,8,128]{4,3,2,1,0:T(8,128)(2,1)S(1)} %copy.187), channel_id=1, replica_groups=mesh['group'=2,'tm'=4,'space'=2,'layer'=2] {'tm'}, dimensions={0} | all-to-all | bytes 524288 | tf_op jit(solution)/shard_map/all_to_all | solution.py:116
  137.8 1.2 collective-permute-start.14
  139.3 1.3 collective-permute-start.16
  140.6 6.4 %collective-permute-start.17 = (bf16[8,1,8,128]{3,1,0,2:T(2,128)(2,1)}, bf16[8,1,8,128]{3,1,0,2:T(2,128)(2,1)}, u32[]{:S(2)}, u32[]{:S(2)}) collective-permute-start(bf16[8,1,8,128]{3,1,0,2:T(2,128)(2,1)} %get-tuple-element.32), channel_id=1, source_target_pairs={{1,0},{3,2},{5,4},{7,6},{9,8},{11,10},{13,12},{15,14},{17,16},{19,... | collective-permute-start | bytes 49160 | tf_op jit(solution)/shard_map/ppermute | solution.py:25
  147.9 1.4 gather_fusion.12
  149.3 1.4 gather_fusion.13
  150.7 1.4 gather_fusion.14
  152.8 1.8 bitcast_dynamic-update-slice_fusion.3
  154.6 1.8 bitcast_dynamic-update-slice_fusion.2
  156.4 1.8 bitcast_dynamic-update-slice_fusion.1
  159.1 1.6 fusion.45
  160.7 1.6 fusion.43
  162.3 2.1 %fusion.2 = f32[8,8,16,128,1]{3,2,4,1,0:T(8,128)S(1)} fusion(bf16[8,16,8,7,128]{4,1,3,0,2:T(8,128)(2,1)} %fusion.43, bf16[8,7,128,128]{3,2,1,0:T(8,128)(2,1)S(1)} %copy-done), kind=kOutput, calls=%fused_computation.18 | convolution fusion | flops 234881024 | bytes 4194304 | tf_op jit(solution)/shard_map/rlejp,ejpq->rleq/dot_general | solution.py:63
  165.0 10.9 %all_to_all.129 = bf16[4,2,16,8,128]{4,3,1,0,2:T(8,128)(2,1)S(1)} all-to-all(bf16[4,2,16,8,128]{4,3,1,0,2:T(8,128)(2,1)S(1)} %copy.198), channel_id=1, replica_groups=mesh['group'=2,'tm'=4,'space'=2,'layer'=2] {'tm'}, dimensions={2} | all-to-all | bytes 524288 | tf_op jit(solution)/shard_map/all_to_all | solution.py:136
  176.6 7.2 %all_to_all.130 = bf16[16,4,8,128]{3,2,1,0:T(8,128)(2,1)S(1)} all-to-all(bf16[16,4,8,128]{3,2,1,0:T(8,128)(2,1)S(1)} %copy.200), channel_id=1, replica_groups=mesh['group'=2,'tm'=4,'space'=2,'layer'=2] {'tm'}, dimensions={0} | all-to-all | bytes 262144 | tf_op jit(solution)/shard_map/all_to_all | solution.py:143
  (196 shorter events, 34.5 us)
Async XLA Ops:
  0.0 25.4 %copy-start = (bf16[8,7,128,128]{3,2,1,0:T(8,128)(2,1)S(1)}, bf16[8,7,128,128]{3,2,1,0:T(8,128)(2,1)}, u32[]{:S(2)}) copy-start(bf16[8,7,128,128]{3,2,1,0:T(8,128)(2,1)} %param.16) | copy-start | bytes 5505028
  0.0 17.0 %slice-start = ((f32[4,16,8,128]{3,2,1,0:T(8,128)}), f32[3,16,8,128]{3,2,1,0:T(8,128)S(1)}, s32[]{:S(2)}) async-start(f32[4,16,8,128]{3,2,1,0:T(8,128)} %param.11), calls=%async_computation.8 | async-start | bytes 393216 | tf_op jit(solution)/shard_map/slice | solution.py:104
  1.8 15.8 %collective-permute-start.1 = (bf16[4,16,2,128]{3,1,0,2:T(8,128)(2,1)S(1)}, bf16[4,16,2,128]{3,1,0,2:T(8,128)(2,1)S(1)}, u32[]{:S(2)}, u32[]{:S(2)}) collective-permute-start(bf16[4,16,2,128]{3,1,0,2:T(8,128)(2,1)S(1)} %get-tuple-element.46), channel_id=1, source_target_pairs={{0,2},{2,0},{1,3},{3,1},{4,6},{6,4},{5,7},{7,5},{8,10},{10,8},{9,1... | collective-permute-start | bytes 98312 | tf_op jit(solution)/shard_map/ppermute | solution.py:22
  3.9 13.8 %collective-permute-start.2 = (bf16[4,16,2,128]{3,1,0,2:T(8,128)(2,1)S(1)}, bf16[4,16,2,128]{3,1,0,2:T(8,128)(2,1)S(1)}, u32[]{:S(2)}, u32[]{:S(2)}) collective-permute-start(bf16[4,16,2,128]{3,1,0,2:T(8,128)(2,1)S(1)} %get-tuple-element.47), channel_id=1, source_target_pairs={{2,0},{0,2},{3,1},{1,3},{6,4},{4,6},{7,5},{5,7},{10,8},{8,10},{11,... | collective-permute-start | bytes 98312 | tf_op jit(solution)/shard_map/ppermute | solution.py:25
  4.0 19.9 %collective-permute-start.3 = (bf16[4,1,8,128]{3,1,0,2:T(2,128)(2,1)S(1)}, bf16[4,1,8,128]{3,1,0,2:T(2,128)(2,1)S(1)}, u32[]{:S(2)}, u32[]{:S(2)}) collective-permute-start(bf16[4,1,8,128]{3,1,0,2:T(2,128)(2,1)S(1)} %get-tuple-element.45), channel_id=1, source_target_pairs={{0,1},{2,3},{4,5},{6,7},{8,9},{10,11},{12,13},{14,15},{16,17},{18,... | collective-permute-start | bytes 24584 | tf_op jit(solution)/shard_map/ppermute | solution.py:22
  5.3 19.4 %collective-permute-start.4 = (bf16[4,1,8,128]{3,1,0,2:T(2,128)(2,1)S(1)}, bf16[4,1,8,128]{3,1,0,2:T(2,128)(2,1)S(1)}, u32[]{:S(2)}, u32[]{:S(2)}) collective-permute-start(bf16[4,1,8,128]{3,1,0,2:T(2,128)(2,1)S(1)} %get-tuple-element.44), channel_id=1, source_target_pairs={{1,0},{3,2},{5,4},{7,6},{9,8},{11,10},{13,12},{15,14},{17,16},{19,... | collective-permute-start | bytes 24584 | tf_op jit(solution)/shard_map/ppermute | solution.py:25
  9.2 16.2 %collective-permute-start = (f32[1,16,8,128]{3,1,0,2:T(8,128)S(1)}, f32[1,16,8,128]{3,1,0,2:T(8,128)S(1)}, u32[]{:S(2)}, u32[]{:S(2)}) collective-permute-start(f32[1,16,8,128]{3,1,0,2:T(8,128)S(1)} %copy.251), channel_id=1, source_target_pairs={{0,4},{4,8},{8,12},{1,5},{5,9},{9,13},{2,6},{6,10},{10,14},{3,7},{... | collective-permute-start | bytes 196616 | tf_op jit(solution)/shard_map/ppermute | solution.py:33
  14.6 10.1 %copy-start.19 = (pred[8]{0:T(512)(128)(4,1)}, pred[8]{0:T(512)(128)(4,1)S(1)}, u32[]{:S(2)}) copy-start(pred[8]{0:T(512)(128)(4,1)S(1)} %get-tuple-element.10) | copy-start | bytes 28
  14.6 10.1 %copy-start.23 = (pred[8]{0:T(512)(128)(4,1)}, pred[8]{0:T(512)(128)(4,1)S(1)}, u32[]{:S(2)}) copy-start(pred[8]{0:T(512)(128)(4,1)S(1)} %get-tuple-element.48) | copy-start | bytes 28
  14.6 10.1 %copy-start.25 = (pred[8]{0:T(512)(128)(4,1)}, pred[8]{0:T(512)(128)(4,1)S(1)}, u32[]{:S(2)}) copy-start(pred[8]{0:T(512)(128)(4,1)S(1)} %get-tuple-element.50) | copy-start | bytes 28
  14.6 4.9 %copy-start.28 = (s32[1024]{0:T(1024)}, s32[1024]{0:T(1024)S(1)}, u32[]{:S(2)}) copy-start(s32[1024]{0:T(1024)S(1)} %get-tuple-element.58) | copy-start | bytes 12292
  16.1 9.3 %copy-start.4 = (f32[16,8,128]{2,0,1:T(8,128)}, f32[16,8,128]{2,0,1:T(8,128)S(1)}, u32[]{:S(2)}) copy-start(f32[16,8,128]{2,0,1:T(8,128)S(1)} %copy.159) | copy-start | bytes 196612
  16.1 9.3 %copy-start.2 = (f32[16,8,128]{2,1,0:T(8,128)S(1)}, f32[16,8,128]{2,1,0:T(8,128)}, u32[]{:S(2)}) copy-start(f32[16,8,128]{2,1,0:T(8,128)} %param.12) | copy-start | bytes 196612
  17.0 8.4 %copy-start.6 = (f32[16,8,128]{2,0,1:T(8,128)}, f32[16,8,128]{2,0,1:T(8,128)S(1)}, u32[]{:S(2)}) copy-start(f32[16,8,128]{2,0,1:T(8,128)S(1)} %copy.163) | copy-start | bytes 196612
  17.0 8.4 %copy-start.1 = (f32[4,16,8,128]{3,2,1,0:T(8,128)S(1)}, f32[4,16,8,128]{3,2,1,0:T(8,128)}, u32[]{:S(2)}) copy-start(f32[4,16,8,128]{3,2,1,0:T(8,128)} %param.11) | copy-start | bytes 786436
  17.1 8.4 %copy-start.9 = (f32[8,128]{1,0:T(8,128)S(1)}, f32[8,128]{1,0:T(8,128)}, u32[]{:S(2)}) copy-start(f32[8,128]{1,0:T(8,128)} %param.15) | copy-start | bytes 12292
  25.5 6.0 %copy-start.35 = (f32[4]{0:T(128)S(1)}, f32[4]{0:T(128)}, u32[]{:S(2)}) copy-start(f32[4]{0:T(128)} %dynamic_slice.6) | copy-start | bytes 52
  25.5 11.5 %copy-start.31 = (f32[16]{0:T(128)S(1)}, f32[16]{0:T(128)}, u32[]{:S(2)}) copy-start(f32[16]{0:T(128)} %convert_power_fusion) | copy-start | bytes 196
  27.2 14.6 %copy-start.8 = (f32[16,8,128]{2,1,0:T(8,128)S(1)}, f32[16,8,128]{2,1,0:T(8,128)}, u32[]{:S(2)}) copy-start(f32[16,8,128]{2,1,0:T(8,128)} %param.13) | copy-start | bytes 196612
  27.9 9.0 %all-to-all-start = ((bf16[4,16,8,128]{3,0,2,1:T(4,128)(2,1)}), bf16[4,16,8,128]{3,0,2,1:T(4,128)(2,1)S(1)}, u32[]{:S(2)}, u32[]{:S(2)}) async-start(bf16[4,16,8,128]{3,0,2,1:T(4,128)(2,1)} %copy.164), calls=%async_computation | async-start | bytes 262144 | tf_op jit(solution)/shard_map/all_to_all | solution.py:109
  38.3 10.9 %all-to-all-start.1 = ((bf16[16,2,4,8,128]{4,3,2,1,0:T(8,128)(2,1)}), bf16[16,2,4,8,128]{4,3,2,1,0:T(8,128)(2,1)S(1)}, u32[]{:S(2)}, u32[]{:S(2)}) async-start(bf16[16,2,4,8,128]{4,3,2,1,0:T(8,128)(2,1)} %copy.166), calls=%async_computation.1 | async-start | bytes 524288 | tf_op jit(solution)/shard_map/all_to_all | solution.py:116
  41.8 7.7 %copy-start.11 = (f32[4]{0:T(128)}, f32[4]{0:T(128)S(1)}, u32[]{:S(2)}) copy-start(f32[4]{0:T(128)S(1)} %get-tuple-element.54) | copy-start | bytes 52
  41.8 7.8 %copy-start.15 = (f32[4]{0:T(128)}, f32[4]{0:T(128)S(1)}, u32[]{:S(2)}) copy-start(f32[4]{0:T(128)S(1)} %get-tuple-element.55) | copy-start | bytes 52
  50.3 9.5 %collective-permute-start.5 = (bf16[8,16,2,128]{3,1,0,2:T(8,128)(2,1)S(1)}, bf16[8,16,2,128]{3,1,0,2:T(8,128)(2,1)S(1)}, u32[]{:S(2)}, u32[]{:S(2)}) collective-permute-start(bf16[8,16,2,128]{3,1,0,2:T(8,128)(2,1)S(1)} %get-tuple-element.38), channel_id=1, source_target_pairs={{0,2},{2,0},{1,3},{3,1},{4,6},{6,4},{5,7},{7,5},{8,10},{10,8},{9,1... | collective-permute-start | bytes 196616 | tf_op jit(solution)/shard_map/ppermute | solution.py:22
  51.5 8.3 %collective-permute-start.6 = (bf16[8,16,2,128]{3,1,0,2:T(8,128)(2,1)S(1)}, bf16[8,16,2,128]{3,1,0,2:T(8,128)(2,1)S(1)}, u32[]{:S(2)}, u32[]{:S(2)}) collective-permute-start(bf16[8,16,2,128]{3,1,0,2:T(8,128)(2,1)S(1)} %get-tuple-element.39), channel_id=1, source_target_pairs={{2,0},{0,2},{3,1},{1,3},{6,4},{4,6},{7,5},{5,7},{10,8},{8,10},{11,... | collective-permute-start | bytes 196616 | tf_op jit(solution)/shard_map/ppermute | solution.py:25
  51.7 19.4 %collective-permute-start.7 = (bf16[8,1,8,128]{3,1,0,2:T(2,128)(2,1)}, bf16[8,1,8,128]{3,1,0,2:T(2,128)(2,1)}, u32[]{:S(2)}, u32[]{:S(2)}) collective-permute-start(bf16[8,1,8,128]{3,1,0,2:T(2,128)(2,1)} %get-tuple-element.37), channel_id=1, source_target_pairs={{0,1},{2,3},{4,5},{6,7},{8,9},{10,11},{12,13},{14,15},{16,17},{18,... | collective-permute-start | bytes 49160 | tf_op jit(solution)/shard_map/ppermute | solution.py:22
  53.0 19.7 %collective-permute-start.8 = (bf16[8,1,8,128]{3,1,0,2:T(2,128)(2,1)}, bf16[8,1,8,128]{3,1,0,2:T(2,128)(2,1)}, u32[]{:S(2)}, u32[]{:S(2)}) collective-permute-start(bf16[8,1,8,128]{3,1,0,2:T(2,128)(2,1)} %get-tuple-element.36), channel_id=1, source_target_pairs={{1,0},{3,2},{5,4},{7,6},{9,8},{11,10},{13,12},{15,14},{17,16},{19,... | collective-permute-start | bytes 49160 | tf_op jit(solution)/shard_map/ppermute | solution.py:25
  59.8 10.4 %copy-start.20 = (pred[8]{0:T(512)(128)(4,1)S(1)}, pred[8]{0:T(512)(128)(4,1)}, u32[]{:S(2)}) copy-start(pred[8]{0:T(512)(128)(4,1)} %copy-done.19) | copy-start | bytes 28
  77.7 11.8 %all-to-all-start.2 = ((bf16[4,2,16,8,128]{4,3,1,0,2:T(8,128)(2,1)}), bf16[4,2,16,8,128]{4,3,1,0,2:T(8,128)(2,1)S(1)}, u32[]{:S(2)}, u32[]{:S(2)}) async-start(bf16[4,2,16,8,128]{4,3,1,0,2:T(8,128)(2,1)} %copy.177), calls=%async_computation.2 | async-start | bytes 524288 | tf_op jit(solution)/shard_map/all_to_all | solution.py:136
  81.1 19.1 %copy-start.33 = (f32[16]{0:T(128)}, f32[16]{0:T(128)S(1)}, u32[]{:S(2)}) copy-start(f32[16]{0:T(128)S(1)} %power_multiply_fusion) | copy-start | bytes 196
  97.3 14.3 %copy-start.27 = (pred[8]{0:T(512)(128)(4,1)S(1)}, pred[8]{0:T(512)(128)(4,1)}, u32[]{:S(2)}) copy-start(pred[8]{0:T(512)(128)(4,1)} %get-tuple-element.52) | copy-start | bytes 28
  97.3 14.9 %copy-start.26 = (pred[8]{0:T(512)(128)(4,1)S(1)}, pred[8]{0:T(512)(128)(4,1)}, u32[]{:S(2)}) copy-start(pred[8]{0:T(512)(128)(4,1)} %copy-done.25) | copy-start | bytes 28
  97.3 15.7 %copy-start.24 = (pred[8]{0:T(512)(128)(4,1)S(1)}, pred[8]{0:T(512)(128)(4,1)}, u32[]{:S(2)}) copy-start(pred[8]{0:T(512)(128)(4,1)} %copy-done.23) | copy-start | bytes 28
  97.4 16.4 %copy-start.21 = (pred[8]{0:T(512)(128)(4,1)S(1)}, pred[8]{0:T(512)(128)(4,1)}, u32[]{:S(2)}) copy-start(pred[8]{0:T(512)(128)(4,1)} %copy-done.19) | copy-start | bytes 28
  98.1 10.5 %collective-permute-start.10 = (bf16[4,16,2,128]{3,1,0,2:T(8,128)(2,1)S(1)}, bf16[4,16,2,128]{3,1,0,2:T(8,128)(2,1)S(1)}, u32[]{:S(2)}, u32[]{:S(2)}) collective-permute-start(bf16[4,16,2,128]{3,1,0,2:T(8,128)(2,1)S(1)} %get-tuple-element.42), channel_id=1, source_target_pairs={{0,2},{2,0},{1,3},{3,1},{4,6},{6,4},{5,7},{7,5},{8,10},{10,8},{9,1... | collective-permute-start | bytes 98312 | tf_op jit(solution)/shard_map/ppermute | solution.py:22
  99.3 9.4 %collective-permute-start.11 = (bf16[4,16,2,128]{3,1,0,2:T(8,128)(2,1)S(1)}, bf16[4,16,2,128]{3,1,0,2:T(8,128)(2,1)S(1)}, u32[]{:S(2)}, u32[]{:S(2)}) collective-permute-start(bf16[4,16,2,128]{3,1,0,2:T(8,128)(2,1)S(1)} %get-tuple-element.43), channel_id=1, source_target_pairs={{2,0},{0,2},{3,1},{1,3},{6,4},{4,6},{7,5},{5,7},{10,8},{8,10},{11,... | collective-permute-start | bytes 98312 | tf_op jit(solution)/shard_map/ppermute | solution.py:25
  100.3 14.3 %collective-permute-start.12 = (bf16[4,1,8,128]{3,1,0,2:T(2,128)(2,1)S(1)}, bf16[4,1,8,128]{3,1,0,2:T(2,128)(2,1)S(1)}, u32[]{:S(2)}, u32[]{:S(2)}) collective-permute-start(bf16[4,1,8,128]{3,1,0,2:T(2,128)(2,1)S(1)} %get-tuple-element.41), channel_id=1, source_target_pairs={{0,1},{2,3},{4,5},{6,7},{8,9},{10,11},{12,13},{14,15},{16,17},{18,... | collective-permute-start | bytes 24584 | tf_op jit(solution)/shard_map/ppermute | solution.py:22
  101.6 13.6 %collective-permute-start.13 = (bf16[4,1,8,128]{3,1,0,2:T(2,128)(2,1)S(1)}, bf16[4,1,8,128]{3,1,0,2:T(2,128)(2,1)S(1)}, u32[]{:S(2)}, u32[]{:S(2)}) collective-permute-start(bf16[4,1,8,128]{3,1,0,2:T(2,128)(2,1)S(1)} %get-tuple-element.40), channel_id=1, source_target_pairs={{1,0},{3,2},{5,4},{7,6},{9,8},{11,10},{13,12},{15,14},{17,16},{19,... | collective-permute-start | bytes 24584 | tf_op jit(solution)/shard_map/ppermute | solution.py:25
  106.1 11.6 %collective-permute-start.9 = (f32[1,16,8,128]{3,1,0,2:T(8,128)}, f32[1,16,8,128]{3,1,0,2:T(8,128)S(1)}, u32[]{:S(2)}, u32[]{:S(2)}) collective-permute-start(f32[1,16,8,128]{3,1,0,2:T(8,128)} %slice.244), channel_id=1, source_target_pairs={{0,4},{4,8},{8,12},{1,5},{5,9},{9,13},{2,6},{6,10},{10,14},{3,7},{... | collective-permute-start | bytes 196616 | tf_op jit(solution)/shard_map/ppermute | solution.py:33
  117.7 8.5 %copy-start.32 = (f32[16]{0:T(128)S(1)}, f32[16]{0:T(128)}, u32[]{:S(2)}) copy-start(f32[16]{0:T(128)} %convert_power_fusion) | copy-start | bytes 196
  117.9 18.9 %copy-start.13 = (f32[4]{0:T(128)S(1)}, f32[4]{0:T(128)}, u32[]{:S(2)}) copy-start(f32[4]{0:T(128)} %copy-done.11) | copy-start | bytes 52
  117.9 18.9 %copy-start.17 = (f32[4]{0:T(128)S(1)}, f32[4]{0:T(128)}, u32[]{:S(2)}) copy-start(f32[4]{0:T(128)} %copy-done.15) | copy-start | bytes 52
  137.8 10.0 %collective-permute-start.14 = (bf16[8,16,2,128]{3,1,0,2:T(8,128)(2,1)S(1)}, bf16[8,16,2,128]{3,1,0,2:T(8,128)(2,1)S(1)}, u32[]{:S(2)}, u32[]{:S(2)}) collective-permute-start(bf16[8,16,2,128]{3,1,0,2:T(8,128)(2,1)S(1)} %get-tuple-element.34), channel_id=1, source_target_pairs={{0,2},{2,0},{1,3},{3,1},{4,6},{6,4},{5,7},{7,5},{8,10},{10,8},{9,1... | collective-permute-start | bytes 196616 | tf_op jit(solution)/shard_map/ppermute | solution.py:22
  139.0 8.8 %collective-permute-start.15 = (bf16[8,16,2,128]{3,1,0,2:T(8,128)(2,1)S(1)}, bf16[8,16,2,128]{3,1,0,2:T(8,128)(2,1)S(1)}, u32[]{:S(2)}, u32[]{:S(2)}) collective-permute-start(bf16[8,16,2,128]{3,1,0,2:T(8,128)(2,1)S(1)} %get-tuple-element.35), channel_id=1, source_target_pairs={{2,0},{0,2},{3,1},{1,3},{6,4},{4,6},{7,5},{5,7},{10,8},{8,10},{11,... | collective-permute-start | bytes 196616 | tf_op jit(solution)/shard_map/ppermute | solution.py:25
  139.3 19.8 %collective-permute-start.16 = (bf16[8,1,8,128]{3,1,0,2:T(2,128)(2,1)}, bf16[8,1,8,128]{3,1,0,2:T(2,128)(2,1)}, u32[]{:S(2)}, u32[]{:S(2)}) collective-permute-start(bf16[8,1,8,128]{3,1,0,2:T(2,128)(2,1)} %get-tuple-element.33), channel_id=1, source_target_pairs={{0,1},{2,3},{4,5},{6,7},{8,9},{10,11},{12,13},{14,15},{16,17},{18,... | collective-permute-start | bytes 49160 | tf_op jit(solution)/shard_map/ppermute | solution.py:22
  140.6 20.1 %collective-permute-start.17 = (bf16[8,1,8,128]{3,1,0,2:T(2,128)(2,1)}, bf16[8,1,8,128]{3,1,0,2:T(2,128)(2,1)}, u32[]{:S(2)}, u32[]{:S(2)}) collective-permute-start(bf16[8,1,8,128]{3,1,0,2:T(2,128)(2,1)} %get-tuple-element.32), channel_id=1, source_target_pairs={{1,0},{3,2},{5,4},{7,6},{9,8},{11,10},{13,12},{15,14},{17,16},{19,... | collective-permute-start | bytes 49160 | tf_op jit(solution)/shard_map/ppermute | solution.py:25
  147.9 10.4 %copy-start.22 = (pred[8]{0:T(512)(128)(4,1)S(1)}, pred[8]{0:T(512)(128)(4,1)}, u32[]{:S(2)}) copy-start(pred[8]{0:T(512)(128)(4,1)} %copy-done.19) | copy-start | bytes 28
  164.5 11.5 %copy-start.34 = (f32[16]{0:T(128)S(1)}, f32[16]{0:T(128)}, u32[]{:S(2)}) copy-start(f32[16]{0:T(128)} %copy-done.33) | copy-start | bytes 196
  (10 other events, 25.1 us)
where the time goes:
time: 188 us; the launch traced here: 185 us
  starting transfers between devices  48 us (26%)
  blocking collectives  43.5 us (23%)
  other arithmetic  33.7 us (18%)
  local copies, waits for them, and re-layouts  27.9 us (15%)
  waiting for transfers between devices  21.1 us (11%)
  matrix products  9.43 us (5%)
    unnamed x21, other arithmetic  24.6 us
    ppermute x8, starting transfers between devices, padded(): lax.ppermute(lax.slice_in_dim(block, 0, width, axis=dim), axis, backward)  20.8 us
    gather x16, local copies, waits for them, and re-layouts, tile_part(): picked.append(jnp.take(wide, place[:, slot], axis=2))  15 us
    all_to_all x2, blocking collectives, shards(): lax.all_to_all(moved.astype(jnp.bfloat16), 'tm', split_axis=0, concat_axi...  14.4 us
    all_to_all x1, blocking collectives, shards(): piece = lax.all_to_all(final, 'tm', split_axis=2, concat_axis=0, tiled=True)  10.9 us
    ppermute x8, starting transfers between devices, padded(): lax.ppermute(lax.slice_in_dim(block, block.shape[dim] - width, None, axis...  10.8 us
    all_to_all x1, blocking collectives, shards(): lax.all_to_all(jnp.stack([part_re.astype(jnp.bfloat16), part_im.astype(jn...  10 us
    all_to_all x1, waiting for transfers between devices, shards(): piece = lax.all_to_all(final, 'tm', split_axis=2, concat_axis=0, tiled=True)  8.33 us
  transfers between devices with their start and end apart: 21, of which 3 were waited for; matrix products, arithmetic and copies ran while one was open for 27% of the time, Pallas kernels for 0%

commit v1 on v0

v1 whole, which is shorter than its diff:
```python
import math

import jax
import jax.numpy as jnp
import numpy as np
from jax import lax
from jax.experimental import pallas as pl
from jax.experimental.pallas import tpu as pltpu
from jax.sharding import PartitionSpec as P

NEWTON = 2
APPLICATIONS = 2 * NEWTON
OFFSETS = (-2, -1, 1, 2)
GROUP = 4

corner_weight = 0.25


def transform_tables(steps):
    beta = corner_weight ** (1.0 / steps)
    half = steps // 2
    counter = np.arange(steps)
    angle = ((counter[:, None] * counter[None, :]) % steps) * (2.0 * math.pi / steps)
    rising = np.power(beta, counter)
    falling = np.power(beta, -counter.astype(np.float64)) / steps
    fwd_re = np.cos(angle) * rising[None, :]
    fwd_im = -np.sin(angle) * rising[None, :]
    back_re = np.cos(angle) * falling[:, None]
    back_im = -np.sin(angle) * falling[:, None]
    forward = np.concatenate([fwd_re[:half], fwd_re[half : half + 1], fwd_im[1:half]], 0)
    twice = np.where(np.arange(half) == 0, 1.0, 2.0)
    backward = np.concatenate(
        [
            back_re[:, :half] * twice,
            back_re[:, half : half + 1],
            back_im[:, 1:half] * 2.0,
        ],
        1,
    )
    phase = counter * (2.0 * math.pi / steps)
    eigen_re = 1.0 - beta * np.cos(phase)
    eigen_im = beta * np.sin(phase)
    low_re = eigen_re[:half]
    low_im = np.where(np.arange(half) == 0, 0.0, eigen_im[:half])
    high_re = np.concatenate([eigen_re[half : half + 1], eigen_re[1:half]])
    eigen = np.stack([low_re, low_im, high_re]).astype(np.float32)
    return forward, backward, eigen


def newton(values, old, tiles, slots, coef, diag, eigen, forward, backward, packed, spec, inverse,
           base, window_at, all_layers, write):
    layers, steps, width = values.shape[1:]
    half = steps // 2
    wide, inner = layers - 2, layers - 4

    def applied(array, at, low, count, element):
        parts = [array[at, low : low + count]]
        for offset in OFFSETS:
            parts.append(array[at + offset, low : low + count])
        parts.append(array[at, low - 1 : low - 1 + count])
        parts.append(array[at, low + 1 : low + 1 + count])
        rows = jnp.concatenate([part.reshape(count * steps, width) for part in parts], axis=1)
        blocks = [tiles[element, 0]]
        for place in range(4):
            blocks.append(tiles[element, slots[element, place]])
        blocks.append(tiles[element, 5])
        blocks.append(tiles[element, 6])
        weights = jnp.concatenate(blocks, axis=0)
        out = jnp.dot(rows, weights, preferred_element_type=jnp.float32)
        return out.reshape(count, steps, width)

    layer = lax.broadcasted_iota(jnp.int32, (wide, 1, width), 0) + (base + window_at + 1)
    inside = jnp.where((layer >= 0) & (layer < all_layers), 1.0, 0.0).astype(jnp.float32)
    time = lax.broadcasted_iota(jnp.int32, (wide, steps, width), 1)
    for element in range(8):
        image = applied(values, element + 2, 1, wide, element)
        state = values[element + 2, 1 : 1 + wide].astype(jnp.float32)
        rows = slice(window_at + 1, window_at + 1 + wide)
        start = coef[0, rows, element : element + 1, :]
        reaction = coef[1, rows, element : element + 1, :]
        source = coef[2, rows, element : element + 1, :]
        own = diag[element : element + 1, :][None]
        previous = jnp.where(time == 0, start, pltpu.roll(state, 1, 1))
        residual = (
            state - previous + own * state + image + reaction * state * state * state - source
        )
        rhs = (-residual).astype(jnp.bfloat16).reshape(wide * steps, width)
        out = jnp.dot(forward[...], rhs, preferred_element_type=jnp.float32)
        out = out.astype(jnp.bfloat16).astype(jnp.float32).reshape(wide, steps, width)
        real = own + 3.0 * reaction * start * start
        low = eigen[0][None] + real
        high = eigen[2][None] + real
        imag = eigen[1][None]
        low_over = inside / (low * low + imag * imag)
        high_over = inside / (high * high + imag * imag)
        first = low * low_over
        cross = -imag * low_over
        last = high * high_over
        part_a, part_b = out[:, :half], out[:, half:]
        sol = jnp.concatenate(
            [first * part_a - cross * part_b, cross * part_a + last * part_b], axis=1
        )
        packed[element] = sol.astype(jnp.bfloat16)
        if 2 <= element < 6:
            spec[element - 2] = out
            inverse[element - 2, 0] = first
            inverse[element - 2, 1] = cross
            inverse[element - 2, 2] = last
    for own in range(4):
        image = applied(packed, own + 2, 1, inner, own + 2)
        left = spec[own, 1 : 1 + inner] - image
        part_a, part_b = left[:, :half], left[:, half:]
        first = inverse[own, 0, 1 : 1 + inner]
        cross = inverse[own, 1, 1 : 1 + inner]
        last = inverse[own, 2, 1 : 1 + inner]
        final = jnp.concatenate(
            [first * part_a - cross * part_b, cross * part_a + last * part_b], axis=1
        )
        final = final.astype(jnp.bfloat16).reshape(inner * steps, width)
        delta = jnp.dot(backward[...], final, preferred_element_type=jnp.float32)
        delta = delta.astype(jnp.bfloat16).astype(jnp.float32).reshape(inner, steps, width)
        state = values[own + 4, 2 : 2 + inner].astype(jnp.float32) + delta
        write(own, state.astype(jnp.bfloat16))


def first_kernel(all_layers, where, slots, own, beside, across, order, tiles, coef, diag, eigen,
                 forward, backward, out, values, packed, spec, inverse):
    steps, rows, width = own.shape
    core = where[0]
    size = steps * GROUP * 4
    for group in range(rows // (GROUP * 4)):
        cut = pl.ds(group * GROUP * 4, GROUP * 4)
        near, far = beside[:, cut, :], across[:, cut, :]
        left = jnp.where(core == 0, far, near)
        right = jnp.where(core == 0, near, far)
        for at, part in ((0, left), (4, own[:, cut, :]), (8, right)):
            moved = jnp.dot(
                order[...], part.reshape(size, width), preferred_element_type=jnp.float32
            )
            moved = moved.astype(jnp.bfloat16).reshape(4, GROUP, steps, width)
            values[at : at + 4, group * GROUP : (group + 1) * GROUP] = moved

    def write(element, state):
        out[element] = state

    newton(values, None, tiles, slots, coef, diag, eigen, forward, backward, packed, spec, inverse,
           where[1], 0, all_layers, write)


def second_kernel(all_layers, where, slots, own, beside, across, order, tiles, coef, diag, eigen,
                  forward, backward, out, values, packed, spec, inverse, solved):
    core = where[0]
    near, far = beside[...], across[...]
    values[0:4] = jnp.where(core == 0, far, near)
    values[4:8] = own[...]
    values[8:12] = jnp.where(core == 0, near, far)
    steps, width = own.shape[2:]

    def write(element, state):
        solved[element] = state

    newton(values, None, tiles, slots, coef, diag, eigen, forward, backward, packed, spec, inverse,
           where[1], 2, all_layers, write)
    size = steps * GROUP * 4
    for group in range(solved.shape[1] // GROUP):
        part = solved[:, group * GROUP : (group + 1) * GROUP].reshape(size, width)
        moved = jnp.dot(order[...], part, preferred_element_type=jnp.float32)
        cut = pl.ds(group * GROUP * 4, GROUP * 4)
        out[:, cut, :] = moved.astype(jnp.bfloat16).reshape(steps, GROUP * 4, width)


def call(kernel, out_shape, scratch, scalars, arrays):
    return pl.pallas_call(
        kernel,
        out_shape=jax.ShapeDtypeStruct(out_shape, jnp.bfloat16),
        in_specs=[pl.BlockSpec(memory_space=pltpu.SMEM)] * len(scalars)
        + [pl.BlockSpec(memory_space=pltpu.VMEM)] * len(arrays),
        out_specs=pl.BlockSpec(memory_space=pltpu.VMEM),
        scratch_shapes=scratch,
        compiler_params=pltpu.CompilerParams(vmem_limit_bytes=48 * 1024 * 1024),
    )(*scalars, *arrays)


def shards(state_guess, start_state, reaction, source, self_diag, tiles, neighbors):
    local_steps, local_layers, local_elems, width = state_guess.shape
    count = lax.axis_size("tm")
    sections = lax.axis_size("space")
    mine, core = lax.axis_index("tm"), lax.axis_index("layer")
    steps = local_steps * count
    all_layers = local_layers * 2
    chip_layers = all_layers // count
    window = -(-(chip_layers + 2 * APPLICATIONS) // GROUP) * GROUP
    half = local_elems // 2
    swap = [(0, 1), (1, 0)]
    circle = []
    for section in range(sections):
        one, other = 2 * section + 1, 2 * ((section + 1) % sections)
        circle += [(one, other), (other, one)]

    def over_core(array):
        return lax.ppermute(array, "layer", swap)

    def over_circle(array):
        return lax.ppermute(array, ("space", "layer"), circle)

    def exchanged(parts):
        return [parts[0]] + [
            lax.ppermute(parts[k], "tm", [(i, i ^ k) for i in range(count)])
            for k in range(1, count)
        ]

    forward, backward, eigen = transform_tables(steps)
    low = lax.bitwise_xor(mine, jnp.arange(count, dtype=jnp.int32)) * local_steps
    times = (low[:, None] + jnp.arange(local_steps, dtype=jnp.int32)[None]).reshape(steps)
    size = 4 * GROUP * steps
    row = jnp.arange(size, dtype=jnp.int32)
    solver = (row // (GROUP * steps), row // steps % GROUP, row % steps)
    arrival = (row % 4, row // 4 % GROUP, jnp.repeat(times, GROUP * 4))
    target = (solver[0] * GROUP + solver[1]) * steps + solver[2]
    from_there = (arrival[0] * GROUP + arrival[1]) * steps + arrival[2]
    order = (target[:, None] == from_there[None, :]).astype(jnp.bfloat16)
    order_back = (from_there[:, None] == target[None, :]).astype(jnp.bfloat16)

    pair = state_guess.astype(jnp.bfloat16).reshape(local_steps, local_layers, 2, half, width)
    flat = (local_steps, local_layers * half, width)
    keep = lax.dynamic_index_in_dim(pair, core, 2, keepdims=False).reshape(flat)
    give = lax.dynamic_index_in_dim(pair, 1 - core, 2, keepdims=False).reshape(flat)
    got = over_core(give)
    below = jnp.zeros((local_steps, APPLICATIONS * half, width), jnp.bfloat16)
    above = jnp.zeros(
        (local_steps, (window - chip_layers - APPLICATIONS) * half, width), jnp.bfloat16
    )
    whole = jnp.concatenate(
        [below, jnp.where(core == 0, keep, got), jnp.where(core == 0, got, keep), above], 1
    )
    pieces = [
        lax.dynamic_slice_in_dim(
            whole, lax.bitwise_xor(mine, k) * (chip_layers * half), window * half, 1
        )
        for k in range(count)
    ]
    own = jnp.concatenate(exchanged(pieces), 0)

    at = 4 * core
    edge_tiles = lax.dynamic_slice_in_dim(tiles, 6 * core, 2, 0)
    edge_tiles = over_circle(edge_tiles)
    near_tiles = lax.dynamic_slice_in_dim(
        jnp.concatenate([edge_tiles, tiles, edge_tiles], 0), at, 8, 0
    )
    total = local_elems * sections
    ids = lax.axis_index("space") * local_elems + jnp.arange(local_elems, dtype=jnp.int32)
    wanted = (ids[:, None] + jnp.array(OFFSETS, jnp.int32)[None] + total) % total
    slots = jnp.sum(
        (wanted[:, :, None] == neighbors[:, None, :])
        * jnp.arange(1, 5, dtype=jnp.int32)[None, None],
        -1,
    )
    fields = jnp.stack([start_state, reaction, source])
    other = over_core(fields)
    fields = jnp.concatenate(
        [jnp.where(core == 0, fields, other), jnp.where(core == 0, other, fields)], 1
    )
    fields = jnp.pad(
        fields,
        ((0, 0), (APPLICATIONS, window - chip_layers - APPLICATIONS), (0, 0), (0, 0)),
    )
    fields = lax.dynamic_slice_in_dim(fields, mine * chip_layers, window, 1)
    slot_rows = jnp.pad(slots.astype(jnp.float32), ((0, 0), (0, width - 4)))
    bundle = jnp.concatenate(
        [fields.reshape(3 * window, local_elems, width), self_diag[None], slot_rows[None]], 0
    )
    edge = over_circle(lax.dynamic_slice_in_dim(bundle, 6 * core, 2, 1))
    bundle = lax.dynamic_slice_in_dim(jnp.concatenate([edge, bundle, edge], 1), at, 8, 1)
    coef = bundle[: 3 * window].reshape(3, window, 8, width)
    diag = bundle[3 * window]
    slots = bundle[3 * window + 1, :, :4].astype(jnp.int32)
    place = jnp.stack([core, mine * chip_layers - APPLICATIONS]).astype(jnp.int32)
    eigen = jnp.asarray(np.broadcast_to(eigen[:, :, None], eigen.shape + (width,)))

    def table(matrix, layers):
        return jnp.asarray(np.kron(np.eye(layers), matrix).astype(np.float32)).astype(jnp.bfloat16)

    def scratch(layers):
        return [
            pltpu.VMEM((12, layers, steps, width), jnp.bfloat16),
            pltpu.VMEM((8, layers - 2, steps, width), jnp.bfloat16),
            pltpu.VMEM((4, layers - 2, steps, width), jnp.float32),
            pltpu.VMEM((4, 3, layers - 2, steps // 2, width), jnp.float32),
        ]

    state = call(
        lambda *refs: first_kernel(all_layers, *refs),
        (4, window - 4, steps, width),
        scratch(window),
        [place, slots],
        [own, over_core(own), over_circle(own), order, near_tiles, coef, diag, eigen,
         table(forward, window - 2), table(backward, window - 4)],
    )
    last = window - 8
    solved = call(
        lambda *refs: second_kernel(all_layers, *refs),
        (steps, last * half, width),
        scratch(window - 4) + [pltpu.VMEM((4, last, steps, width), jnp.bfloat16)],
        [place, slots],
        [state, over_core(state), over_circle(state), order_back, near_tiles, coef, diag, eigen,
         table(forward, window - 6), table(backward, last)],
    )
    parts = exchanged([solved[k * local_steps : (k + 1) * local_steps] for k in range(count)])
    parts = jnp.stack(parts).reshape(2, count // 2, local_steps, last, half, width)
    parts = parts[:, :, :, :chip_layers]
    same = (mine // (count // 2)) == core
    keep = jnp.where(same, parts[0], parts[1])
    got = over_core(jnp.where(same, parts[1], parts[0]))
    both = jnp.concatenate(
        [jnp.where(core == 0, keep, got), jnp.where(core == 0, got, keep)], 3
    )
    ranks = lax.bitwise_xor(
        mine % (count // 2), jnp.arange(count // 2, dtype=jnp.int32)
    )
    both = jnp.take(both, ranks, axis=0)
    both = jnp.transpose(both, (1, 0, 2, 3, 4))
    return both.reshape(state_guess.shape).astype(jnp.float32)


def solution(mesh):
    in_specs = (
        P("tm", ("group", "layer"), "space", None),
        P(("group", "layer"), "space", None),
        P(("group", "layer"), "space", None),
        P(("group", "layer"), "space", None),
        P("space", None),
        P("space", None, None, None),
        P("space", None),
    )
    out_specs = P("tm", ("group", "layer"), "space", None)
    return jax.shard_map(shards, mesh=mesh, in_specs=in_specs, out_specs=out_specs, check_vma=False)
```

time: 188 us -> 52.9 us (0.28); the launches traced: 185 us -> 52.4 us
  blocking collectives: 43.5 us -> 0 us
  starting transfers between devices: 48 us -> 16.1 us
  other arithmetic: 33.7 us -> 3.87 us
  local copies, waits for them, and re-layouts: 27.9 us -> 2.96 us
  matrix products: 9.43 us -> 0 us
  Pallas kernels: 0 us -> 8.09 us
    all_to_all x5 -> x0, blocking collectives: 43.5 us -> none  [the longest x2 14.4 us: shards(): lax.all_to_all(moved.astype(jnp.bfloat16), 'tm', split_axis=0, concat_axi...]
    unnamed x21 -> x0, other arithmetic: 24.6 us -> none
    ppermute x18 -> x15, starting transfers between devices: 37.6 us -> 16.1 us  [the longest x6 7.28 us: exchanged(): lax.ppermute(parts[k], 'tm', [(i, i ^ k) for i in range(count)])]
    all_to_all x3 -> x0, waiting for transfers between devices: 21.1 us -> none  [the longest x1 8.33 us: shards(): piece = lax.all_to_all(final, 'tm', split_axis=2, concat_axis=0, tiled=True)]
    ppermute x18 -> x15, waiting for transfers between devices: 0.05 us -> 21 us  [the longest x4 12.8 us: over_circle(): return lax.ppermute(array, ('space', 'layer'), circle)]
    gather x16 -> x1, local copies, waits for them, and re-layouts: 15 us -> 0.57 us  [shards(): both = jnp.take(both, ranks, axis=0)]
    all_to_all x3 -> x0, starting transfers between devices: 10.4 us -> none  [the longest x1 3.58 us: shards(): lax.all_to_all(neg_rhs, 'tm', split_axis=1, concat_axis=0, tiled=True)]
    dot_general x12 -> x0, matrix products: 9.43 us -> none  [the longest x4 7.66 us: tile_part(): jnp.einsum('rlejp,ejpq->rleq', stacked, tiles, preferred_element_type=jnp...]
  transfers between devices with their start and end apart: 21 -> 15, of which waited for: 3 -> 7; matrix products, arithmetic and copies ran while one was open for 27% -> 7% of each run, Pallas kernels for 0% -> 0%
where the time goes in v1:
time: 52.9 us; the launch traced here: 52.4 us
  waiting for transfers between devices  21 us (40%)
  starting transfers between devices  16.1 us (30%)
  Pallas kernels  8.09 us (15%)
  other arithmetic  3.87 us (7%)
  local copies, waits for them, and re-layouts  2.96 us (6%)
    ppermute x4, waiting for transfers between devices, over_circle(): return lax.ppermute(array, ('space', 'layer'), circle)  12.8 us
    pallas_call x2, Pallas kernels, call(): pl.pallas_call(kernel, out_shape=jax.ShapeDtypeStruct(out_shape, jnp.bflo...  8.09 us
    ppermute x6, waiting for transfers between devices, exchanged(): lax.ppermute(parts[k], 'tm', [(i, i ^ k) for i in range(count)])  7.35 us
    ppermute x6, starting transfers between devices, exchanged(): lax.ppermute(parts[k], 'tm', [(i, i ^ k) for i in range(count)])  7.28 us
    ppermute x5, starting transfers between devices, over_core(): return lax.ppermute(array, 'layer', swap)  4.72 us
    ppermute x4, starting transfers between devices, over_circle(): return lax.ppermute(array, ('space', 'layer'), circle)  4.14 us
    dynamic_slice x1, local copies, waits for them, and re-layouts, shards(): edge_tiles = lax.dynamic_slice_in_dim(tiles, 6 * core, 2, 0)  1.06 us
  transfers between devices with their start and end apart: 15, of which 7 were waited for; matrix products, arithmetic and copies ran while one was open for 7% of the time, Pallas kernels for 0%

profile of v1, /device:TPU:1, one launch (start us, length us, event | category | flops | bytes accessed | tf_op | source)
XLA Modules:
  0.0 52.4 jit_solution(12113243882231349733)
XLA Ops:
  0.0 1.0 %convert_element_type.46 = bf16[4,16,8,128]{3,2,1,0:T(8,128)(2,1)S(1)} convert(f32[4,16,8,128]{3,2,1,0:T(8,128)} %param.13) | non-fusion elementwise | flops 65536 | bytes 393216 | tf_op jit(solution)/shard_map/convert_element_type | solution.py:224
  1.1 0.1 constant_dynamic-slice_fusion.6
  1.2 0.1 collective-permute-start.2
  1.2 0.9 %pad_maximum_fusion.1 = f32[3,16,8,128]{3,2,1,0:T(8,128)S(1)} fusion(f32[1,16,8,128]{3,2,1,0:T(8,128)} %bitcast.38, f32[1,16,8,128]{3,2,1,0:T(8,128)} %bitcast.40, f32[1,16,8,128]{3,2,1,0:T(8,128)} %bitcast.42), kind=kLoop, calls=%fused_computation.30 | loop fusion | flops 98304 | bytes 393216 | tf_op jit(solution)/shard_map/stack | solution.py:258
  2.2 0.6 %collective-permute-start = (f32[3,16,8,128]{3,2,1,0:T(8,128)S(1)}, f32[3,16,8,128]{3,2,1,0:T(8,128)S(1)}, u32[]{:S(2)}, u32[]{:S(2)}) collective-permute-start(f32[3,16,8,128]{3,2,1,0:T(8,128)S(1)} %pad_maximum_fusion.1), channel_id=1, source_target_pairs={{0,1},{1,0},{2,3},{3,2},{4,5},{5,4},{6,7},{7,6},{8,9},{9,8},{10,11... | collective-permute-start | bytes 589832 | tf_op jit(solution)/shard_map/ppermute | solution.py:201
  2.7 1.1 %constant_dynamic-slice_fusion = bf16[2,7,128,128]{3,2,1,0:T(8,128)(2,1)S(1)} fusion(bf16[8,7,128,128]{3,2,1,0:T(8,128)(2,1)} %param.18, s32[]{:T(128)S(6)} %select_n.222), kind=kLoop, calls=%fused_computation.47 | loop fusion | bytes 917508 | tf_op jit(solution)/shard_map/dynamic_slice | solution.py:245
  3.8 2.7 %collective-permute-start.8 = (bf16[2,7,128,128]{3,2,1,0:T(8,128)(2,1)S(1)}, bf16[2,7,128,128]{3,2,1,0:T(8,128)(2,1)S(1)}, u32[]{:S(2)}, u32[]{:S(2)}) collective-permute-start(bf16[2,7,128,128]{3,2,1,0:T(8,128)(2,1)S(1)} %constant_dynamic-slice_fusion), channel_id=1, source_target_pairs={{1,2},{2,1},{3,0},{0,3},{5,6},{6,5},{7,4},{4,7},{9,10},{10,9},{11,... | collective-permute-start | bytes 1376264 | tf_op jit(solution)/shard_map/ppermute | solution.py:204
  6.5 0.1 add_select_fusion
  6.5 0.1 select_reduce_fusion
  6.6 0.1 copy.21
  6.7 0.1 iota_add_fusion.1
  6.8 0.1 add.286
  6.9 0.1 broadcast_in_dim.16
  7.0 0.1 reshape.278
  7.1 0.1 compare_convert_fusion
  7.2 0.1 pad_add_fusion.refs_0_
  7.4 1.4 %collective-permute-start.3 = (bf16[4,64,128]{2,1,0:T(8,128)(2,1)S(1)}, bf16[4,64,128]{2,1,0:T(8,128)(2,1)S(1)}, u32[]{:S(2)}, u32[]{:S(2)}) collective-permute-start(bf16[4,64,128]{2,1,0:T(8,128)(2,1)S(1)} %get-tuple-element.12), channel_id=1, source_target_pairs={{0,4},{4,0},{8,12},{12,8},{1,5},{5,1},{9,13},{13,9},{2,6},{6,2},{1... | collective-permute-start | bytes 196616 | tf_op jit(solution)/shard_map/ppermute | solution.py:208
  8.8 2.3 %collective-permute-start.4 = (bf16[4,64,128]{2,1,0:T(8,128)(2,1)S(1)}, bf16[4,64,128]{2,1,0:T(8,128)(2,1)S(1)}, u32[]{:S(2)}, u32[]{:S(2)}) collective-permute-start(bf16[4,64,128]{2,1,0:T(8,128)(2,1)S(1)} %get-tuple-element.11), channel_id=1, source_target_pairs={{0,8},{4,12},{8,0},{12,4},{1,9},{5,13},{9,1},{13,5},{2,10},{6,14},... | collective-permute-start | bytes 196616 | tf_op jit(solution)/shard_map/ppermute | solution.py:208
  11.1 0.1 fusion.7
  11.3 0.9 %collective-permute-start.1 = (f32[50,2,128]{2,1,0:T(2,128)S(1)}, f32[50,2,128]{2,1,0:T(2,128)S(1)}, u32[]{:S(2)}, u32[]{:S(2)}) collective-permute-start(f32[50,2,128]{2,1,0:T(2,128)S(1)} %fusion.13), channel_id=1, source_target_pairs={{1,2},{2,1},{3,0},{0,3},{5,6},{6,5},{7,4},{4,7},{9,10},{10,9},{11,... | collective-permute-start | bytes 153608 | tf_op jit(solution)/shard_map/ppermute | solution.py:204
  12.2 0.6 %collective-permute-done.4 = bf16[4,64,128]{2,1,0:T(8,128)(2,1)S(1)} collective-permute-done((bf16[4,64,128]{2,1,0:T(8,128)(2,1)S(1)}, bf16[4,64,128]{2,1,0:T(8,128)(2,1)S(1)}, u32[]{:S(2)}, u32[]{:S(2)}) %collective-permute-start.4) | collective-permute-done | bytes 65568 | tf_op jit(solution)/shard_map/ppermute | solution.py:208
  12.8 3.3 %collective-permute-done.5 = bf16[4,64,128]{2,1,0:T(8,128)(2,1)S(1)} collective-permute-done((bf16[4,64,128]{2,1,0:T(8,128)(2,1)S(1)}, bf16[4,64,128]{2,1,0:T(8,128)(2,1)S(1)}, u32[]{:S(2)}, u32[]{:S(2)}) %collective-permute-start.5) | collective-permute-done | bytes 65568 | tf_op jit(solution)/shard_map/ppermute | solution.py:208
  16.1 1.7 %collective-permute-start.6 = (bf16[16,64,128]{2,1,0:T(8,128)(2,1)S(1)}, bf16[16,64,128]{2,1,0:T(8,128)(2,1)S(1)}, u32[]{:S(2)}, u32[]{:S(2)}) collective-permute-start(bf16[16,64,128]{2,1,0:T(8,128)(2,1)S(1)} %pad_maximum_fusion.refs_2_), channel_id=1, source_target_pairs={{0,1},{1,0},{2,3},{3,2},{4,5},{5,4},{6,7},{7,6},{8,9},{9,8},{10,11... | collective-permute-start | bytes 786440 | tf_op jit(solution)/shard_map/ppermute | solution.py:201
  17.9 0.2 collective-permute-start.7
  18.1 0.2 fusion.3
  18.3 0.0 copy-start.9
  18.4 0.0 copy-start
  18.4 0.7 %fusion.1.refs_6_ = bf16[8,7,128,128]{3,2,1,0:T(8,128)(2,1)S(1)} fusion(s32[]{:T(128)S(6)} %select_n.223, bf16[2,7,128,128]{3,2,1,0:T(8,128)(2,1)S(1)} %collective-permute-done.8, bf16[8,7,128,128]{3,2,1,0:T(8,128)(2,1)S(1)} %copy-done.4), kind=kLoop, calls=%fused_computation.5 | loop fusion | flops 1835008 | bytes 4128772 | tf_op jit(solution)/shard_map/concatenate | solution.py:248
  19.1 6.8 %collective-permute-done.7.refs_4_ = bf16[16,64,128]{2,1,0:T(8,128)(2,1)S(1)} collective-permute-done((bf16[16,64,128]{2,1,0:T(8,128)(2,1)S(1)}, bf16[16,64,128]{2,1,0:T(8,128)(2,1)S(1)}, u32[]{:S(2)}, u32[]{:S(2)}) %collective-permute-start.7) | collective-permute-done | bytes 262176 | tf_op jit(solution)/shard_map/ppermute | solution.py:204
  25.9 0.1 jit_solution_.3.refs_9_
  25.9 4.4 %shard_map.127.refs_2_ = bf16[4,12,16,128]{3,2,1,0:T(8,128)(2,1)S(1)} custom-call(s32[2]{0:T(128)S(1)} %pad_add_fusion.refs_0_, s32[8,4]{1,0:T(8,128)S(1)} %fusion.14.refs_1_, bf16[16,64,128]{2,1,0:T(8,128)(2,1)S(1)} %pad_maximum_fusion.refs_2_, bf16[16,64,128]{2,1,0:T(8,128)(2,1)S(1)} %collective-permute-done.6.refs_3_, ...), custom_call_target="tpu_custom_call" | custom-call | tf_op jit(solution)/shard_map/pallas_call | solution.py:173
  30.4 0.4 collective-permute-start.10
  30.7 0.4 collective-permute-start.9
  31.1 6.0 %collective-permute-done.10.refs_4_ = bf16[4,12,16,128]{3,2,1,0:T(8,128)(2,1)S(1)} collective-permute-done((bf16[4,12,16,128]{3,2,1,0:T(8,128)(2,1)S(1)}, bf16[4,12,16,128]{3,2,1,0:T(8,128)(2,1)S(1)}, u32[]{:S(2)}, u32[]{:S(2)}) %collective-permute-start.10) | collective-permute-done | bytes 196640 | tf_op jit(solution)/shard_map/ppermute | solution.py:204
  37.1 3.7 %shard_map.128 = bf16[16,32,128]{2,1,0:T(8,128)(2,1)S(1)} custom-call(s32[2]{0:T(128)S(1)} %pad_add_fusion.refs_0_, s32[8,4]{1,0:T(8,128)S(1)} %fusion.14.refs_1_, bf16[4,12,16,128]{3,2,1,0:T(8,128)(2,1)S(1)} %shard_map.127.refs_2_, bf16[4,12,16,128]{3,2,1,0:T(8,128)(2,1)S(1)} %collective-permute-done.9.refs_3_, ...), custom_call_target="tpu_custom_call" | custom-call | tf_op jit(solution)/shard_map/pallas_call | solution.py:173
  40.8 1.0 %collective-permute-start.11 = (bf16[4,32,128]{2,1,0:T(8,128)(2,1)S(1)}, bf16[4,32,128]{2,1,0:T(8,128)(2,1)S(1)}, u32[]{:S(2)}, u32[]{:S(2)}) collective-permute-start(bf16[4,32,128]{2,1,0:T(8,128)(2,1)S(1)} %get-tuple-element.16), channel_id=1, source_target_pairs={{0,4},{4,0},{8,12},{12,8},{1,5},{5,1},{9,13},{13,9},{2,6},{6,2},{1... | collective-permute-start | bytes 98312 | tf_op jit(solution)/shard_map/ppermute | solution.py:208
  41.8 1.4 %collective-permute-start.12 = (bf16[4,32,128]{2,1,0:T(8,128)(2,1)S(1)}, bf16[4,32,128]{2,1,0:T(8,128)(2,1)S(1)}, u32[]{:S(2)}, u32[]{:S(2)}) collective-permute-start(bf16[4,32,128]{2,1,0:T(8,128)(2,1)S(1)} %get-tuple-element.15), channel_id=1, source_target_pairs={{0,8},{4,12},{8,0},{12,4},{1,9},{5,13},{9,1},{13,5},{2,10},{6,14},... | collective-permute-start | bytes 98312 | tf_op jit(solution)/shard_map/ppermute | solution.py:208
  43.3 1.2 %collective-permute-start.13 = (bf16[4,32,128]{2,1,0:T(8,128)(2,1)S(1)}, bf16[4,32,128]{2,1,0:T(8,128)(2,1)S(1)}, u32[]{:S(2)}, u32[]{:S(2)}) collective-permute-start(bf16[4,32,128]{2,1,0:T(8,128)(2,1)S(1)} %get-tuple-element.14), channel_id=1, source_target_pairs={{0,12},{4,8},{8,4},{12,0},{1,13},{5,9},{9,5},{13,1},{2,14},{6,10},... | collective-permute-start | bytes 98312 | tf_op jit(solution)/shard_map/ppermute | solution.py:208
  44.4 1.4 %collective-permute-done.12 = bf16[4,32,128]{2,1,0:T(8,128)(2,1)S(1)} collective-permute-done((bf16[4,32,128]{2,1,0:T(8,128)(2,1)S(1)}, bf16[4,32,128]{2,1,0:T(8,128)(2,1)S(1)}, u32[]{:S(2)}, u32[]{:S(2)}) %collective-permute-start.12) | collective-permute-done | bytes 32800 | tf_op jit(solution)/shard_map/ppermute | solution.py:208
  45.8 2.0 %collective-permute-done.13 = bf16[4,32,128]{2,1,0:T(8,128)(2,1)S(1)} collective-permute-done((bf16[4,32,128]{2,1,0:T(8,128)(2,1)S(1)}, bf16[4,32,128]{2,1,0:T(8,128)(2,1)S(1)}, u32[]{:S(2)}, u32[]{:S(2)}) %collective-permute-start.13) | collective-permute-done | bytes 32800 | tf_op jit(solution)/shard_map/ppermute | solution.py:208
  47.9 0.1 broadcast_select_fusion.4
  47.9 2.0 %collective-permute-start.14 = (bf16[2,4,8,4,128]{4,3,2,1,0:T(4,128)(2,1)S(1)}, bf16[2,4,8,4,128]{4,3,2,1,0:T(4,128)(2,1)S(1)}, u32[]{:S(2)}, u32[]{:S(2)}) collective-permute-start(bf16[2,4,8,4,128]{4,3,2,1,0:T(4,128)(2,1)S(1)} %broadcast_select_fusion.4), channel_id=1, source_target_pairs={{0,1},{1,0},{2,3},{3,2},{4,5},{5,4},{6,7},{7,6},{8,9},{9,8},{10,11... | collective-permute-start | bytes 196616 | tf_op jit(solution)/shard_map/ppermute | solution.py:201
  49.9 0.9 %collective-permute-done.14 = bf16[2,4,8,4,128]{4,3,2,1,0:T(4,128)(2,1)S(1)} collective-permute-done((bf16[2,4,8,4,128]{4,3,2,1,0:T(4,128)(2,1)S(1)}, bf16[2,4,8,4,128]{4,3,2,1,0:T(4,128)(2,1)S(1)}, u32[]{:S(2)}, u32[]{:S(2)}) %collective-permute-start.14) | collective-permute-done | bytes 65568 | tf_op jit(solution)/shard_map/ppermute | solution.py:201
  50.8 0.1 broadcast_select_fusion.7
  50.9 0.1 pad_maximum_fusion.3
  51.0 0.6 %gather_fusion = bf16[2,4,8,8,128]{4,3,2,1,0:T(8,128)(2,1)S(1)} fusion(bf16[2,4,8,8,128]{4,3,2,1,0:T(8,128)(2,1)S(1)} %pad_maximum_fusion.3, s32[1024]{0:T(1024)S(1)} %pad_clamp_fusion), kind=kCustom, calls=%fused_computation | custom fusion | bytes 262152 | tf_op jit(solution)/shard_map/jit(_take)/gather | solution.py:320
  51.6 0.1 convert_bitcast_fusion
  51.7 0.7 %copy.27 = f32[4,2,8,8,128]{4,3,2,1,0:T(8,128)} copy(f32[4,2,8,8,128]{4,3,2,0,1:T(8,128)S(1)} %convert_bitcast_fusion) | data formatting | bytes 524288 | tf_op jit(solution)/shard_map/convert_element_type | solution.py:322
  (51 shorter events, 0.3 us)
Async XLA Ops:
  0.0 6.5 %copy-start.11 = (s32[4]{0:T(128)S(1)}, s32[4]{0:T(128)}, u32[]{:S(2)}) copy-start(s32[4]{0:T(128)} %constant.189.clone) | copy-start | bytes 52
  0.0 11.1 %copy-start.7 = (f32[16,8,128]{2,1,0:T(8,128)S(1)}, f32[16,8,128]{2,1,0:T(8,128)}, u32[]{:S(2)}) copy-start(f32[16,8,128]{2,1,0:T(8,128)} %param.14) | copy-start | bytes 196612
  0.0 11.1 %copy-start.6 = (f32[16,8,128]{2,1,0:T(8,128)S(1)}, f32[16,8,128]{2,1,0:T(8,128)}, u32[]{:S(2)}) copy-start(f32[16,8,128]{2,1,0:T(8,128)} %param.15) | copy-start | bytes 196612
  0.0 11.1 %copy-start.5 = (f32[16,8,128]{2,1,0:T(8,128)S(1)}, f32[16,8,128]{2,1,0:T(8,128)}, u32[]{:S(2)}) copy-start(f32[16,8,128]{2,1,0:T(8,128)} %param.16) | copy-start | bytes 196612
  0.0 6.5 %copy-start.10 = (s32[8,4]{0,1:T(4,128)S(1)}, s32[8,4]{0,1:T(4,128)}, u32[]{:S(2)}) copy-start(s32[8,4]{0,1:T(4,128)} %param.19) | copy-start | bytes 388
  1.2 6.1 %collective-permute-start.2 = (bf16[4,64,128]{2,1,0:T(8,128)(2,1)S(1)}, bf16[4,64,128]{2,1,0:T(8,128)(2,1)S(1)}, u32[]{:S(2)}, u32[]{:S(2)}) collective-permute-start(bf16[4,64,128]{2,1,0:T(8,128)(2,1)S(1)} %bitcast.50), channel_id=1, source_target_pairs={{0,1},{1,0},{2,3},{3,2},{4,5},{5,4},{6,7},{7,6},{8,9},{9,8},{10,11... | collective-permute-start | bytes 196616 | tf_op jit(solution)/shard_map/ppermute | solution.py:201
  2.2 8.9 %collective-permute-start = (f32[3,16,8,128]{3,2,1,0:T(8,128)S(1)}, f32[3,16,8,128]{3,2,1,0:T(8,128)S(1)}, u32[]{:S(2)}, u32[]{:S(2)}) collective-permute-start(f32[3,16,8,128]{3,2,1,0:T(8,128)S(1)} %pad_maximum_fusion.1), channel_id=1, source_target_pairs={{0,1},{1,0},{2,3},{3,2},{4,5},{5,4},{6,7},{7,6},{8,9},{9,8},{10,11... | collective-permute-start | bytes 589832 | tf_op jit(solution)/shard_map/ppermute | solution.py:201
  2.7 8.5 %copy-start.8 = (f32[8,128]{1,0:T(8,128)S(1)}, f32[8,128]{1,0:T(8,128)}, u32[]{:S(2)}) copy-start(f32[8,128]{1,0:T(8,128)} %param.17) | copy-start | bytes 12292
  3.8 14.6 %collective-permute-start.8 = (bf16[2,7,128,128]{3,2,1,0:T(8,128)(2,1)S(1)}, bf16[2,7,128,128]{3,2,1,0:T(8,128)(2,1)S(1)}, u32[]{:S(2)}, u32[]{:S(2)}) collective-permute-start(bf16[2,7,128,128]{3,2,1,0:T(8,128)(2,1)S(1)} %constant_dynamic-slice_fusion), channel_id=1, source_target_pairs={{1,2},{2,1},{3,0},{0,3},{5,6},{6,5},{7,4},{4,7},{9,10},{10,9},{11,... | collective-permute-start | bytes 1376264 | tf_op jit(solution)/shard_map/ppermute | solution.py:204
  7.4 11.0 %copy-start.4 = (bf16[8,7,128,128]{3,2,1,0:T(8,128)(2,1)S(1)}, bf16[8,7,128,128]{3,2,1,0:T(8,128)(2,1)}, u32[]{:S(2)}) copy-start(bf16[8,7,128,128]{3,2,1,0:T(8,128)(2,1)} %param.18) | copy-start | bytes 5505028
  7.4 4.8 %collective-permute-start.3 = (bf16[4,64,128]{2,1,0:T(8,128)(2,1)S(1)}, bf16[4,64,128]{2,1,0:T(8,128)(2,1)S(1)}, u32[]{:S(2)}, u32[]{:S(2)}) collective-permute-start(bf16[4,64,128]{2,1,0:T(8,128)(2,1)S(1)} %get-tuple-element.12), channel_id=1, source_target_pairs={{0,4},{4,0},{8,12},{12,8},{1,5},{5,1},{9,13},{13,9},{2,6},{6,2},{1... | collective-permute-start | bytes 196616 | tf_op jit(solution)/shard_map/ppermute | solution.py:208
  8.8 4.0 %collective-permute-start.4 = (bf16[4,64,128]{2,1,0:T(8,128)(2,1)S(1)}, bf16[4,64,128]{2,1,0:T(8,128)(2,1)S(1)}, u32[]{:S(2)}, u32[]{:S(2)}) collective-permute-start(bf16[4,64,128]{2,1,0:T(8,128)(2,1)S(1)} %get-tuple-element.11), channel_id=1, source_target_pairs={{0,8},{4,12},{8,0},{12,4},{1,9},{5,13},{9,1},{13,5},{2,10},{6,14},... | collective-permute-start | bytes 196616 | tf_op jit(solution)/shard_map/ppermute | solution.py:208
  11.1 5.0 %collective-permute-start.5 = (bf16[4,64,128]{2,1,0:T(8,128)(2,1)S(1)}, bf16[4,64,128]{2,1,0:T(8,128)(2,1)S(1)}, u32[]{:S(2)}, u32[]{:S(2)}) collective-permute-start(bf16[4,64,128]{2,1,0:T(8,128)(2,1)S(1)} %get-tuple-element.10), channel_id=1, source_target_pairs={{0,12},{4,8},{8,4},{12,0},{1,13},{5,9},{9,5},{13,1},{2,14},{6,10},... | collective-permute-start | bytes 196616 | tf_op jit(solution)/shard_map/ppermute | solution.py:208
  11.3 6.8 %collective-permute-start.1 = (f32[50,2,128]{2,1,0:T(2,128)S(1)}, f32[50,2,128]{2,1,0:T(2,128)S(1)}, u32[]{:S(2)}, u32[]{:S(2)}) collective-permute-start(f32[50,2,128]{2,1,0:T(2,128)S(1)} %fusion.13), channel_id=1, source_target_pairs={{1,2},{2,1},{3,0},{0,3},{5,6},{6,5},{7,4},{4,7},{9,10},{10,9},{11,... | collective-permute-start | bytes 153608 | tf_op jit(solution)/shard_map/ppermute | solution.py:204
  16.1 3.0 %collective-permute-start.6 = (bf16[16,64,128]{2,1,0:T(8,128)(2,1)S(1)}, bf16[16,64,128]{2,1,0:T(8,128)(2,1)S(1)}, u32[]{:S(2)}, u32[]{:S(2)}) collective-permute-start(bf16[16,64,128]{2,1,0:T(8,128)(2,1)S(1)} %pad_maximum_fusion.refs_2_), channel_id=1, source_target_pairs={{0,1},{1,0},{2,3},{3,2},{4,5},{5,4},{6,7},{7,6},{8,9},{9,8},{10,11... | collective-permute-start | bytes 786440 | tf_op jit(solution)/shard_map/ppermute | solution.py:201
  17.9 8.0 %collective-permute-start.7 = (bf16[16,64,128]{2,1,0:T(8,128)(2,1)S(1)}, bf16[16,64,128]{2,1,0:T(8,128)(2,1)S(1)}, u32[]{:S(2)}, u32[]{:S(2)}) collective-permute-start(bf16[16,64,128]{2,1,0:T(8,128)(2,1)S(1)} %pad_maximum_fusion.refs_2_), channel_id=1, source_target_pairs={{1,2},{2,1},{3,0},{0,3},{5,6},{6,5},{7,4},{4,7},{9,10},{10,9},{11,... | collective-permute-start | bytes 786440 | tf_op jit(solution)/shard_map/ppermute | solution.py:204
  18.3 7.5 %copy-start.9 = (f32[3,8]{1,0:T(4,128)S(1)}, f32[3,8]{1,0:T(4,128)}, u32[]{:S(2)}) copy-start(f32[3,8]{1,0:T(4,128)} %constant.190.clone) | copy-start | bytes 292
  18.4 7.6 %copy-start = (bf16[224,224]{1,0:T(8,128)(2,1)S(1)}, bf16[224,224]{1,0:T(8,128)(2,1)}, u32[]{:S(2)}) copy-start(bf16[224,224]{1,0:T(8,128)(2,1)} %constant.199.refs_10_) | copy-start | bytes 301060
  18.4 7.6 %copy-start.1 = (bf16[192,192]{1,0:T(8,128)(2,1)S(1)}, bf16[192,192]{1,0:T(8,128)(2,1)}, u32[]{:S(2)}) copy-start(bf16[192,192]{1,0:T(8,128)(2,1)} %constant.200.refs_11_) | copy-start | bytes 221188
  19.1 18.0 %copy-start.2 = (bf16[160,160]{1,0:T(8,128)(2,1)S(1)}, bf16[160,160]{1,0:T(8,128)(2,1)}, u32[]{:S(2)}) copy-start(bf16[160,160]{1,0:T(8,128)(2,1)} %constant.201.refs_10_) | copy-start | bytes 153604
  19.1 18.0 %copy-start.3 = (bf16[128,128]{1,0:T(8,128)(2,1)S(1)}, bf16[128,128]{1,0:T(8,128)(2,1)}, u32[]{:S(2)}) copy-start(bf16[128,128]{1,0:T(8,128)(2,1)} %constant.202.refs_11_) | copy-start | bytes 98308
  30.4 6.7 %collective-permute-start.10 = (bf16[4,12,16,128]{3,2,1,0:T(8,128)(2,1)S(1)}, bf16[4,12,16,128]{3,2,1,0:T(8,128)(2,1)S(1)}, u32[]{:S(2)}, u32[]{:S(2)}) collective-permute-start(bf16[4,12,16,128]{3,2,1,0:T(8,128)(2,1)S(1)} %shard_map.127.refs_2_), channel_id=1, source_target_pairs={{1,2},{2,1},{3,0},{0,3},{5,6},{6,5},{7,4},{4,7},{9,10},{10,9},{11,... | collective-permute-start | bytes 589832 | tf_op jit(solution)/shard_map/ppermute | solution.py:204
  30.7 6.4 %collective-permute-start.9 = (bf16[4,12,16,128]{3,2,1,0:T(8,128)(2,1)S(1)}, bf16[4,12,16,128]{3,2,1,0:T(8,128)(2,1)S(1)}, u32[]{:S(2)}, u32[]{:S(2)}) collective-permute-start(bf16[4,12,16,128]{3,2,1,0:T(8,128)(2,1)S(1)} %shard_map.127.refs_2_), channel_id=1, source_target_pairs={{0,1},{1,0},{2,3},{3,2},{4,5},{5,4},{6,7},{7,6},{8,9},{9,8},{10,11... | collective-permute-start | bytes 589832 | tf_op jit(solution)/shard_map/ppermute | solution.py:201
  40.8 3.6 %collective-permute-start.11 = (bf16[4,32,128]{2,1,0:T(8,128)(2,1)S(1)}, bf16[4,32,128]{2,1,0:T(8,128)(2,1)S(1)}, u32[]{:S(2)}, u32[]{:S(2)}) collective-permute-start(bf16[4,32,128]{2,1,0:T(8,128)(2,1)S(1)} %get-tuple-element.16), channel_id=1, source_target_pairs={{0,4},{4,0},{8,12},{12,8},{1,5},{5,1},{9,13},{13,9},{2,6},{6,2},{1... | collective-permute-start | bytes 98312 | tf_op jit(solution)/shard_map/ppermute | solution.py:208
  41.8 4.0 %collective-permute-start.12 = (bf16[4,32,128]{2,1,0:T(8,128)(2,1)S(1)}, bf16[4,32,128]{2,1,0:T(8,128)(2,1)S(1)}, u32[]{:S(2)}, u32[]{:S(2)}) collective-permute-start(bf16[4,32,128]{2,1,0:T(8,128)(2,1)S(1)} %get-tuple-element.15), channel_id=1, source_target_pairs={{0,8},{4,12},{8,0},{12,4},{1,9},{5,13},{9,1},{13,5},{2,10},{6,14},... | collective-permute-start | bytes 98312 | tf_op jit(solution)/shard_map/ppermute | solution.py:208
  43.3 4.6 %collective-permute-start.13 = (bf16[4,32,128]{2,1,0:T(8,128)(2,1)S(1)}, bf16[4,32,128]{2,1,0:T(8,128)(2,1)S(1)}, u32[]{:S(2)}, u32[]{:S(2)}) collective-permute-start(bf16[4,32,128]{2,1,0:T(8,128)(2,1)S(1)} %get-tuple-element.14), channel_id=1, source_target_pairs={{0,12},{4,8},{8,4},{12,0},{1,13},{5,9},{9,5},{13,1},{2,14},{6,10},... | collective-permute-start | bytes 98312 | tf_op jit(solution)/shard_map/ppermute | solution.py:208
  47.9 2.9 %collective-permute-start.14 = (bf16[2,4,8,4,128]{4,3,2,1,0:T(4,128)(2,1)S(1)}, bf16[2,4,8,4,128]{4,3,2,1,0:T(4,128)(2,1)S(1)}, u32[]{:S(2)}, u32[]{:S(2)}) collective-permute-start(bf16[2,4,8,4,128]{4,3,2,1,0:T(4,128)(2,1)S(1)} %broadcast_select_fusion.4), channel_id=1, source_target_pairs={{0,1},{1,0},{2,3},{3,2},{4,5},{5,4},{6,7},{7,6},{8,9},{9,8},{10,11... | collective-permute-start | bytes 196616 | tf_op jit(solution)/shard_map/ppermute | solution.py:201

commit v2 on v1

v2 whole, which is shorter than its diff:
```python
import math

import jax
import jax.numpy as jnp
import numpy as np
from jax import lax
from jax.experimental import pallas as pl
from jax.experimental.pallas import tpu as pltpu
from jax.sharding import PartitionSpec as P

NEWTON = 2
APPLICATIONS = 2 * NEWTON
OFFSETS = (-2, -1, 1, 2)
GROUP = 4

corner_weight = 0.25


def transform_tables(steps):
    beta = corner_weight ** (1.0 / steps)
    half = steps // 2
    counter = np.arange(steps)
    angle = ((counter[:, None] * counter[None, :]) % steps) * (2.0 * math.pi / steps)
    rising = np.power(beta, counter)
    falling = np.power(beta, -counter.astype(np.float64)) / steps
    fwd_re = np.cos(angle) * rising[None, :]
    fwd_im = -np.sin(angle) * rising[None, :]
    back_re = np.cos(angle) * falling[:, None]
    back_im = -np.sin(angle) * falling[:, None]
    forward = np.concatenate([fwd_re[:half], fwd_re[half : half + 1], fwd_im[1:half]], 0)
    twice = np.where(np.arange(half) == 0, 1.0, 2.0)
    backward = np.concatenate(
        [
            back_re[:, :half] * twice,
            back_re[:, half : half + 1],
            back_im[:, 1:half] * 2.0,
        ],
        1,
    )
    phase = counter * (2.0 * math.pi / steps)
    eigen_re = 1.0 - beta * np.cos(phase)
    eigen_im = beta * np.sin(phase)
    low_re = eigen_re[:half]
    low_im = np.where(np.arange(half) == 0, 0.0, eigen_im[:half])
    high_re = np.concatenate([eigen_re[half : half + 1], eigen_re[1:half]])
    eigen = np.stack([low_re, low_im, high_re]).astype(np.float32)
    return forward, backward, eigen


def newton(values, weights_of, coef, diag, forward, backward, packed, spec, inverse,
           base, window_at, all_layers, write):
    layers, steps, width = values.shape[1:]
    half = steps // 2
    wide, inner = layers - 2, layers - 4
    sublane = lax.broadcasted_iota(jnp.int32, (half, width), 0)
    eigen = []
    for numbers in transform_tables(steps)[2]:
        column = jnp.full((half, width), float(numbers[0]), jnp.float32)
        for at in range(1, half):
            column = jnp.where(sublane == at, float(numbers[at]), column)
        eigen.append(column)

    def applied(array, at, low, count, element):
        parts = [array[at, low : low + count]]
        for offset in OFFSETS:
            parts.append(array[at + offset, low : low + count])
        parts.append(array[at, low - 1 : low - 1 + count])
        parts.append(array[at, low + 1 : low + 1 + count])
        rows = jnp.concatenate([part.reshape(count * steps, width) for part in parts], axis=1)
        weights = jnp.concatenate(weights_of(element), axis=0)
        out = jnp.dot(rows, weights, preferred_element_type=jnp.float32)
        return out.reshape(count, steps, width)

    for element in range(8):
        mid = 2 <= element < 6
        low, count = (1, wide) if mid else (2, inner)
        image = applied(values, element + 2, low, count, element)
        state = values[element + 2, low : low + count].astype(jnp.float32)
        rows = slice(window_at + low, window_at + low + count)
        start = coef[0, rows, element : element + 1, :]
        reaction = coef[1, rows, element : element + 1, :]
        source = coef[2, rows, element : element + 1, :]
        own = diag[element : element + 1, :][None]
        time = lax.broadcasted_iota(jnp.int32, (count, steps, width), 1)
        previous = jnp.where(time == 0, start, pltpu.roll(state, 1, 1))
        residual = (
            state - previous + own * state + image + reaction * state * state * state - source
        )
        rhs = (-residual).astype(jnp.bfloat16).reshape(count * steps, width)
        cut = count * steps
        out = jnp.dot(forward[:cut, :cut], rhs, preferred_element_type=jnp.float32)
        out = out.astype(jnp.bfloat16).astype(jnp.float32).reshape(count, steps, width)
        layer = lax.broadcasted_iota(jnp.int32, (count, 1, width), 0) + (base + window_at + low)
        inside = jnp.where((layer >= 0) & (layer < all_layers), 1.0, 0.0).astype(jnp.float32)
        real = own + 3.0 * reaction * start * start
        near = eigen[0][None] + real
        far = eigen[2][None] + real
        imag = eigen[1][None]
        near_over = inside / (near * near + imag * imag)
        far_over = inside / (far * far + imag * imag)
        first = near * near_over
        cross = -imag * near_over
        last = far * far_over
        part_a, part_b = out[:, :half], out[:, half:]
        sol = jnp.concatenate(
            [first * part_a - cross * part_b, cross * part_a + last * part_b], axis=1
        )
        packed[element, low - 1 : low - 1 + count] = sol.astype(jnp.bfloat16)
        if mid:
            spec[element - 2] = out
            inverse[element - 2, 0] = first
            inverse[element - 2, 1] = cross
            inverse[element - 2, 2] = last
    for own in range(4):
        image = applied(packed, own + 2, 1, inner, own + 2)
        left = spec[own, 1 : 1 + inner] - image
        part_a, part_b = left[:, :half], left[:, half:]
        first = inverse[own, 0, 1 : 1 + inner]
        cross = inverse[own, 1, 1 : 1 + inner]
        last = inverse[own, 2, 1 : 1 + inner]
        final = jnp.concatenate(
            [first * part_a - cross * part_b, cross * part_a + last * part_b], axis=1
        )
        final = final.astype(jnp.bfloat16).reshape(inner * steps, width)
        delta = jnp.dot(backward[...], final, preferred_element_type=jnp.float32)
        delta = delta.astype(jnp.bfloat16).astype(jnp.float32).reshape(inner, steps, width)
        state = values[own + 4, 2 : 2 + inner].astype(jnp.float32) + delta
        write(own, state.astype(jnp.bfloat16))


def chooser(where, tiles, edge_tiles, total):
    core, first = where[0, 0], where[0, 2]

    def blocks(table, ids, at, element, row):
        places = [0]
        for offset in OFFSETS:
            wanted = lax.rem(element + (offset + total), total)
            slot = jnp.int32(1)
            for column in range(1, 4):
                slot = jnp.where(where[ids + column, at] == wanted, column + 1, slot)
            places.append(slot)
        return [table[row, place] for place in places + [5, 6]]

    def weights_of(element):
        local = element - 2 + 4 * core
        number = first + local + total
        if 2 <= element < 6:
            return blocks(tiles, 1, local, number, local)
        outer = element if element < 2 else element - 6
        inside = element + 2 if element < 2 else element - 2
        here = blocks(tiles, 1, inside, number, inside)
        there = blocks(edge_tiles, 5, 6 - 6 * core + outer, number, outer)
        away = core == (0 if element < 2 else 1)
        return [jnp.where(away, two, one) for one, two in zip(here, there)]

    return weights_of


def fields_kernel(where, start, reaction, source, start_two, reaction_two, source_two, diag,
                  ids, _, bundle, edge):
    layers = start.shape[0]
    core, base = where[0], where[1]
    window = bundle.shape[0] // 3
    for at, (one, two) in enumerate(
        ((start, start_two), (reaction, reaction_two), (source, source_two))
    ):
        for place in range(window):
            layer = jnp.clip(base + place, 0, 2 * layers - 1)
            own = layer // layers == core
            layer = lax.rem(layer, layers)
            row = jnp.where(own, one[layer], two[layer])
            bundle[at * window + place] = row
            edge[at * window + place] = jnp.where(core == 0, row[0:2], row[6:8])
    edge[3 * window] = jnp.where(core == 0, diag[0:2], diag[6:8])
    for at in range(2):
        edge[3 * window + 1 + at, :, 0:8] = ids[2 * at : 2 * at + 2].astype(jnp.float32)


def first_kernel(all_layers, total, count, where, order, tiles, edge_one, edge_two, bundle,
                 bundle_edge, diag_own, forward, backward, *rest):
    chunks = [rest[count * k : count * (k + 1)] for k in range(3)]
    out, message, coef, diag, edge_tiles, arrived, values, packed, spec, inverse = rest[3 * count :]
    steps, rows, width = arrived.shape[1:]
    core, mine = where[0, 0], where[0, 3]
    local = steps // count
    for at, parts in ((1, chunks[0]), (2 - 2 * core, chunks[1]), (2 * core, chunks[2])):
        for k, part in enumerate(parts):
            arrived[at, pl.ds(lax.bitwise_xor(mine, k) * local, local)] = part[...]
    size = steps * GROUP * 4
    groups = rows // (GROUP * 4)
    for at in range(3):
        for group in range(0, groups, 2):
            both = [
                arrived[at, :, place * GROUP * 4 : (place + 1) * GROUP * 4].reshape(size, width)
                for place in range(group, min(group + 2, groups))
            ]
            moved = jnp.dot(
                order[...], jnp.concatenate(both, axis=1), preferred_element_type=jnp.float32
            ).astype(jnp.bfloat16)
            for k in range(len(both)):
                values[4 * at : 4 * at + 4, (group + k) * GROUP : (group + k + 1) * GROUP] = moved[
                    :, k * width : (k + 1) * width
                ].reshape(4, GROUP, steps, width)

    window = bundle.shape[0] // 3
    sublane = lax.broadcasted_iota(jnp.int32, (8, width), 0)

    def widened(row, pair):
        turned = jnp.where(core == 0, pltpu.roll(row, 2, 0), pltpu.roll(row, 6, 0))
        for k in range(2):
            turned = jnp.where(
                sublane == 6 * core + k, jnp.broadcast_to(pair[k : k + 1], (8, width)), turned
            )
        return turned

    for at in range(3):
        for place in range(window):
            coef[at, place] = widened(bundle[at * window + place], bundle_edge[at * window + place])
    diag[...] = widened(diag_own[...], bundle_edge[3 * window])
    edge_tiles[where[0, 4]] = edge_one[...]
    edge_tiles[1 - where[0, 4]] = edge_two[...]

    def write(element, state):
        out[element] = state

    weights_of = chooser(where, tiles, edge_tiles, total)
    newton(values, weights_of, coef, diag, forward, backward, packed, spec, inverse,
           where[0, 1], 0, all_layers, write)
    layers = out.shape[1]
    for at in range(2):
        message[at * (layers - 2) : (at + 1) * (layers - 2)] = out[2 * core + at, 1 : layers - 1]
        begin = 2 * (layers - 2) + at * (layers - 4)
        message[begin : begin + layers - 4] = out[2 - 2 * core + at, 2 : layers - 2]


def second_kernel(all_layers, total, count, where, order, tiles,
                  edge_tiles, coef, diag, forward, backward, own, beside, across, out,
                  values, packed, spec, inverse, solved):
    core, mine = where[0, 0], where[0, 3]
    layers, steps, width = own.shape[1:]
    values[4:8] = own[...]
    values[pl.ds(8 - 8 * core, 4)] = beside[...]
    for at in range(2):
        values[2 + 6 * core + at, 1 : layers - 1] = across[
            at * (layers - 2) : (at + 1) * (layers - 2)
        ]
        begin = 2 * (layers - 2) + at * (layers - 4)
        values[10 * core + at, 2 : layers - 2] = across[begin : begin + layers - 4]

    def write(element, state):
        solved[element] = state

    weights_of = chooser(where, tiles, edge_tiles, total)
    newton(values, weights_of, coef, diag, forward, backward, packed, spec, inverse,
           where[0, 1], 2, all_layers, write)
    size = steps * GROUP * 4
    local = steps // count
    half = count // 2
    for group in range(solved.shape[1] // GROUP):
        part = solved[:, group * GROUP : (group + 1) * GROUP].reshape(size, width)
        moved = jnp.dot(order[...], part, preferred_element_type=jnp.float32)
        moved = moved.astype(jnp.bfloat16).reshape(steps, GROUP * 4, width)
        cut = pl.ds(group * GROUP * 4, GROUP * 4)
        for goal in range(count):
            side = lax.bitwise_xor(goal // half, core)
            place = lax.bitwise_xor(goal % half, lax.rem(mine, half))
            out[side, pl.ds(place * local, local), cut] = moved[goal * local : (goal + 1) * local]


def last_kernel(count, where, order, *rest):
    parts, out = rest[:-1], rest[-1]
    steps, layers, elems, width = out.shape
    half = count // 2
    layers //= half
    mine = where[3]
    upper, lower = mine // half, lax.rem(mine, half)
    for k, part in enumerate(parts):
        both = [part[lax.bitwise_xor(upper, side)].reshape(-1, width) for side in range(2)]
        moved = jnp.dot(
            order[...], jnp.concatenate(both, axis=0), preferred_element_type=jnp.float32
        )
        place = lax.bitwise_xor(lower, k)
        out[:, pl.ds(place * layers, layers)] = moved.reshape(steps, layers, elems, width)


def call(kernel, out_shape, scratch, scalars, arrays, later_than=()):
    vmem = pl.BlockSpec(memory_space=pltpu.VMEM)
    return pl.pallas_call(
        kernel,
        out_shape=out_shape,
        in_specs=[pl.BlockSpec(memory_space=pltpu.SMEM)] * len(scalars)
        + [vmem] * len(arrays)
        + [pl.BlockSpec(memory_space=pl.ANY)] * len(later_than),
        out_specs=jax.tree.map(lambda _: vmem, out_shape),
        scratch_shapes=scratch,
        compiler_params=pltpu.CompilerParams(vmem_limit_bytes=32 * 1024 * 1024),
    )(*scalars, *arrays, *later_than)


def shards(state_guess, start_state, reaction, source, self_diag, tiles, neighbors):
    local_steps, local_layers, local_elems, width = state_guess.shape
    count = lax.axis_size("tm")
    sections = lax.axis_size("space")
    mine, core = lax.axis_index("tm"), lax.axis_index("layer")
    steps = local_steps * count
    all_layers = local_layers * 2
    chip_layers = all_layers // count
    window = -(-(chip_layers + 2 * APPLICATIONS) // GROUP) * GROUP
    half = local_elems // 2
    swap = [(0, 1), (1, 0)]
    circle = []
    for section in range(sections):
        one, other = 2 * section + 1, 2 * ((section + 1) % sections)
        circle += [(one, other), (other, one)]

    def over_core(array):
        return lax.ppermute(array, "layer", swap)

    def over_circle(array):
        return lax.ppermute(array, ("space", "layer"), circle)

    def exchanged(parts):
        return [parts[0]] + [
            lax.ppermute(parts[k], "tm", [(i, i ^ k) for i in range(count)])
            for k in range(1, count)
        ]

    def held(shape, dtype=jnp.bfloat16):
        return jax.ShapeDtypeStruct(shape, dtype)

    pair = state_guess.astype(jnp.bfloat16).reshape(local_steps, local_layers, 2, half, width)
    flat = (local_steps, local_layers * half, width)
    keep = lax.dynamic_index_in_dim(pair, core, 2, keepdims=False).reshape(flat)
    give = lax.dynamic_index_in_dim(pair, 1 - core, 2, keepdims=False).reshape(flat)
    got = over_core(give)
    below = jnp.zeros((local_steps, APPLICATIONS * half, width), jnp.bfloat16)
    above = jnp.zeros(
        (local_steps, (window - chip_layers - APPLICATIONS) * half, width), jnp.bfloat16
    )
    whole = jnp.concatenate(
        [below, jnp.where(core == 0, keep, got), jnp.where(core == 0, got, keep), above], 1
    )
    pieces = [
        lax.dynamic_slice_in_dim(
            whole, lax.bitwise_xor(mine, k) * (chip_layers * half), window * half, 1
        )
        for k in range(count)
    ]
    chunks = exchanged(pieces)
    across = [over_circle(chunk) for chunk in chunks]
    beside = [over_core(chunk) for chunk in chunks]

    section = lax.axis_index("space") * local_elems
    place = jnp.stack(
        [core, mine * chip_layers - APPLICATIONS, section, mine, lax.axis_index("group")]
    ).astype(jnp.int32)
    edge_one = over_circle(
        lax.dynamic_index_in_dim(tiles, 6 * core + lax.axis_index("group"), 0, keepdims=False)
    )
    edge_two = lax.ppermute(edge_one, "group", swap)
    fields = (start_state, reaction, source)
    others = [over_core(field) for field in fields]
    ids = neighbors.T
    bundle, bundle_edge = call(
        fields_kernel,
        (
            held((3 * window, local_elems, width), jnp.float32),
            held((3 * window + 3, 2, width), jnp.float32),
        ),
        [],
        [place],
        [*fields, *others, self_diag, ids],
        [chunks[1]],
    )
    bundle_edge = over_circle(bundle_edge)
    edge_ids = bundle_edge[3 * window + 1 :, :, :local_elems].reshape(4, local_elems)
    where = jnp.concatenate(
        [jnp.pad(place[None], ((0, 0), (0, local_elems - 5))), ids, edge_ids.astype(jnp.int32)], 0
    )

    forward, backward, _ = transform_tables(steps)
    order = np.zeros((4, GROUP, steps, steps, GROUP, 4), np.float32)
    for element in range(4):
        for layer in range(GROUP):
            order[element, layer, :, :, layer, element] = np.eye(steps)
    order = order.reshape(4 * GROUP * steps, steps * GROUP * 4)
    last = window - 8
    order_last = np.zeros(
        (local_steps, chip_layers, 2, half, 2, local_steps, last, half), np.float32
    )
    for step in range(local_steps):
        for layer in range(chip_layers):
            for side in range(2):
                order_last[step, layer, side, :, side, step, layer, :] = np.eye(half)
    order_last = order_last.reshape(local_steps * chip_layers * 2 * half, -1)

    def constant(matrix):
        return jnp.asarray(matrix.astype(jnp.bfloat16))

    def table(matrix, layers):
        return constant(np.kron(np.eye(layers), matrix))

    def scratch(layers):
        return [
            pltpu.VMEM((12, layers, steps, width), jnp.bfloat16),
            pltpu.VMEM((8, layers - 2, steps, width), jnp.bfloat16),
            pltpu.VMEM((4, layers - 2, steps, width), jnp.float32),
            pltpu.VMEM((4, 3, layers - 2, steps // 2, width), jnp.float32),
        ]

    total = local_elems * sections
    state, edge, coef, diag, edge_tiles = call(
        lambda *refs: first_kernel(all_layers, total, count, *refs),
        (
            held((4, window - 4, steps, width)),
            held((2 * (window - 6) + 2 * (window - 8), steps, width)),
            held((3, window, 8, width), jnp.float32),
            held((8, width), jnp.float32),
            held((2,) + tiles.shape[1:]),
        ),
        [pltpu.VMEM((3, steps, window * half, width), jnp.bfloat16)] + scratch(window),
        [where],
        [constant(order), tiles, edge_one, edge_two, bundle, bundle_edge, self_diag,
         table(forward, window - 2), table(backward, window - 4), *chunks, *beside, *across],
    )
    solved = call(
        lambda *refs: second_kernel(all_layers, total, count, *refs),
        held((2, steps // 2, last * half, width)),
        scratch(window - 4) + [pltpu.VMEM((4, last, steps, width), jnp.bfloat16)],
        [where],
        [constant(order.T), tiles, edge_tiles, coef, diag,
         table(forward, window - 6), table(backward, last),
         state, over_core(state), over_circle(edge)],
    )

    keep, got = solved[0], over_core(solved[1])
    parts = []
    for k in range(count // 2):
        cut = slice(k * local_steps, (k + 1) * local_steps)
        pairs = []
        for device in range(count):
            high, low = device // (count // 2), device % (count // 2)
            for side in range(2):
                goal = side * (count // 2) + (low ^ k)
                pairs.append((2 * device + side, 2 * goal + high))
        parts.append(lax.ppermute(jnp.stack([keep[cut], got[cut]]), ("tm", "layer"), pairs))
    return call(
        lambda *refs: last_kernel(count, *refs),
        held(state_guess.shape, jnp.float32),
        [],
        [place],
        [constant(order_last), *parts],
    )


def solution(mesh):
    in_specs = (
        P("tm", ("group", "layer"), "space", None),
        P(("group", "layer"), "space", None),
        P(("group", "layer"), "space", None),
        P(("group", "layer"), "space", None),
        P("space", None),
        P("space", None, None, None),
        P("space", None),
    )
    out_specs = P("tm", ("group", "layer"), "space", None)
    return jax.shard_map(shards, mesh=mesh, in_specs=in_specs, out_specs=out_specs, check_vma=False)
```

time: 52.9 us -> 51.8 us (0.979)
  waiting for transfers between devices: 21 us -> 15.9 us
  starting transfers between devices: 16.1 us -> 21 us
  other arithmetic: 3.87 us -> 1.13 us
  Pallas kernels: 8.09 us -> 9.98 us
    ppermute x0 -> x3, starting transfers between devices: none -> 6.27 us  [the longest x2 5.03 us: shards(): lax.ppermute(jnp.stack([keep[cut], got[cut]]), ('tm', 'layer'), pairs)]
    ppermute x6 -> x3, waiting for transfers between devices: 7.35 us -> 2.06 us  [exchanged(): lax.ppermute(parts[k], 'tm', [(i, i ^ k) for i in range(count)])]
    ppermute x0 -> x3, waiting for transfers between devices: none -> 4.18 us  [the longest x2 4.18 us: shards(): lax.ppermute(jnp.stack([keep[cut], got[cut]]), ('tm', 'layer'), pairs)]
    ppermute x4 -> x7, waiting for transfers between devices: 12.8 us -> 8.65 us  [over_circle(): return lax.ppermute(array, ('space', 'layer'), circle)]
    ppermute x4 -> x7, starting transfers between devices: 4.14 us -> 8.23 us  [over_circle(): return lax.ppermute(array, ('space', 'layer'), circle)]
    ppermute x6 -> x3, starting transfers between devices: 7.28 us -> 3.74 us  [exchanged(): lax.ppermute(parts[k], 'tm', [(i, i ^ k) for i in range(count)])]
    unnamed x24 -> x28, local copies, waits for them, and re-layouts: 0.07 us -> 2.09 us
    ppermute x5 -> x10, starting transfers between devices: 4.72 us -> 2.73 us  [over_core(): return lax.ppermute(array, 'layer', swap)]
  transfers between devices with their start and end apart: 15 -> 23, of which waited for: 7 -> 8; matrix products, arithmetic and copies ran while one was open for 7% -> 4% of each run, Pallas kernels for 0% -> 1%
where the time goes in v2:
time: 51.8 us; the launch traced here: 51.5 us
  starting transfers between devices  21 us (41%)
  waiting for transfers between devices  15.9 us (31%)
  Pallas kernels  9.98 us (19%)
  local copies, waits for them, and re-layouts  3.25 us (6%)
  other arithmetic  1.13 us (2%)
    pallas_call x4, Pallas kernels, call(): pl.pallas_call(kernel, out_shape=out_shape, in_specs=[pl.BlockSpec(memory...  9.98 us
    ppermute x7, waiting for transfers between devices, over_circle(): return lax.ppermute(array, ('space', 'layer'), circle)  8.65 us
    ppermute x7, starting transfers between devices, over_circle(): return lax.ppermute(array, ('space', 'layer'), circle)  8.23 us
    ppermute x2, starting transfers between devices, shards(): lax.ppermute(jnp.stack([keep[cut], got[cut]]), ('tm', 'layer'), pairs)  5.03 us
    ppermute x2, waiting for transfers between devices, shards(): lax.ppermute(jnp.stack([keep[cut], got[cut]]), ('tm', 'layer'), pairs)  4.18 us
    ppermute x3, starting transfers between devices, exchanged(): lax.ppermute(parts[k], 'tm', [(i, i ^ k) for i in range(count)])  3.74 us
    ppermute x10, starting transfers between devices, over_core(): return lax.ppermute(array, 'layer', swap)  2.73 us
    unnamed x28, local copies, waits for them, and re-layouts  2.09 us
  transfers between devices with their start and end apart: 23, of which 8 were waited for; matrix products, arithmetic and copies ran while one was open for 4% of the time, Pallas kernels for 1%

profile of v2, /device:TPU:1, one launch (start us, length us, event | category | flops | bytes accessed | tf_op | source)
XLA Modules:
  0.0 51.5 jit_solution(7552202813553962725)
XLA Ops:
  0.0 0.0 copy-start
  0.1 0.1 collective-permute-start
  0.2 0.5 collective-permute-start.1
  0.6 0.1 collective-permute-start.2
  0.7 1.1 %convert_element_type.9 = bf16[4,16,8,128]{3,2,1,0:T(8,128)(2,1)S(1)} convert(f32[4,16,8,128]{3,2,1,0:T(8,128)} %param.14) | non-fusion elementwise | flops 65536 | bytes 393216 | tf_op jit(solution)/shard_map/convert_element_type | solution.py:331
  1.8 0.1 constant_dynamic-slice_fusion.5
  1.8 0.4 collective-permute-start.3
  2.2 1.0 %dynamic-slice_bitcast_fusion = bf16[7,128,128]{2,1,0:T(8,128)(2,1)S(1)} fusion(bf16[8,7,128,128]{3,2,1,0:T(8,128)(2,1)} %refs_2_.3, s32[]{:T(128)S(6)} %select_n.41), kind=kLoop, calls=%fused_computation | loop fusion | bytes 458756 | tf_op jit(solution)/shard_map/jit(dynamic_index_in_dim)/squeeze | solution.py:358
  3.2 2.7 %collective-permute-start.6 = (bf16[7,128,128]{2,1,0:T(8,128)(2,1)S(1)}, bf16[7,128,128]{2,1,0:T(8,128)(2,1)S(1)}, u32[]{:S(2)}, u32[]{:S(2)}) collective-permute-start(bf16[7,128,128]{2,1,0:T(8,128)(2,1)S(1)} %dynamic-slice_bitcast_fusion), channel_id=1, source_target_pairs={{1,2},{2,1},{3,0},{0,3},{5,6},{6,5},{7,4},{4,7},{9,10},{10,9},{11,... | collective-permute-start | bytes 688136 | tf_op jit(solution)/shard_map/ppermute | solution.py:320
  5.9 0.0 collective-permute-done.3
  6.0 1.4 %collective-permute-start.4 = (bf16[4,64,128]{2,1,0:T(8,128)(2,1)S(1)}, bf16[4,64,128]{2,1,0:T(8,128)(2,1)S(1)}, u32[]{:S(2)}, u32[]{:S(2)}) collective-permute-start(bf16[4,64,128]{2,1,0:T(8,128)(2,1)S(1)} %get-tuple-element.22), channel_id=1, source_target_pairs={{0,4},{4,0},{8,12},{12,8},{1,5},{5,1},{9,13},{13,9},{2,6},{6,2},{1... | collective-permute-start | bytes 196616 | tf_op jit(solution)/shard_map/ppermute | solution.py:324
  7.3 0.0 collective-permute-done.start_two
  7.3 2.2 %collective-permute-start.9 = (bf16[4,64,128]{2,1,0:T(8,128)(2,1)S(1)}, bf16[4,64,128]{2,1,0:T(8,128)(2,1)S(1)}, u32[]{:S(2)}, u32[]{:S(2)}) collective-permute-start(bf16[4,64,128]{2,1,0:T(8,128)(2,1)S(1)} %get-tuple-element.19), channel_id=1, source_target_pairs={{0,12},{4,8},{8,4},{12,0},{1,13},{5,9},{9,5},{13,1},{2,14},{6,10},... | collective-permute-start | bytes 196616 | tf_op jit(solution)/shard_map/ppermute | solution.py:324
  9.5 0.0 collective-permute-done.1.reaction_two
  9.5 0.2 collective-permute-start.8
  9.7 0.1 stack.37.where.refs_0_
  9.8 0.0 copy-start.11
  9.8 0.7 %copy-done.11 = f32[8,128]{1,0:T(8,128)S(1)} copy-done((f32[8,128]{1,0:T(8,128)S(1)}, f32[8,128]{1,0:T(8,128)}, u32[]{:S(2)}) %copy-start.11) | copy-done | bytes 4120
  10.5 0.7 %copy-done.13 = s32[8,4]{0,1:T(4,128)S(1)} copy-done((s32[8,4]{0,1:T(4,128)S(1)}, s32[8,4]{0,1:T(4,128)}, u32[]{:S(2)}) %copy-start.13) | copy-done | bytes 152
  11.2 0.7 %shard_map.136 = (f32[48,8,128]{2,1,0:T(8,128)S(1)}, f32[51,2,128]{2,1,0:T(2,128)S(1)}) custom-call(s32[5]{0:T(128)S(1)} %stack.37.where.refs_0_, f32[16,8,128]{2,1,0:T(8,128)S(1)} %copy-done.7, f32[16,8,128]{2,1,0:T(8,128)S(1)} %copy-done.8, f32[16,8,128]{2,1,0:T(8,128)S(1)} %copy-done.9, f32[16,8,128]{2,1,0:T(8,128)S(1)} %collective-permute-done.start_two, ...), custom_call_target="tpu_custom_call" | custom-call | tf_op jit(solution)/shard_map/pallas_call | solution.py:288
  11.9 0.9 %collective-permute-start.5 = (f32[51,2,128]{2,1,0:T(2,128)S(1)}, f32[51,2,128]{2,1,0:T(2,128)S(1)}, u32[]{:S(2)}, u32[]{:S(2)}) collective-permute-start(f32[51,2,128]{2,1,0:T(2,128)S(1)} %get-tuple-element.12), channel_id=1, source_target_pairs={{1,2},{2,1},{3,0},{0,3},{5,6},{6,5},{7,4},{4,7},{9,10},{10,9},{11,... | collective-permute-start | bytes 156680 | tf_op jit(solution)/shard_map/ppermute | solution.py:320
  12.8 0.9 %collective-permute-start.14 = (bf16[4,64,128]{2,1,0:T(8,128)(2,1)S(1)}, bf16[4,64,128]{2,1,0:T(8,128)(2,1)S(1)}, u32[]{:S(2)}, u32[]{:S(2)}) collective-permute-start(bf16[4,64,128]{2,1,0:T(8,128)(2,1)S(1)} %get-tuple-element.21.refs_10_), channel_id=1, source_target_pairs={{1,2},{2,1},{3,0},{0,3},{5,6},{6,5},{7,4},{4,7},{9,10},{10,9},{11,... | collective-permute-start | bytes 196616 | tf_op jit(solution)/shard_map/ppermute | solution.py:320
  13.7 0.7 %collective-permute-start.10 = (bf16[4,64,128]{2,1,0:T(8,128)(2,1)S(1)}, bf16[4,64,128]{2,1,0:T(8,128)(2,1)S(1)}, u32[]{:S(2)}, u32[]{:S(2)}) collective-permute-start(bf16[4,64,128]{2,1,0:T(8,128)(2,1)S(1)} %get-tuple-element.21.refs_10_), channel_id=1, source_target_pairs={{0,1},{1,0},{2,3},{3,2},{4,5},{5,4},{6,7},{7,6},{8,9},{9,8},{10,11... | collective-permute-start | bytes 196616 | tf_op jit(solution)/shard_map/ppermute | solution.py:317
  14.4 2.1 %collective-permute-done.8.refs_12_ = bf16[4,64,128]{2,1,0:T(8,128)(2,1)S(1)} collective-permute-done((bf16[4,64,128]{2,1,0:T(8,128)(2,1)S(1)}, bf16[4,64,128]{2,1,0:T(8,128)(2,1)S(1)}, u32[]{:S(2)}, u32[]{:S(2)}) %collective-permute-start.8) | collective-permute-done | bytes 65568 | tf_op jit(solution)/shard_map/ppermute | solution.py:324
  16.5 0.5 %collective-permute-start.17 = (bf16[4,64,128]{2,1,0:T(8,128)(2,1)S(1)}, bf16[4,64,128]{2,1,0:T(8,128)(2,1)S(1)}, u32[]{:S(2)}, u32[]{:S(2)}) collective-permute-start(bf16[4,64,128]{2,1,0:T(8,128)(2,1)S(1)} %collective-permute-done.9.refs_13_), channel_id=1, source_target_pairs={{1,2},{2,1},{3,0},{0,3},{5,6},{6,5},{7,4},{4,7},{9,10},{10,9},{11,... | collective-permute-start | bytes 196616 | tf_op jit(solution)/shard_map/ppermute | solution.py:320
  17.0 0.1 collective-permute-start.13
  17.1 1.2 %collective-permute-start.7 = (bf16[7,128,128]{2,1,0:T(8,128)(2,1)S(1)}, bf16[7,128,128]{2,1,0:T(8,128)(2,1)S(1)}, u32[]{:S(2)}, u32[]{:S(2)}) collective-permute-start(bf16[7,128,128]{2,1,0:T(8,128)(2,1)S(1)} %collective-permute-done.6.refs_3_), channel_id=1, source_target_pairs={{0,16},{16,0},{1,17},{17,1},{2,18},{18,2},{3,19},{19,3},{4,20},{20... | collective-permute-start | bytes 688136 | tf_op jit(solution)/shard_map/ppermute | solution.py:360
  18.4 1.8 %collective-permute-start.16 = (bf16[4,64,128]{2,1,0:T(8,128)(2,1)S(1)}, bf16[4,64,128]{2,1,0:T(8,128)(2,1)S(1)}, u32[]{:S(2)}, u32[]{:S(2)}) collective-permute-start(bf16[4,64,128]{2,1,0:T(8,128)(2,1)S(1)} %collective-permute-done.8.refs_12_), channel_id=1, source_target_pairs={{1,2},{2,1},{3,0},{0,3},{5,6},{6,5},{7,4},{4,7},{9,10},{10,9},{11,... | collective-permute-start | bytes 196616 | tf_op jit(solution)/shard_map/ppermute | solution.py:320
  20.2 0.7 %collective-permute-done.17.refs_21_ = bf16[4,64,128]{2,1,0:T(8,128)(2,1)S(1)} collective-permute-done((bf16[4,64,128]{2,1,0:T(8,128)(2,1)S(1)}, bf16[4,64,128]{2,1,0:T(8,128)(2,1)S(1)}, u32[]{:S(2)}, u32[]{:S(2)}) %collective-permute-start.17) | collective-permute-done | bytes 65568 | tf_op jit(solution)/shard_map/ppermute | solution.py:320
  20.9 0.2 collective-permute-start.15
  21.1 0.1 collective-permute-start.11
  21.3 1.8 %collective-permute-done.16.refs_20_ = bf16[4,64,128]{2,1,0:T(8,128)(2,1)S(1)} collective-permute-done((bf16[4,64,128]{2,1,0:T(8,128)(2,1)S(1)}, bf16[4,64,128]{2,1,0:T(8,128)(2,1)S(1)}, u32[]{:S(2)}, u32[]{:S(2)}) %collective-permute-start.16) | collective-permute-done | bytes 65568 | tf_op jit(solution)/shard_map/ppermute | solution.py:320
  23.1 1.7 %collective-permute-done.15.refs_19_ = bf16[4,64,128]{2,1,0:T(8,128)(2,1)S(1)} collective-permute-done((bf16[4,64,128]{2,1,0:T(8,128)(2,1)S(1)}, bf16[4,64,128]{2,1,0:T(8,128)(2,1)S(1)}, u32[]{:S(2)}, u32[]{:S(2)}) %collective-permute-start.15) | collective-permute-done | bytes 65568 | tf_op jit(solution)/shard_map/ppermute | solution.py:320
  24.8 0.0 copy-start.12
  24.8 0.7 %copy-done.12 = f32[8,128]{1,0:T(8,128)S(1)} copy-done((f32[8,128]{1,0:T(8,128)S(1)}, f32[8,128]{1,0:T(8,128)}, u32[]{:S(2)}) %copy-start.12) | copy-done | bytes 4120
  25.5 4.2 %shard_map.137 = (bf16[4,12,16,128]{3,2,1,0:T(8,128)(2,1)S(1)}, bf16[36,16,128]{2,1,0:T(8,128)(2,1)S(1)}, f32[3,16,8,128]{3,2,1,0:T(8,128)S(1)}, f32[8,128]{1,0:T(8,128)S(1)}, bf16[2,7,128,128]{3,2,1,0:T(8,128)(2,1)S(1)}) custom-call(s32[9,8]{1,0:T(8,128)S(1)} %fusion.refs_0_, bf16[256,256]{1,0:T(8,128)(2,1)S(1)} %copy-done.2, ...), custom_call_target="tpu_custom_call" | custom-call | tf_op jit(solution)/shard_map/pallas_call | solution.py:288
  29.8 0.4 collective-permute-start.18
  30.2 1.2 %collective-permute-start.19 = (bf16[36,16,128]{2,1,0:T(8,128)(2,1)S(1)}, bf16[36,16,128]{2,1,0:T(8,128)(2,1)S(1)}, u32[]{:S(2)}, u32[]{:S(2)}) collective-permute-start(bf16[36,16,128]{2,1,0:T(8,128)(2,1)S(1)} %get-tuple-element.18), channel_id=1, source_target_pairs={{1,2},{2,1},{3,0},{0,3},{5,6},{6,5},{7,4},{4,7},{9,10},{10,9},{11,... | collective-permute-start | bytes 442376 | tf_op jit(solution)/shard_map/ppermute | solution.py:320
  31.4 4.4 %collective-permute-done.19.refs_10_ = bf16[36,16,128]{2,1,0:T(8,128)(2,1)S(1)} collective-permute-done((bf16[36,16,128]{2,1,0:T(8,128)(2,1)S(1)}, bf16[36,16,128]{2,1,0:T(8,128)(2,1)S(1)}, u32[]{:S(2)}, u32[]{:S(2)}) %collective-permute-start.19) | collective-permute-done | bytes 147488 | tf_op jit(solution)/shard_map/ppermute | solution.py:320
  35.8 0.0 copy-start.1
  35.8 3.6 %shard_map.138 = bf16[2,8,32,128]{3,2,1,0:T(8,128)(2,1)S(1)} custom-call(s32[9,8]{1,0:T(8,128)S(1)} %fusion.refs_0_, bf16[256,256]{1,0:T(8,128)(2,1)S(1)} %copy-done.3, bf16[8,7,128,128]{3,2,1,0:T(8,128)(2,1)S(1)} %copy-done, bf16[2,7,128,128]{3,2,1,0:T(8,128)(2,1)S(1)} %get-tuple-element.14.refs_3_, f32[3,16,8,128]{3,2,1,0:T(8,128)S(1)} %get-tuple-element.15.refs_4_, ...), custom_call_target="tpu_custom_call" | custom-call | tf_op jit(solution)/shard_map/pallas_call | solution.py:288
  39.5 0.3 collective-permute-start.20
  39.7 1.0 %collective-permute-done.20 = bf16[8,32,128]{2,1,0:T(8,128)(2,1)S(1)} collective-permute-done((bf16[8,32,128]{2,1,0:T(8,128)(2,1)S(1)}, bf16[8,32,128]{2,1,0:T(8,128)(2,1)S(1)}, u32[]{:S(2)}, u32[]{:S(2)}) %collective-permute-start.20) | collective-permute-done | bytes 65568 | tf_op jit(solution)/shard_map/ppermute | solution.py:317
  40.8 3.7 %collective-permute-start.21 = (bf16[2,4,32,128]{3,2,1,0:T(8,128)(2,1)S(1)}, bf16[2,4,32,128]{3,2,1,0:T(8,128)(2,1)S(1)}, u32[]{:S(2)}, u32[]{:S(2)}) collective-permute-start(bf16[2,4,32,128]{3,2,1,0:T(8,128)(2,1)S(1)} %pad_maximum_fusion.1), channel_id=1, source_target_pairs={{0,0},{1,8},{4,4},{5,12},{8,1},{9,9},{12,5},{13,13},{2,2},{3,10},{... | collective-permute-start | bytes 196616 | tf_op jit(solution)/shard_map/ppermute | solution.py:446
  44.5 1.4 %collective-permute-start.22 = (bf16[2,4,32,128]{3,2,1,0:T(8,128)(2,1)S(1)}, bf16[2,4,32,128]{3,2,1,0:T(8,128)(2,1)S(1)}, u32[]{:S(2)}, u32[]{:S(2)}) collective-permute-start(bf16[2,4,32,128]{3,2,1,0:T(8,128)(2,1)S(1)} %pad_maximum_fusion.2), channel_id=1, source_target_pairs={{0,4},{1,12},{4,0},{5,8},{8,5},{9,13},{12,1},{13,9},{2,6},{3,14},{... | collective-permute-start | bytes 196616 | tf_op jit(solution)/shard_map/ppermute | solution.py:446
  45.8 2.1 %collective-permute-done.21.refs_2_ = bf16[2,4,32,128]{3,2,1,0:T(8,128)(2,1)S(1)} collective-permute-done((bf16[2,4,32,128]{3,2,1,0:T(8,128)(2,1)S(1)}, bf16[2,4,32,128]{3,2,1,0:T(8,128)(2,1)S(1)}, u32[]{:S(2)}, u32[]{:S(2)}) %collective-permute-start.21) | collective-permute-done | bytes 65568 | tf_op jit(solution)/shard_map/ppermute | solution.py:446
  48.0 2.1 %collective-permute-done.22.refs_3_ = bf16[2,4,32,128]{3,2,1,0:T(8,128)(2,1)S(1)} collective-permute-done((bf16[2,4,32,128]{3,2,1,0:T(8,128)(2,1)S(1)}, bf16[2,4,32,128]{3,2,1,0:T(8,128)(2,1)S(1)}, u32[]{:S(2)}, u32[]{:S(2)}) %collective-permute-start.22) | collective-permute-done | bytes 65568 | tf_op jit(solution)/shard_map/ppermute | solution.py:446
  50.0 1.5 %shard_map.139 = f32[4,16,8,128]{3,2,1,0:T(8,128)} custom-call(s32[5]{0:T(128)S(1)} %stack.37.where.refs_0_, bf16[256,256]{1,0:T(8,128)(2,1)S(1)} %copy-done.1, bf16[2,4,32,128]{3,2,1,0:T(8,128)(2,1)S(1)} %collective-permute-done.21.refs_2_, bf16[2,4,32,128]{3,2,1,0:T(8,128)(2,1)S(1)} %collective-permute-done.22.refs_3_), custom_call_target="tpu_custom_call" | custom-call | tf_op jit(solution)/shard_map/pallas_call | solution.py:288
  (45 shorter events, 0.2 us)
Async XLA Ops:
  0.0 24.8 %copy-start.5 = (bf16[192,192]{1,0:T(8,128)(2,1)S(1)}, bf16[192,192]{1,0:T(8,128)(2,1)}, u32[]{:S(2)}) copy-start(bf16[192,192]{1,0:T(8,128)(2,1)} %constant.63.clone.refs_9_) | copy-start | bytes 221188
  0.0 24.8 %copy-start.4 = (bf16[224,224]{1,0:T(8,128)(2,1)S(1)}, bf16[224,224]{1,0:T(8,128)(2,1)}, u32[]{:S(2)}) copy-start(bf16[224,224]{1,0:T(8,128)(2,1)} %constant.62.clone.refs_8_) | copy-start | bytes 301060
  0.0 24.8 %copy-start.2 = (bf16[256,256]{1,0:T(8,128)(2,1)S(1)}, bf16[256,256]{1,0:T(8,128)(2,1)}, u32[]{:S(2)}) copy-start(bf16[256,256]{1,0:T(8,128)(2,1)} %constant.61.clone.refs_1_) | copy-start | bytes 393220
  0.0 9.8 %copy-start.7 = (f32[16,8,128]{2,1,0:T(8,128)S(1)}, f32[16,8,128]{2,1,0:T(8,128)}, u32[]{:S(2)}) copy-start(f32[16,8,128]{2,1,0:T(8,128)} %start.1) | copy-start | bytes 196612
  0.0 9.8 %copy-start.8 = (f32[16,8,128]{2,1,0:T(8,128)S(1)}, f32[16,8,128]{2,1,0:T(8,128)}, u32[]{:S(2)}) copy-start(f32[16,8,128]{2,1,0:T(8,128)} %reaction.1) | copy-start | bytes 196612
  0.0 9.8 %copy-start.9 = (f32[16,8,128]{2,1,0:T(8,128)S(1)}, f32[16,8,128]{2,1,0:T(8,128)}, u32[]{:S(2)}) copy-start(f32[16,8,128]{2,1,0:T(8,128)} %source.1) | copy-start | bytes 196612
  0.0 24.8 %copy-start = (bf16[8,7,128,128]{3,2,1,0:T(8,128)(2,1)S(1)}, bf16[8,7,128,128]{3,2,1,0:T(8,128)(2,1)}, u32[]{:S(2)}) copy-start(bf16[8,7,128,128]{3,2,1,0:T(8,128)(2,1)} %refs_2_.3) | copy-start | bytes 5505028
  0.1 7.3 %collective-permute-start = (f32[16,8,128]{2,1,0:T(8,128)}, f32[16,8,128]{2,1,0:T(8,128)S(1)}, u32[]{:S(2)}, u32[]{:S(2)}) collective-permute-start(f32[16,8,128]{2,1,0:T(8,128)} %start.1), channel_id=1, source_target_pairs={{0,1},{1,0},{2,3},{3,2},{4,5},{5,4},{6,7},{7,6},{8,9},{9,8},{10,11... | collective-permute-start | bytes 196616 | tf_op jit(solution)/shard_map/ppermute | solution.py:317
  0.2 9.4 %collective-permute-start.1 = (f32[16,8,128]{2,1,0:T(8,128)}, f32[16,8,128]{2,1,0:T(8,128)S(1)}, u32[]{:S(2)}, u32[]{:S(2)}) collective-permute-start(f32[16,8,128]{2,1,0:T(8,128)} %reaction.1), channel_id=1, source_target_pairs={{0,1},{1,0},{2,3},{3,2},{4,5},{5,4},{6,7},{7,6},{8,9},{9,8},{10,11... | collective-permute-start | bytes 196616 | tf_op jit(solution)/shard_map/ppermute | solution.py:317
  0.6 9.2 %collective-permute-start.2 = (f32[16,8,128]{2,1,0:T(8,128)}, f32[16,8,128]{2,1,0:T(8,128)S(1)}, u32[]{:S(2)}, u32[]{:S(2)}) collective-permute-start(f32[16,8,128]{2,1,0:T(8,128)} %source.1), channel_id=1, source_target_pairs={{0,1},{1,0},{2,3},{3,2},{4,5},{5,4},{6,7},{7,6},{8,9},{9,8},{10,11... | collective-permute-start | bytes 196616 | tf_op jit(solution)/shard_map/ppermute | solution.py:317
  1.8 4.0 %collective-permute-start.3 = (bf16[4,64,128]{2,1,0:T(8,128)(2,1)S(1)}, bf16[4,64,128]{2,1,0:T(8,128)(2,1)S(1)}, u32[]{:S(2)}, u32[]{:S(2)}) collective-permute-start(bf16[4,64,128]{2,1,0:T(8,128)(2,1)S(1)} %bitcast.28), channel_id=1, source_target_pairs={{0,1},{1,0},{2,3},{3,2},{4,5},{5,4},{6,7},{7,6},{8,9},{9,8},{10,11... | collective-permute-start | bytes 196616 | tf_op jit(solution)/shard_map/ppermute | solution.py:317
  3.2 13.9 %collective-permute-start.6 = (bf16[7,128,128]{2,1,0:T(8,128)(2,1)S(1)}, bf16[7,128,128]{2,1,0:T(8,128)(2,1)S(1)}, u32[]{:S(2)}, u32[]{:S(2)}) collective-permute-start(bf16[7,128,128]{2,1,0:T(8,128)(2,1)S(1)} %dynamic-slice_bitcast_fusion), channel_id=1, source_target_pairs={{1,2},{2,1},{3,0},{0,3},{5,6},{6,5},{7,4},{4,7},{9,10},{10,9},{11,... | collective-permute-start | bytes 688136 | tf_op jit(solution)/shard_map/ppermute | solution.py:320
  6.0 3.8 %collective-permute-start.4 = (bf16[4,64,128]{2,1,0:T(8,128)(2,1)S(1)}, bf16[4,64,128]{2,1,0:T(8,128)(2,1)S(1)}, u32[]{:S(2)}, u32[]{:S(2)}) collective-permute-start(bf16[4,64,128]{2,1,0:T(8,128)(2,1)S(1)} %get-tuple-element.22), channel_id=1, source_target_pairs={{0,4},{4,0},{8,12},{12,8},{1,5},{5,1},{9,13},{13,9},{2,6},{6,2},{1... | collective-permute-start | bytes 196616 | tf_op jit(solution)/shard_map/ppermute | solution.py:324
  7.3 6.4 %collective-permute-start.9 = (bf16[4,64,128]{2,1,0:T(8,128)(2,1)S(1)}, bf16[4,64,128]{2,1,0:T(8,128)(2,1)S(1)}, u32[]{:S(2)}, u32[]{:S(2)}) collective-permute-start(bf16[4,64,128]{2,1,0:T(8,128)(2,1)S(1)} %get-tuple-element.19), channel_id=1, source_target_pairs={{0,12},{4,8},{8,4},{12,0},{1,13},{5,9},{9,5},{13,1},{2,14},{6,10},... | collective-permute-start | bytes 196616 | tf_op jit(solution)/shard_map/ppermute | solution.py:324
  9.5 7.0 %collective-permute-start.8 = (bf16[4,64,128]{2,1,0:T(8,128)(2,1)S(1)}, bf16[4,64,128]{2,1,0:T(8,128)(2,1)S(1)}, u32[]{:S(2)}, u32[]{:S(2)}) collective-permute-start(bf16[4,64,128]{2,1,0:T(8,128)(2,1)S(1)} %get-tuple-element.20), channel_id=1, source_target_pairs={{0,8},{4,12},{8,0},{12,4},{1,9},{5,13},{9,1},{13,5},{2,10},{6,14},... | collective-permute-start | bytes 196616 | tf_op jit(solution)/shard_map/ppermute | solution.py:324
  9.8 0.7 %copy-start.11 = (f32[8,128]{1,0:T(8,128)S(1)}, f32[8,128]{1,0:T(8,128)}, u32[]{:S(2)}) copy-start(f32[8,128]{1,0:T(8,128)} %refs_7_.2) | copy-start | bytes 12292
  10.5 0.7 %copy-start.13 = (s32[8,4]{0,1:T(4,128)S(1)}, s32[8,4]{0,1:T(4,128)}, u32[]{:S(2)}) copy-start(s32[8,4]{0,1:T(4,128)} %param.20) | copy-start | bytes 388
  11.9 5.2 %collective-permute-start.5 = (f32[51,2,128]{2,1,0:T(2,128)S(1)}, f32[51,2,128]{2,1,0:T(2,128)S(1)}, u32[]{:S(2)}, u32[]{:S(2)}) collective-permute-start(f32[51,2,128]{2,1,0:T(2,128)S(1)} %get-tuple-element.12), channel_id=1, source_target_pairs={{1,2},{2,1},{3,0},{0,3},{5,6},{6,5},{7,4},{4,7},{9,10},{10,9},{11,... | collective-permute-start | bytes 156680 | tf_op jit(solution)/shard_map/ppermute | solution.py:320
  12.8 5.6 %collective-permute-start.14 = (bf16[4,64,128]{2,1,0:T(8,128)(2,1)S(1)}, bf16[4,64,128]{2,1,0:T(8,128)(2,1)S(1)}, u32[]{:S(2)}, u32[]{:S(2)}) collective-permute-start(bf16[4,64,128]{2,1,0:T(8,128)(2,1)S(1)} %get-tuple-element.21.refs_10_), channel_id=1, source_target_pairs={{1,2},{2,1},{3,0},{0,3},{5,6},{6,5},{7,4},{4,7},{9,10},{10,9},{11,... | collective-permute-start | bytes 196616 | tf_op jit(solution)/shard_map/ppermute | solution.py:320
  13.7 6.5 %collective-permute-start.10 = (bf16[4,64,128]{2,1,0:T(8,128)(2,1)S(1)}, bf16[4,64,128]{2,1,0:T(8,128)(2,1)S(1)}, u32[]{:S(2)}, u32[]{:S(2)}) collective-permute-start(bf16[4,64,128]{2,1,0:T(8,128)(2,1)S(1)} %get-tuple-element.21.refs_10_), channel_id=1, source_target_pairs={{0,1},{1,0},{2,3},{3,2},{4,5},{5,4},{6,7},{7,6},{8,9},{9,8},{10,11... | collective-permute-start | bytes 196616 | tf_op jit(solution)/shard_map/ppermute | solution.py:317
  16.5 4.4 %collective-permute-start.17 = (bf16[4,64,128]{2,1,0:T(8,128)(2,1)S(1)}, bf16[4,64,128]{2,1,0:T(8,128)(2,1)S(1)}, u32[]{:S(2)}, u32[]{:S(2)}) collective-permute-start(bf16[4,64,128]{2,1,0:T(8,128)(2,1)S(1)} %collective-permute-done.9.refs_13_), channel_id=1, source_target_pairs={{1,2},{2,1},{3,0},{0,3},{5,6},{6,5},{7,4},{4,7},{9,10},{10,9},{11,... | collective-permute-start | bytes 196616 | tf_op jit(solution)/shard_map/ppermute | solution.py:320
  17.0 4.1 %collective-permute-start.13 = (bf16[4,64,128]{2,1,0:T(8,128)(2,1)S(1)}, bf16[4,64,128]{2,1,0:T(8,128)(2,1)S(1)}, u32[]{:S(2)}, u32[]{:S(2)}) collective-permute-start(bf16[4,64,128]{2,1,0:T(8,128)(2,1)S(1)} %collective-permute-done.9.refs_13_), channel_id=1, source_target_pairs={{0,1},{1,0},{2,3},{3,2},{4,5},{5,4},{6,7},{7,6},{8,9},{9,8},{10,11... | collective-permute-start | bytes 196616 | tf_op jit(solution)/shard_map/ppermute | solution.py:317
  17.1 7.6 %collective-permute-start.7 = (bf16[7,128,128]{2,1,0:T(8,128)(2,1)S(1)}, bf16[7,128,128]{2,1,0:T(8,128)(2,1)S(1)}, u32[]{:S(2)}, u32[]{:S(2)}) collective-permute-start(bf16[7,128,128]{2,1,0:T(8,128)(2,1)S(1)} %collective-permute-done.6.refs_3_), channel_id=1, source_target_pairs={{0,16},{16,0},{1,17},{17,1},{2,18},{18,2},{3,19},{19,3},{4,20},{20... | collective-permute-start | bytes 688136 | tf_op jit(solution)/shard_map/ppermute | solution.py:360
  18.4 4.7 %collective-permute-start.16 = (bf16[4,64,128]{2,1,0:T(8,128)(2,1)S(1)}, bf16[4,64,128]{2,1,0:T(8,128)(2,1)S(1)}, u32[]{:S(2)}, u32[]{:S(2)}) collective-permute-start(bf16[4,64,128]{2,1,0:T(8,128)(2,1)S(1)} %collective-permute-done.8.refs_12_), channel_id=1, source_target_pairs={{1,2},{2,1},{3,0},{0,3},{5,6},{6,5},{7,4},{4,7},{9,10},{10,9},{11,... | collective-permute-start | bytes 196616 | tf_op jit(solution)/shard_map/ppermute | solution.py:320
  20.2 2.9 %collective-permute-start.12 = (bf16[4,64,128]{2,1,0:T(8,128)(2,1)S(1)}, bf16[4,64,128]{2,1,0:T(8,128)(2,1)S(1)}, u32[]{:S(2)}, u32[]{:S(2)}) collective-permute-start(bf16[4,64,128]{2,1,0:T(8,128)(2,1)S(1)} %collective-permute-done.8.refs_12_), channel_id=1, source_target_pairs={{0,1},{1,0},{2,3},{3,2},{4,5},{5,4},{6,7},{7,6},{8,9},{9,8},{10,11... | collective-permute-start | bytes 196616 | tf_op jit(solution)/shard_map/ppermute | solution.py:317
  20.9 3.9 %collective-permute-start.15 = (bf16[4,64,128]{2,1,0:T(8,128)(2,1)S(1)}, bf16[4,64,128]{2,1,0:T(8,128)(2,1)S(1)}, u32[]{:S(2)}, u32[]{:S(2)}) collective-permute-start(bf16[4,64,128]{2,1,0:T(8,128)(2,1)S(1)} %collective-permute-done.4._.refs_11_), channel_id=1, source_target_pairs={{1,2},{2,1},{3,0},{0,3},{5,6},{6,5},{7,4},{4,7},{9,10},{10,9},{11,... | collective-permute-start | bytes 196616 | tf_op jit(solution)/shard_map/ppermute | solution.py:320
  21.1 3.6 %collective-permute-start.11 = (bf16[4,64,128]{2,1,0:T(8,128)(2,1)S(1)}, bf16[4,64,128]{2,1,0:T(8,128)(2,1)S(1)}, u32[]{:S(2)}, u32[]{:S(2)}) collective-permute-start(bf16[4,64,128]{2,1,0:T(8,128)(2,1)S(1)} %collective-permute-done.4._.refs_11_), channel_id=1, source_target_pairs={{0,1},{1,0},{2,3},{3,2},{4,5},{5,4},{6,7},{7,6},{8,9},{9,8},{10,11... | collective-permute-start | bytes 196616 | tf_op jit(solution)/shard_map/ppermute | solution.py:317
  24.8 0.7 %copy-start.12 = (f32[8,128]{1,0:T(8,128)S(1)}, f32[8,128]{1,0:T(8,128)}, u32[]{:S(2)}) copy-start(f32[8,128]{1,0:T(8,128)} %refs_7_.2) | copy-start | bytes 12292
  25.5 10.3 %copy-start.3 = (bf16[256,256]{1,0:T(8,128)(2,1)S(1)}, bf16[256,256]{1,0:T(8,128)(2,1)}, u32[]{:S(2)}) copy-start(bf16[256,256]{1,0:T(8,128)(2,1)} %constant.64.clone.refs_1_) | copy-start | bytes 393220
  25.5 10.3 %copy-start.6 = (bf16[160,160]{1,0:T(8,128)(2,1)S(1)}, bf16[160,160]{1,0:T(8,128)(2,1)}, u32[]{:S(2)}) copy-start(bf16[160,160]{1,0:T(8,128)(2,1)} %constant.65.clone.refs_6_) | copy-start | bytes 153604
  25.5 10.3 %copy-start.10 = (bf16[128,128]{1,0:T(8,128)(2,1)S(1)}, bf16[128,128]{1,0:T(8,128)(2,1)}, u32[]{:S(2)}) copy-start(bf16[128,128]{1,0:T(8,128)(2,1)} %constant.66.clone.refs_7_) | copy-start | bytes 98308
  29.8 6.1 %collective-permute-start.18 = (bf16[4,12,16,128]{3,2,1,0:T(8,128)(2,1)S(1)}, bf16[4,12,16,128]{3,2,1,0:T(8,128)(2,1)S(1)}, u32[]{:S(2)}, u32[]{:S(2)}) collective-permute-start(bf16[4,12,16,128]{3,2,1,0:T(8,128)(2,1)S(1)} %get-tuple-element.17.refs_8_), channel_id=1, source_target_pairs={{0,1},{1,0},{2,3},{3,2},{4,5},{5,4},{6,7},{7,6},{8,9},{9,8},{10,11... | collective-permute-start | bytes 589832 | tf_op jit(solution)/shard_map/ppermute | solution.py:317
  30.2 5.6 %collective-permute-start.19 = (bf16[36,16,128]{2,1,0:T(8,128)(2,1)S(1)}, bf16[36,16,128]{2,1,0:T(8,128)(2,1)S(1)}, u32[]{:S(2)}, u32[]{:S(2)}) collective-permute-start(bf16[36,16,128]{2,1,0:T(8,128)(2,1)S(1)} %get-tuple-element.18), channel_id=1, source_target_pairs={{1,2},{2,1},{3,0},{0,3},{5,6},{6,5},{7,4},{4,7},{9,10},{10,9},{11,... | collective-permute-start | bytes 442376 | tf_op jit(solution)/shard_map/ppermute | solution.py:320
  35.8 14.2 %copy-start.1 = (bf16[256,256]{1,0:T(8,128)(2,1)S(1)}, bf16[256,256]{1,0:T(8,128)(2,1)}, u32[]{:S(2)}) copy-start(bf16[256,256]{1,0:T(8,128)(2,1)} %constant.67.clone.refs_1_) | copy-start | bytes 393220
  39.5 1.3 %collective-permute-start.20 = (bf16[8,32,128]{2,1,0:T(8,128)(2,1)S(1)}, bf16[8,32,128]{2,1,0:T(8,128)(2,1)S(1)}, u32[]{:S(2)}, u32[]{:S(2)}) collective-permute-start(bf16[8,32,128]{2,1,0:T(8,128)(2,1)S(1)} %slice_bitcast_fusion), channel_id=1, source_target_pairs={{0,1},{1,0},{2,3},{3,2},{4,5},{5,4},{6,7},{7,6},{8,9},{9,8},{10,11... | collective-permute-start | bytes 196616 | tf_op jit(solution)/shard_map/ppermute | solution.py:317
  40.8 7.2 %collective-permute-start.21 = (bf16[2,4,32,128]{3,2,1,0:T(8,128)(2,1)S(1)}, bf16[2,4,32,128]{3,2,1,0:T(8,128)(2,1)S(1)}, u32[]{:S(2)}, u32[]{:S(2)}) collective-permute-start(bf16[2,4,32,128]{3,2,1,0:T(8,128)(2,1)S(1)} %pad_maximum_fusion.1), channel_id=1, source_target_pairs={{0,0},{1,8},{4,4},{5,12},{8,1},{9,9},{12,5},{13,13},{2,2},{3,10},{... | collective-permute-start | bytes 196616 | tf_op jit(solution)/shard_map/ppermute | solution.py:446
  44.5 5.6 %collective-permute-start.22 = (bf16[2,4,32,128]{3,2,1,0:T(8,128)(2,1)S(1)}, bf16[2,4,32,128]{3,2,1,0:T(8,128)(2,1)S(1)}, u32[]{:S(2)}, u32[]{:S(2)}) collective-permute-start(bf16[2,4,32,128]{3,2,1,0:T(8,128)(2,1)S(1)} %pad_maximum_fusion.2), channel_id=1, source_target_pairs={{0,4},{1,12},{4,0},{5,8},{8,5},{9,13},{12,1},{13,9},{2,6},{3,14},{... | collective-permute-start | bytes 196616 | tf_op jit(solution)/shard_map/ppermute | solution.py:446

commit v3 on v2

v3 whole, which is shorter than its diff:
```python
import math

import jax
import jax.numpy as jnp
import numpy as np
from jax import lax
from jax.experimental import pallas as pl
from jax.experimental.pallas import tpu as pltpu
from jax.sharding import PartitionSpec as P

NEWTON = 2
APPLICATIONS = 2 * NEWTON
OFFSETS = (-2, -1, 1, 2)
GROUP = 4

corner_weight = 0.25


def transform_tables(steps):
    beta = corner_weight ** (1.0 / steps)
    half = steps // 2
    counter = np.arange(steps)
    angle = ((counter[:, None] * counter[None, :]) % steps) * (2.0 * math.pi / steps)
    rising = np.power(beta, counter)
    falling = np.power(beta, -counter.astype(np.float64)) / steps
    fwd_re = np.cos(angle) * rising[None, :]
    fwd_im = -np.sin(angle) * rising[None, :]
    back_re = np.cos(angle) * falling[:, None]
    back_im = -np.sin(angle) * falling[:, None]
    forward = np.concatenate([fwd_re[:half], fwd_re[half : half + 1], fwd_im[1:half]], 0)
    twice = np.where(np.arange(half) == 0, 1.0, 2.0)
    backward = np.concatenate(
        [
            back_re[:, :half] * twice,
            back_re[:, half : half + 1],
            back_im[:, 1:half] * 2.0,
        ],
        1,
    )
    phase = counter * (2.0 * math.pi / steps)
    eigen_re = 1.0 - beta * np.cos(phase)
    eigen_im = beta * np.sin(phase)
    low_re = eigen_re[:half]
    low_im = np.where(np.arange(half) == 0, 0.0, eigen_im[:half])
    high_re = np.concatenate([eigen_re[half : half + 1], eigen_re[1:half]])
    eigen = np.stack([low_re, low_im, high_re]).astype(np.float32)
    return forward, backward, eigen


def applied(array, at, low, count, across, along):
    steps, width = array.shape[2:]

    def rows(element, first):
        return array[element, first : first + count].reshape(count * steps, width)

    parts = [rows(at + offset, low) for offset in range(-2, 4)]
    level = jnp.dot(
        jnp.concatenate(parts, axis=1), across[...], preferred_element_type=jnp.float32
    )
    outs = []
    for k in range(2):
        both = jnp.concatenate([rows(at + k, low - 1), rows(at + k, low + 1)], axis=1)
        out = jnp.dot(both, along[k][...], preferred_element_type=jnp.float32)
        out = out + level[:, k * width : (k + 1) * width]
        outs.append(out.reshape(count, steps, width))
    return outs


def halves(inverse, element, rows, array):
    first, cross, last = (inverse[element, k, rows] for k in range(3))
    half = array.shape[1] // 2
    part_a, part_b = array[:, :half], array[:, half:]
    return jnp.concatenate(
        [first * part_a - cross * part_b, cross * part_a + last * part_b], axis=1
    )


def newton(values, across, along, coef, diag, inverse, forward, backward, packed, spec, window_at,
           write):
    layers, steps, width = values.shape[1:]
    wide, inner = layers - 2, layers - 4
    for pair in range(4):
        mid = pair in (1, 2)
        low, count = (1, wide) if mid else (2, inner)
        rows = slice(window_at + low, window_at + low + count)
        images = applied(
            values, 2 * pair + 2, low, count, across[pair], (along[2 * pair], along[2 * pair + 1])
        )
        rhs = []
        for k, image in enumerate(images):
            element = 2 * pair + k
            state = values[element + 2, low : low + count].astype(jnp.float32)
            start = coef[0, rows, element : element + 1, :]
            reaction = coef[1, rows, element : element + 1, :]
            source = coef[2, rows, element : element + 1, :]
            own = diag[element : element + 1, :][None]
            time = lax.broadcasted_iota(jnp.int32, (count, steps, width), 1)
            previous = jnp.where(time == 0, start, pltpu.roll(state, 1, 1))
            residual = (
                state - previous + own * state + image + reaction * state * state * state - source
            )
            rhs.append((-residual).astype(jnp.bfloat16).reshape(count * steps, width))
        cut = count * steps
        out = jnp.dot(
            forward[:cut, :cut], jnp.concatenate(rhs, axis=1), preferred_element_type=jnp.float32
        )
        out = out.astype(jnp.bfloat16).astype(jnp.float32)
        rows = slice(window_at + low - 1, window_at + low - 1 + count)
        for k in range(2):
            element = 2 * pair + k
            part = out[:, k * width : (k + 1) * width].reshape(count, steps, width)
            sol = halves(inverse, element, rows, part)
            packed[element, low - 1 : low - 1 + count] = sol.astype(jnp.bfloat16)
            if mid:
                spec[element - 2] = part
    rows = slice(window_at + 1, window_at + 1 + inner)
    for pair in (1, 2):
        images = applied(
            packed, 2 * pair, 1, inner, across[pair], (along[2 * pair], along[2 * pair + 1])
        )
        finals = []
        for k, image in enumerate(images):
            element = 2 * pair + k
            final = halves(inverse, element, rows, spec[element - 2, 1 : 1 + inner] - image)
            finals.append(final.astype(jnp.bfloat16).reshape(inner * steps, width))
        delta = jnp.dot(
            backward[...], jnp.concatenate(finals, axis=1), preferred_element_type=jnp.float32
        )
        delta = delta.astype(jnp.bfloat16).astype(jnp.float32)
        for k in range(2):
            element = 2 * pair + k
            part = delta[:, k * width : (k + 1) * width].reshape(inner, steps, width)
            state = values[element + 2, 2 : 2 + inner].astype(jnp.float32) + part
            write(element - 2, state.astype(jnp.bfloat16))


def chooser(where, tiles, edge_tiles, total):
    core, first = where[0, 0], where[0, 2]

    def blocks(table, ids, at, element, row):
        places = [0]
        for offset in OFFSETS:
            wanted = lax.rem(element + (offset + total), total)
            slot = jnp.int32(1)
            for column in range(1, 4):
                slot = jnp.where(where[ids + column, at] == wanted, column + 1, slot)
            places.append(slot)
        return [table[row, place] for place in places + [5, 6]]

    def weights_of(element):
        local = element - 2 + 4 * core
        number = first + local + total
        if 2 <= element < 6:
            return blocks(tiles, 1, local, number, local)
        outer = element if element < 2 else element - 6
        inside = element + 2 if element < 2 else element - 2
        here = blocks(tiles, 1, inside, number, inside)
        there = blocks(edge_tiles, 5, 6 - 6 * core + outer, number, outer)
        away = core == (0 if element < 2 else 1)
        return [jnp.where(away, two, one) for one, two in zip(here, there)]

    return weights_of


def lay_tiles(weights_of, pair, across, along, to_across, to_along):
    width = along.shape[-1]
    for k in range(2):
        own, two_before, before, behind, two_behind, below, above = weights_of(2 * pair + k)
        lanes = slice(k * width, (k + 1) * width)
        for at, block in enumerate((two_before, before, own, behind, two_behind)):
            across[to_across, (at + k) * width : (at + k + 1) * width, lanes] = block
        empty = 5 - 5 * k
        across[to_across, empty * width : (empty + 1) * width, lanes] = jnp.zeros_like(own)
        along[to_along + k, :width] = below
        along[to_along + k, width:] = above


def pack_kernel(start, reaction, source, _, fields):
    for at, field in enumerate((start, reaction, source)):
        fields[at] = field[...]


def fields_kernel(where, fields, others, diag, ids, _, bundle, edge):
    layers = fields.shape[1]
    core, base = where[0], where[1]
    window = bundle.shape[0] // 3
    for at in range(3):
        for place in range(window):
            layer = jnp.clip(base + place, 0, 2 * layers - 1)
            own = layer // layers == core
            layer = lax.rem(layer, layers)
            row = jnp.where(own, fields[at, layer], others[at, layer])
            bundle[at * window + place] = row
            edge[at * window + place] = jnp.where(core == 0, row[0:2], row[6:8])
    edge[3 * window] = jnp.where(core == 0, diag[0:2], diag[6:8])
    for at in range(2):
        edge[3 * window + 1 + at, :, 0:8] = ids[2 * at : 2 * at + 2].astype(jnp.float32)


def arrive(where, count, chunks, order, arrived, values, at_elements):
    core, mine = where[0, 0], where[0, 3]
    steps, rows, width = arrived.shape
    local = steps // count
    for k, part in enumerate(chunks):
        arrived[pl.ds(lax.bitwise_xor(mine, k) * local, local)] = part[...]
    size = steps * GROUP * 4
    groups = rows // (GROUP * 4)
    for group in range(0, groups, 2):
        both = [
            arrived[:, place * GROUP * 4 : (place + 1) * GROUP * 4].reshape(size, width)
            for place in range(group, min(group + 2, groups))
        ]
        moved = jnp.dot(
            order[...], jnp.concatenate(both, axis=1), preferred_element_type=jnp.float32
        ).astype(jnp.bfloat16)
        for k in range(len(both)):
            values[pl.ds(at_elements, 4), (group + k) * GROUP : (group + k + 1) * GROUP] = moved[
                :, k * width : (k + 1) * width
            ].reshape(4, GROUP, steps, width)


def ready_kernel(all_layers, total, count, where, order, tiles, bundle, bundle_edge, diag_own,
                 *rest):
    own, beside = rest[:count], rest[count : 2 * count]
    coef, diag, inverse, values, across, along, arrived = rest[2 * count :]
    core, base = where[0, 0], where[0, 1]
    arrive(where, count, own, order, arrived, values, 4)
    arrive(where, count, beside, order, arrived, values, 8 - 8 * core)
    window = bundle.shape[0] // 3
    width = bundle.shape[2]
    sublane = lax.broadcasted_iota(jnp.int32, (8, width), 0)

    def widened(row, pair):
        turned = jnp.where(core == 0, pltpu.roll(row, 2, 0), pltpu.roll(row, 6, 0))
        for k in range(2):
            turned = jnp.where(
                sublane == 6 * core + k, jnp.broadcast_to(pair[k : k + 1], (8, width)), turned
            )
        return turned

    for at in range(3):
        for place in range(window):
            coef[at, place] = widened(bundle[at * window + place], bundle_edge[at * window + place])
    diag[...] = widened(diag_own[...], bundle_edge[3 * window])
    wide, half = inverse.shape[2:4]
    row = lax.broadcasted_iota(jnp.int32, (half, width), 0)
    eigen = []
    for numbers in transform_tables(2 * half)[2]:
        column = jnp.full((half, width), float(numbers[0]), jnp.float32)
        for at in range(1, half):
            column = jnp.where(row == at, float(numbers[at]), column)
        eigen.append(column)
    layer = lax.broadcasted_iota(jnp.int32, (wide, 1, width), 0) + (base + 1)
    inside = jnp.where((layer >= 0) & (layer < all_layers), 1.0, 0.0).astype(jnp.float32)
    for element in range(8):
        start = coef[0, 1 : 1 + wide, element : element + 1, :]
        reaction = coef[1, 1 : 1 + wide, element : element + 1, :]
        real = diag[element : element + 1, :][None] + 3.0 * reaction * start * start
        near = eigen[0][None] + real
        far = eigen[2][None] + real
        imag = eigen[1][None]
        near_over = inside / (near * near + imag * imag)
        inverse[element, 0] = near * near_over
        inverse[element, 1] = -imag * near_over
        inverse[element, 2] = far * (inside / (far * far + imag * imag))
    weights_of = chooser(where, tiles, None, total)
    for pair in (1, 2):
        lay_tiles(weights_of, pair, across, along, pair - 1, 2 * pair - 2)


class Joined:
    def __init__(self, outer, inner, each):
        self.outer, self.inner, self.each = outer, inner, each

    def __getitem__(self, at):
        if self.each <= at < 3 * self.each:
            return self.inner.at[at - self.each]
        return self.outer.at[at if at < self.each else at - 2 * self.each]


def first_kernel(total, count, where, order, tiles, edge_one, edge_two, coef, diag, inverse, ready,
                 inner_across, inner_along, forward, backward, *rest):
    chunks = rest[:count]
    out, message, across, along, edge_tiles, arrived, values, packed, spec = rest[count:]
    core, group = where[0, 0], where[0, 4]
    edge_tiles[group] = edge_one[...]
    edge_tiles[1 - group] = edge_two[...]
    weights_of = chooser(where, tiles, edge_tiles, total)
    lay_tiles(weights_of, 0, across, along, 0, 0)
    lay_tiles(weights_of, 3, across, along, 1, 2)
    values[4:8] = ready[4:8]
    values[pl.ds(8 - 8 * core, 4)] = ready[pl.ds(8 - 8 * core, 4)]
    arrive(where, count, chunks, order, arrived, values, 8 * core)

    def write(element, state):
        out[element] = state

    newton(values, Joined(across, inner_across, 1), Joined(along, inner_along, 2), coef, diag,
           inverse, forward, backward, packed, spec, 0, write)
    layers = out.shape[1]
    for at in range(2):
        message[at * (layers - 2) : (at + 1) * (layers - 2)] = out[2 * core + at, 1 : layers - 1]
        begin = 2 * (layers - 2) + at * (layers - 4)
        message[begin : begin + layers - 4] = out[2 - 2 * core + at, 2 : layers - 2]


def second_kernel(count, where, order, coef, diag, inverse, across, along, inner_across,
                  inner_along, forward, backward, own, beside, far, out, values, packed, spec,
                  solved):
    core, mine = where[0, 0], where[0, 3]
    layers, steps, width = own.shape[1:]
    values[4:8] = own[...]
    values[pl.ds(8 - 8 * core, 4)] = beside[...]
    for at in range(2):
        values[2 + 6 * core + at, 1 : layers - 1] = far[
            at * (layers - 2) : (at + 1) * (layers - 2)
        ]
        begin = 2 * (layers - 2) + at * (layers - 4)
        values[10 * core + at, 2 : layers - 2] = far[begin : begin + layers - 4]

    def write(element, state):
        solved[element] = state

    newton(values, Joined(across, inner_across, 1), Joined(along, inner_along, 2), coef, diag,
           inverse, forward, backward, packed, spec, 2, write)
    size = steps * GROUP * 4
    local = steps // count
    for group in range(solved.shape[1] // GROUP):
        part = solved[:, group * GROUP : (group + 1) * GROUP].reshape(size, width)
        moved = jnp.dot(order[...], part, preferred_element_type=jnp.float32)
        moved = moved.astype(jnp.bfloat16).reshape(steps, GROUP * 4, width)
        cut = pl.ds(group * GROUP * 4, GROUP * 4)
        for goal in range(count):
            side = lax.bitwise_xor(goal % 2, core)
            place = lax.bitwise_xor(goal // 2, mine // 2)
            out[side, pl.ds(place * local, local), cut] = moved[goal * local : (goal + 1) * local]


def last_kernel(count, where, order, *rest):
    parts, out = rest[:-1], rest[-1]
    steps, layers, elems, width = out.shape
    half = count // 2
    layers //= half
    mine = where[3]
    for k, part in enumerate(parts):
        both = [part[lax.bitwise_xor(lax.rem(mine, 2), side)].reshape(-1, width) for side in range(2)]
        moved = jnp.dot(
            order[...], jnp.concatenate(both, axis=0), preferred_element_type=jnp.float32
        )
        place = lax.bitwise_xor(mine // 2, k)
        out[:, pl.ds(place * layers, layers)] = moved.reshape(steps, layers, elems, width)


def call(kernel, out_shape, scratch, scalars, arrays, later_than=()):
    vmem = pl.BlockSpec(memory_space=pltpu.VMEM)
    return pl.pallas_call(
        kernel,
        out_shape=out_shape,
        in_specs=[pl.BlockSpec(memory_space=pltpu.SMEM)] * len(scalars)
        + [vmem] * len(arrays)
        + [pl.BlockSpec(memory_space=pl.ANY)] * len(later_than),
        out_specs=jax.tree.map(lambda _: vmem, out_shape),
        scratch_shapes=scratch,
        compiler_params=pltpu.CompilerParams(vmem_limit_bytes=32 * 1024 * 1024),
    )(*scalars, *arrays, *later_than)


def shards(state_guess, start_state, reaction, source, self_diag, tiles, neighbors):
    local_steps, local_layers, local_elems, width = state_guess.shape
    count = lax.axis_size("tm")
    sections = lax.axis_size("space")
    mine, core = lax.axis_index("tm"), lax.axis_index("layer")
    steps = local_steps * count
    all_layers = local_layers * 2
    chip_layers = all_layers // count

    def rank(device):
        return device % 2 * (count // 2) + device // 2

    window = -(-(chip_layers + 2 * APPLICATIONS) // GROUP) * GROUP
    half = local_elems // 2
    swap = [(0, 1), (1, 0)]
    circle = []
    for section in range(sections):
        one, other = 2 * section + 1, 2 * ((section + 1) % sections)
        circle += [(one, other), (other, one)]

    def over_core(array):
        return lax.ppermute(array, "layer", swap)

    def over_circle(array):
        return lax.ppermute(array, ("space", "layer"), circle)

    def exchanged(parts):
        return [parts[0]] + [
            lax.ppermute(parts[k], "tm", [(i, i ^ k) for i in range(count)])
            for k in range(1, count)
        ]

    def held(shape, dtype=jnp.bfloat16):
        return jax.ShapeDtypeStruct(shape, dtype)

    pair = state_guess.astype(jnp.bfloat16).reshape(local_steps, local_layers, 2, half, width)
    flat = (local_steps, local_layers * half, width)
    keep = lax.dynamic_index_in_dim(pair, core, 2, keepdims=False).reshape(flat)
    give = lax.dynamic_index_in_dim(pair, 1 - core, 2, keepdims=False).reshape(flat)
    got = over_core(give)
    below = jnp.zeros((local_steps, APPLICATIONS * half, width), jnp.bfloat16)
    above = jnp.zeros(
        (local_steps, (window - chip_layers - APPLICATIONS) * half, width), jnp.bfloat16
    )
    whole = jnp.concatenate(
        [below, jnp.where(core == 0, keep, got), jnp.where(core == 0, got, keep), above], 1
    )
    pieces = [
        lax.dynamic_slice_in_dim(
            whole, rank(lax.bitwise_xor(mine, k)) * (chip_layers * half), window * half, 1
        )
        for k in range(count)
    ]
    chunks = exchanged(pieces)
    across = [over_circle(chunk) for chunk in chunks]
    beside = [over_core(chunk) for chunk in chunks]

    section = lax.axis_index("space") * local_elems
    place = jnp.stack(
        [core, rank(mine) * chip_layers - APPLICATIONS, section, mine, lax.axis_index("group")]
    ).astype(jnp.int32)
    edge_one = over_circle(
        lax.dynamic_index_in_dim(tiles, 6 * core + lax.axis_index("group"), 0, keepdims=False)
    )
    edge_two = lax.ppermute(edge_one, "group", swap)
    fields = call(
        pack_kernel,
        held((3,) + start_state.shape, jnp.float32),
        [],
        [],
        [start_state, reaction, source],
        [pieces[1]],
    )
    ids = neighbors.T
    bundle, bundle_edge = call(
        fields_kernel,
        (
            held((3 * window, local_elems, width), jnp.float32),
            held((3 * window + 3, 2, width), jnp.float32),
        ),
        [],
        [place],
        [fields, over_core(fields), self_diag, ids],
        [chunks[1]],
    )
    bundle_edge = over_circle(bundle_edge)
    edge_ids = bundle_edge[3 * window + 1 :, :, :local_elems].reshape(4, local_elems)
    where = jnp.concatenate(
        [jnp.pad(place[None], ((0, 0), (0, local_elems - 5))), ids, edge_ids.astype(jnp.int32)], 0
    )

    forward, backward, _ = transform_tables(steps)
    order = np.zeros((4, GROUP, steps, steps, GROUP, 4), np.float32)
    for element in range(4):
        for layer in range(GROUP):
            order[element, layer, :, :, layer, element] = np.eye(steps)
    order = order.reshape(4 * GROUP * steps, steps * GROUP * 4)
    last = window - 8
    order_last = np.zeros(
        (local_steps, chip_layers, 2, half, 2, local_steps, last, half), np.float32
    )
    for step in range(local_steps):
        for layer in range(chip_layers):
            for side in range(2):
                order_last[step, layer, side, :, side, step, layer, :] = np.eye(half)
    order_last = order_last.reshape(local_steps * chip_layers * 2 * half, -1)

    def constant(matrix):
        return jnp.asarray(matrix.astype(jnp.bfloat16))

    def table(matrix, layers):
        return constant(np.kron(np.eye(layers), matrix))

    def scratch(layers):
        return [
            pltpu.VMEM((12, layers, steps, width), jnp.bfloat16),
            pltpu.VMEM((8, layers - 2, steps, width), jnp.bfloat16),
            pltpu.VMEM((4, layers - 2, steps, width), jnp.float32),
        ]

    total = local_elems * sections
    two_across, four_along = held((2, 6 * width, 2 * width)), held((4, 2 * width, width))
    arrived = pltpu.VMEM((steps, window * half, width), jnp.bfloat16)
    coef, diag, inverse, ready, inner_across, inner_along = call(
        lambda *refs: ready_kernel(all_layers, total, count, *refs),
        (
            held((3, window, 8, width), jnp.float32),
            held((8, width), jnp.float32),
            held((8, 3, window - 2, steps // 2, width), jnp.float32),
            held((12, window, steps, width)),
            two_across,
            four_along,
        ),
        [arrived],
        [where],
        [constant(order), tiles, bundle, bundle_edge, self_diag, *chunks, *beside],
    )
    state, edge, outer_across, outer_along = call(
        lambda *refs: first_kernel(total, count, *refs),
        (
            held((4, window - 4, steps, width)),
            held((2 * (window - 6) + 2 * (window - 8), steps, width)),
            two_across,
            four_along,
        ),
        [pltpu.VMEM((2,) + tiles.shape[1:], jnp.bfloat16), arrived] + scratch(window),
        [where],
        [constant(order), tiles, edge_one, edge_two, coef, diag, inverse, ready, inner_across,
         inner_along, table(forward, window - 2), table(backward, window - 4), *across],
    )
    solved = call(
        lambda *refs: second_kernel(count, *refs),
        held((2, steps // 2, last * half, width)),
        scratch(window - 4) + [pltpu.VMEM((4, last, steps, width), jnp.bfloat16)],
        [where],
        [constant(order.T), coef, diag, inverse, outer_across, outer_along, inner_across,
         inner_along, table(forward, window - 6), table(backward, last),
         state, over_core(state), over_circle(edge)],
    )

    keep, got = solved[0], over_core(solved[1])
    parts = []
    for k in range(count // 2):
        cut = slice(k * local_steps, (k + 1) * local_steps)
        pairs = []
        for device in range(count):
            for side in range(2):
                goal = 2 * (device // 2 ^ k) + side
                pairs.append((2 * device + side, 2 * goal + device % 2))
        parts.append(lax.ppermute(jnp.stack([keep[cut], got[cut]]), ("tm", "layer"), pairs))
    return call(
        lambda *refs: last_kernel(count, *refs),
        held(state_guess.shape, jnp.float32),
        [],
        [place],
        [constant(order_last), *parts],
    )


def solution(mesh):
    in_specs = (
        P("tm", ("group", "layer"), "space", None),
        P(("group", "layer"), "space", None),
        P(("group", "layer"), "space", None),
        P(("group", "layer"), "space", None),
        P("space", None),
        P("space", None, None, None),
        P("space", None),
    )
    out_specs = P("tm", ("group", "layer"), "space", None)
    return jax.shard_map(shards, mesh=mesh, in_specs=in_specs, out_specs=out_specs, check_vma=False)
```

time: 51.8 us -> 49.1 us (0.948)
  local copies, waits for them, and re-layouts: 3.25 us -> 0.28 us
  waiting for transfers between devices: 15.9 us -> 18.3 us
  starting transfers between devices: 21 us -> 19.6 us
  Pallas kernels: 9.98 us -> 9.2 us
    unnamed x28 -> x26, local copies, waits for them, and re-layouts: 2.09 us -> 0.07 us
    ppermute x3, waiting for transfers between devices: 2.06 us -> 3.46 us  [exchanged(): lax.ppermute(parts[k], 'tm', [(i, i ^ k) for i in range(count)])]
    ppermute x10 -> x8, waiting for transfers between devices: 1.05 us -> 2.14 us  [over_core(): return lax.ppermute(array, 'layer', swap)]
    ppermute x2, waiting for transfers between devices: 4.18 us -> 3.15 us  [shards(): lax.ppermute(jnp.stack([keep[cut], got[cut]]), ('tm', 'layer'), pairs)]
    ppermute x7, starting transfers between devices: 8.23 us -> 7.28 us  [over_circle(): return lax.ppermute(array, ('space', 'layer'), circle)]
    squeeze x1, local copies, waits for them, and re-layouts: 0.95 us -> 0.02 us  [shards(): lax.dynamic_index_in_dim(tiles, 6 * core + lax.axis_index('group'), 0, ke...]
    ppermute x7, waiting for transfers between devices: 8.65 us -> 9.53 us  [over_circle(): return lax.ppermute(array, ('space', 'layer'), circle)]
    pallas_call x4 -> x6, Pallas kernels: 9.98 us -> 9.2 us  [call(): pl.pallas_call(kernel, out_shape=out_shape, in_specs=[pl.BlockSpec(memory...]
  transfers between devices with their start and end apart: 23 -> 21, of which waited for: 8 -> 10; matrix products, arithmetic and copies ran while one was open for 4% -> 0% of each run, Pallas kernels for 1% -> 4%
where the time goes in v3:
time: 49.1 us; the launch traced here: 49 us
  starting transfers between devices  19.6 us (40%)
  waiting for transfers between devices  18.3 us (37%)
  Pallas kernels  9.2 us (19%)
  other arithmetic  1.18 us (2%)
    ppermute x7, waiting for transfers between devices, over_circle(): return lax.ppermute(array, ('space', 'layer'), circle)  9.53 us
    pallas_call x6, Pallas kernels, call(): pl.pallas_call(kernel, out_shape=out_shape, in_specs=[pl.BlockSpec(memory...  9.2 us
    ppermute x7, starting transfers between devices, over_circle(): return lax.ppermute(array, ('space', 'layer'), circle)  7.28 us
    ppermute x2, starting transfers between devices, shards(): lax.ppermute(jnp.stack([keep[cut], got[cut]]), ('tm', 'layer'), pairs)  4.33 us
    ppermute x3, starting transfers between devices, exchanged(): lax.ppermute(parts[k], 'tm', [(i, i ^ k) for i in range(count)])  3.61 us
    ppermute x3, waiting for transfers between devices, exchanged(): lax.ppermute(parts[k], 'tm', [(i, i ^ k) for i in range(count)])  3.46 us
    ppermute x8, starting transfers between devices, over_core(): return lax.ppermute(array, 'layer', swap)  3.18 us
    ppermute x2, waiting for transfers between devices, shards(): lax.ppermute(jnp.stack([keep[cut], got[cut]]), ('tm', 'layer'), pairs)  3.15 us
  transfers between devices with their start and end apart: 21, of which 10 were waited for; matrix products, arithmetic and copies ran while one was open for 0% of the time, Pallas kernels for 4%

profile of v3, /device:TPU:1, one launch (start us, length us, event | category | flops | bytes accessed | tf_op | source)
XLA Modules:
  0.0 49.0 jit_solution(7831305485239381769)
XLA Ops:
  0.1 1.1 %convert_element_type.9 = bf16[4,16,8,128]{3,2,1,0:T(8,128)(2,1)S(1)} convert(f32[4,16,8,128]{3,2,1,0:T(8,128)} %param.15) | non-fusion elementwise | flops 65536 | bytes 393216 | tf_op jit(solution)/shard_map/convert_element_type | solution.py:403
  1.2 0.1 constant_dynamic-slice_fusion.5
  1.2 0.1 collective-permute-start
  1.5 1.1 %collective-permute-done = bf16[4,64,128]{2,1,0:T(8,128)(2,1)S(1)} collective-permute-done((bf16[4,64,128]{2,1,0:T(8,128)(2,1)S(1)}, bf16[4,64,128]{2,1,0:T(8,128)(2,1)S(1)}, u32[]{:S(2)}, u32[]{:S(2)}) %collective-permute-start) | collective-permute-done | bytes 65568 | tf_op jit(solution)/shard_map/ppermute | solution.py:389
  2.7 0.0 copy-start.4
  2.7 0.0 copy-start.5
  2.7 0.2 collective-permute-start.1
  3.0 2.7 %collective-permute-start.10 = (bf16[7,128,128]{2,1,0:T(8,128)(2,1)S(1)}, bf16[7,128,128]{2,1,0:T(8,128)(2,1)S(1)}, u32[]{:S(2)}, u32[]{:S(2)}) collective-permute-start(bf16[7,128,128]{2,1,0:T(8,128)(2,1)S(1)} %dynamic-slice_bitcast_fusion), channel_id=1, source_target_pairs={{1,2},{2,1},{3,0},{0,3},{5,6},{6,5},{7,4},{4,7},{9,10},{10,9},{11,... | collective-permute-start | bytes 688136 | tf_op jit(solution)/shard_map/ppermute | solution.py:392
  5.6 1.3 %collective-permute-start.2 = (bf16[4,64,128]{2,1,0:T(8,128)(2,1)S(1)}, bf16[4,64,128]{2,1,0:T(8,128)(2,1)S(1)}, u32[]{:S(2)}, u32[]{:S(2)}) collective-permute-start(bf16[4,64,128]{2,1,0:T(8,128)(2,1)S(1)} %get-tuple-element.32._), channel_id=1, source_target_pairs={{0,4},{4,0},{8,12},{12,8},{1,5},{5,1},{9,13},{13,9},{2,6},{6,2},{1... | collective-permute-start | bytes 196616 | tf_op jit(solution)/shard_map/ppermute | solution.py:396
  6.9 2.2 %collective-permute-start.5 = (bf16[4,64,128]{2,1,0:T(8,128)(2,1)S(1)}, bf16[4,64,128]{2,1,0:T(8,128)(2,1)S(1)}, u32[]{:S(2)}, u32[]{:S(2)}) collective-permute-start(bf16[4,64,128]{2,1,0:T(8,128)(2,1)S(1)} %get-tuple-element.29), channel_id=1, source_target_pairs={{0,12},{4,8},{8,4},{12,0},{1,13},{5,9},{9,5},{13,1},{2,14},{6,10},... | collective-permute-start | bytes 196616 | tf_op jit(solution)/shard_map/ppermute | solution.py:396
  9.1 0.1 collective-permute-start.4
  9.3 0.1 stack.37.where.refs_0_
  9.3 0.0 collective-permute-done.2._.refs_7_
  9.3 0.0 collective-permute-done.1.others
  9.4 0.6 %shard_map.146 = (f32[48,8,128]{2,1,0:T(8,128)S(1)}, f32[51,2,128]{2,1,0:T(2,128)S(1)}) custom-call(s32[5]{0:T(128)S(1)} %stack.37.where.refs_0_, f32[3,16,8,128]{3,2,1,0:T(8,128)S(1)} %shard_map.145.fields, f32[3,16,8,128]{3,2,1,0:T(8,128)S(1)} %collective-permute-done.1.others, f32[8,128]{1,0:T(8,128)S(1)} %copy-done.11, s32[4,8]{1,0:T(4,128)S(1)} %bitcast.23, ...), custom_call_target="tpu_custom_call" | custom-call | tf_op jit(solution)/shard_map/pallas_call | solution.py:356
  10.0 1.1 %collective-permute-start.3 = (f32[51,2,128]{2,1,0:T(2,128)S(1)}, f32[51,2,128]{2,1,0:T(2,128)S(1)}, u32[]{:S(2)}, u32[]{:S(2)}) collective-permute-start(f32[51,2,128]{2,1,0:T(2,128)S(1)} %get-tuple-element.17), channel_id=1, source_target_pairs={{1,2},{2,1},{3,0},{0,3},{5,6},{6,5},{7,4},{4,7},{9,10},{10,9},{11,... | collective-permute-start | bytes 156680 | tf_op jit(solution)/shard_map/ppermute | solution.py:392
  11.1 0.0 collective-permute-start.6
  11.1 1.5 %collective-permute-done.5.refs_9_ = bf16[4,64,128]{2,1,0:T(8,128)(2,1)S(1)} collective-permute-done((bf16[4,64,128]{2,1,0:T(8,128)(2,1)S(1)}, bf16[4,64,128]{2,1,0:T(8,128)(2,1)S(1)}, u32[]{:S(2)}, u32[]{:S(2)}) %collective-permute-start.5) | collective-permute-done | bytes 65568 | tf_op jit(solution)/shard_map/ppermute | solution.py:396
  12.6 1.6 %collective-permute-start.7 = (bf16[4,64,128]{2,1,0:T(8,128)(2,1)S(1)}, bf16[4,64,128]{2,1,0:T(8,128)(2,1)S(1)}, u32[]{:S(2)}, u32[]{:S(2)}) collective-permute-start(bf16[4,64,128]{2,1,0:T(8,128)(2,1)S(1)} %collective-permute-done.2._.refs_7_), channel_id=1, source_target_pairs={{0,1},{1,0},{2,3},{3,2},{4,5},{5,4},{6,7},{7,6},{8,9},{9,8},{10,11... | collective-permute-start | bytes 196616 | tf_op jit(solution)/shard_map/ppermute | solution.py:389
  14.2 2.0 %collective-permute-done.4.refs_8_ = bf16[4,64,128]{2,1,0:T(8,128)(2,1)S(1)} collective-permute-done((bf16[4,64,128]{2,1,0:T(8,128)(2,1)S(1)}, bf16[4,64,128]{2,1,0:T(8,128)(2,1)S(1)}, u32[]{:S(2)}, u32[]{:S(2)}) %collective-permute-start.4) | collective-permute-done | bytes 65568 | tf_op jit(solution)/shard_map/ppermute | solution.py:396
  16.2 0.4 collective-permute-start.9
  16.6 0.1 collective-permute-start.8
  16.7 0.0 collective-permute-done.3.refs_4_
  16.7 1.2 %collective-permute-start.11 = (bf16[7,128,128]{2,1,0:T(8,128)(2,1)S(1)}, bf16[7,128,128]{2,1,0:T(8,128)(2,1)S(1)}, u32[]{:S(2)}, u32[]{:S(2)}) collective-permute-start(bf16[7,128,128]{2,1,0:T(8,128)(2,1)S(1)} %collective-permute-done.10.refs_3_), channel_id=1, source_target_pairs={{0,16},{16,0},{1,17},{17,1},{2,18},{18,2},{3,19},{19,3},{4,20},{20... | collective-permute-start | bytes 688136 | tf_op jit(solution)/shard_map/ppermute | solution.py:432
  17.9 0.0 collective-permute-done.6.refs_10_
  17.9 0.8 %collective-permute-start.12 = (bf16[4,64,128]{2,1,0:T(8,128)(2,1)S(1)}, bf16[4,64,128]{2,1,0:T(8,128)(2,1)S(1)}, u32[]{:S(2)}, u32[]{:S(2)}) collective-permute-start(bf16[4,64,128]{2,1,0:T(8,128)(2,1)S(1)} %get-tuple-element.31.refs_6_), channel_id=1, source_target_pairs={{1,2},{2,1},{3,0},{0,3},{5,6},{6,5},{7,4},{4,7},{9,10},{10,9},{11,... | collective-permute-start | bytes 196616 | tf_op jit(solution)/shard_map/ppermute | solution.py:392
  18.8 0.9 %collective-permute-start.15 = (bf16[4,64,128]{2,1,0:T(8,128)(2,1)S(1)}, bf16[4,64,128]{2,1,0:T(8,128)(2,1)S(1)}, u32[]{:S(2)}, u32[]{:S(2)}) collective-permute-start(bf16[4,64,128]{2,1,0:T(8,128)(2,1)S(1)} %collective-permute-done.5.refs_9_), channel_id=1, source_target_pairs={{1,2},{2,1},{3,0},{0,3},{5,6},{6,5},{7,4},{4,7},{9,10},{10,9},{11,... | collective-permute-start | bytes 196616 | tf_op jit(solution)/shard_map/ppermute | solution.py:392
  19.7 0.8 %collective-permute-start.14 = (bf16[4,64,128]{2,1,0:T(8,128)(2,1)S(1)}, bf16[4,64,128]{2,1,0:T(8,128)(2,1)S(1)}, u32[]{:S(2)}, u32[]{:S(2)}) collective-permute-start(bf16[4,64,128]{2,1,0:T(8,128)(2,1)S(1)} %collective-permute-done.4.refs_8_), channel_id=1, source_target_pairs={{1,2},{2,1},{3,0},{0,3},{5,6},{6,5},{7,4},{4,7},{9,10},{10,9},{11,... | collective-permute-start | bytes 196616 | tf_op jit(solution)/shard_map/ppermute | solution.py:392
  20.5 0.9 %collective-permute-start.13 = (bf16[4,64,128]{2,1,0:T(8,128)(2,1)S(1)}, bf16[4,64,128]{2,1,0:T(8,128)(2,1)S(1)}, u32[]{:S(2)}, u32[]{:S(2)}) collective-permute-start(bf16[4,64,128]{2,1,0:T(8,128)(2,1)S(1)} %collective-permute-done.2._.refs_7_), channel_id=1, source_target_pairs={{1,2},{2,1},{3,0},{0,3},{5,6},{6,5},{7,4},{4,7},{9,10},{10,9},{11,... | collective-permute-start | bytes 196616 | tf_op jit(solution)/shard_map/ppermute | solution.py:392
  21.5 1.4 %shard_map.147 = (f32[3,16,8,128]{3,2,1,0:T(8,128)S(1)}, f32[8,128]{1,0:T(8,128)S(1)}, f32[8,3,14,8,128]{4,3,2,1,0:T(8,128)S(1)}, bf16[12,16,16,128]{3,2,1,0:T(8...) custom-call(s32[9,8]{1,0:T(8,128)S(1)} %fusion.refs_0_, ...), custom_call_target="tpu_custom_call" | custom-call | tf_op jit(solution)/shard_map/pallas_call | solution.py:356
  22.9 1.1 %collective-permute-done.15.refs_16_ = bf16[4,64,128]{2,1,0:T(8,128)(2,1)S(1)} collective-permute-done((bf16[4,64,128]{2,1,0:T(8,128)(2,1)S(1)}, bf16[4,64,128]{2,1,0:T(8,128)(2,1)S(1)}, u32[]{:S(2)}, u32[]{:S(2)}) %collective-permute-start.15) | collective-permute-done | bytes 65568 | tf_op jit(solution)/shard_map/ppermute | solution.py:392
  24.0 1.4 %collective-permute-done.14.refs_15_ = bf16[4,64,128]{2,1,0:T(8,128)(2,1)S(1)} collective-permute-done((bf16[4,64,128]{2,1,0:T(8,128)(2,1)S(1)}, bf16[4,64,128]{2,1,0:T(8,128)(2,1)S(1)}, u32[]{:S(2)}, u32[]{:S(2)}) %collective-permute-start.14) | collective-permute-done | bytes 65568 | tf_op jit(solution)/shard_map/ppermute | solution.py:392
  25.4 1.4 %collective-permute-done.13.refs_14_ = bf16[4,64,128]{2,1,0:T(8,128)(2,1)S(1)} collective-permute-done((bf16[4,64,128]{2,1,0:T(8,128)(2,1)S(1)}, bf16[4,64,128]{2,1,0:T(8,128)(2,1)S(1)}, u32[]{:S(2)}, u32[]{:S(2)}) %collective-permute-start.13) | collective-permute-done | bytes 65568 | tf_op jit(solution)/shard_map/ppermute | solution.py:392
  26.8 0.0 copy-start.3
  26.8 0.0 copy-start.6
  26.9 0.0 copy-start.10
  26.9 3.1 %shard_map.148 = (bf16[4,12,16,128]{3,2,1,0:T(8,128)(2,1)S(1)}, bf16[36,16,128]{2,1,0:T(8,128)(2,1)S(1)}, bf16[2,768,256]{2,1,0:T(8,128)(2,1)S(1)}, bf16[4,256,128]{2,1,0:T(8,128)(2,1)S(1)}) custom-call(s32[9,8]{1,0:T(8,128)S(1)} %fusion.refs_0_, bf16[256,256]{1,0:T(8,128)(2,1)S(1)} %copy-done.1, bf16[8,7,128,128]{3,2,1,0:T(8,128)(2,1)S(1)} %copy-done, ...), custom_call_target="tpu_custom_call" | custom-call | tf_op jit(solution)/shard_map/pallas_call | solution.py:356
  29.9 0.5 collective-permute-start.16
  30.4 5.6 %collective-permute-done.17.refs_13_ = bf16[36,16,128]{2,1,0:T(8,128)(2,1)S(1)} collective-permute-done((bf16[36,16,128]{2,1,0:T(8,128)(2,1)S(1)}, bf16[36,16,128]{2,1,0:T(8,128)(2,1)S(1)}, u32[]{:S(2)}, u32[]{:S(2)}) %collective-permute-start.17) | collective-permute-done | bytes 147488 | tf_op jit(solution)/shard_map/ppermute | solution.py:392
  36.0 0.0 copy-start.2
  36.0 2.6 %shard_map.149 = bf16[2,8,32,128]{3,2,1,0:T(8,128)(2,1)S(1)} custom-call(s32[9,8]{1,0:T(8,128)S(1)} %fusion.refs_0_, bf16[256,256]{1,0:T(8,128)(2,1)S(1)} %copy-done.3, f32[3,16,8,128]{3,2,1,0:T(8,128)S(1)} %get-tuple-element.19.refs_5_.refs_2_, f32[8,128]{1,0:T(8,128)S(1)} %get-tuple-element.20.refs_6_.refs_3_, ...), custom_call_target="tpu_custom_call" | custom-call | tf_op jit(solution)/shard_map/pallas_call | solution.py:356
  38.7 0.3 collective-permute-start.18
  38.9 1.0 %collective-permute-done.18 = bf16[8,32,128]{2,1,0:T(8,128)(2,1)S(1)} collective-permute-done((bf16[8,32,128]{2,1,0:T(8,128)(2,1)S(1)}, bf16[8,32,128]{2,1,0:T(8,128)(2,1)S(1)}, u32[]{:S(2)}, u32[]{:S(2)}) %collective-permute-start.18) | collective-permute-done | bytes 65568 | tf_op jit(solution)/shard_map/ppermute | solution.py:389
  40.0 1.9 %collective-permute-start.19 = (bf16[2,4,32,128]{3,2,1,0:T(8,128)(2,1)S(1)}, bf16[2,4,32,128]{3,2,1,0:T(8,128)(2,1)S(1)}, u32[]{:S(2)}, u32[]{:S(2)}) collective-permute-start(bf16[2,4,32,128]{3,2,1,0:T(8,128)(2,1)S(1)} %pad_maximum_fusion.1), channel_id=1, source_target_pairs={{0,0},{1,4},{4,1},{5,5},{8,8},{9,12},{12,9},{13,13},{2,2},{3,6},{6... | collective-permute-start | bytes 196616 | tf_op jit(solution)/shard_map/ppermute | solution.py:537
  41.9 2.4 %collective-permute-start.20 = (bf16[2,4,32,128]{3,2,1,0:T(8,128)(2,1)S(1)}, bf16[2,4,32,128]{3,2,1,0:T(8,128)(2,1)S(1)}, u32[]{:S(2)}, u32[]{:S(2)}) collective-permute-start(bf16[2,4,32,128]{3,2,1,0:T(8,128)(2,1)S(1)} %pad_maximum_fusion.2), channel_id=1, source_target_pairs={{0,8},{1,12},{4,9},{5,13},{8,0},{9,4},{12,1},{13,5},{2,10},{3,14},... | collective-permute-start | bytes 196616 | tf_op jit(solution)/shard_map/ppermute | solution.py:537
  44.3 1.8 %collective-permute-done.19.refs_2_ = bf16[2,4,32,128]{3,2,1,0:T(8,128)(2,1)S(1)} collective-permute-done((bf16[2,4,32,128]{3,2,1,0:T(8,128)(2,1)S(1)}, bf16[2,4,32,128]{3,2,1,0:T(8,128)(2,1)S(1)}, u32[]{:S(2)}, u32[]{:S(2)}) %collective-permute-start.19) | collective-permute-done | bytes 65568 | tf_op jit(solution)/shard_map/ppermute | solution.py:537
  46.1 1.3 %collective-permute-done.20.refs_3_ = bf16[2,4,32,128]{3,2,1,0:T(8,128)(2,1)S(1)} collective-permute-done((bf16[2,4,32,128]{3,2,1,0:T(8,128)(2,1)S(1)}, bf16[2,4,32,128]{3,2,1,0:T(8,128)(2,1)S(1)}, u32[]{:S(2)}, u32[]{:S(2)}) %collective-permute-start.20) | collective-permute-done | bytes 65568 | tf_op jit(solution)/shard_map/ppermute | solution.py:537
  47.5 1.5 %shard_map.150 = f32[4,16,8,128]{3,2,1,0:T(8,128)} custom-call(s32[5]{0:T(128)S(1)} %stack.37.where.refs_0_, bf16[256,256]{1,0:T(8,128)(2,1)S(1)} %copy-done.2, bf16[2,4,32,128]{3,2,1,0:T(8,128)(2,1)S(1)} %collective-permute-done.19.refs_2_, bf16[2,4,32,128]{3,2,1,0:T(8,128)(2,1)S(1)} %collective-permute-done.20.refs_3_), custom_call_target="tpu_custom_call" | custom-call | tf_op jit(solution)/shard_map/pallas_call | solution.py:356
  (41 shorter events, 0.2 us)
Async XLA Ops:
  0.0 21.5 %copy-start.1 = (bf16[256,256]{1,0:T(8,128)(2,1)S(1)}, bf16[256,256]{1,0:T(8,128)(2,1)}, u32[]{:S(2)}) copy-start(bf16[256,256]{1,0:T(8,128)(2,1)} %constant.118.clone.refs_1_) | copy-start | bytes 393220
  0.0 2.7 %copy-start.9 = (f32[16,8,128]{2,1,0:T(8,128)S(1)}, f32[16,8,128]{2,1,0:T(8,128)}, u32[]{:S(2)}) copy-start(f32[16,8,128]{2,1,0:T(8,128)} %source.1) | copy-start | bytes 196612
  0.0 2.7 %copy-start.8 = (f32[16,8,128]{2,1,0:T(8,128)S(1)}, f32[16,8,128]{2,1,0:T(8,128)}, u32[]{:S(2)}) copy-start(f32[16,8,128]{2,1,0:T(8,128)} %reaction.1) | copy-start | bytes 196612
  0.0 2.7 %copy-start.7 = (f32[16,8,128]{2,1,0:T(8,128)S(1)}, f32[16,8,128]{2,1,0:T(8,128)}, u32[]{:S(2)}) copy-start(f32[16,8,128]{2,1,0:T(8,128)} %start.1) | copy-start | bytes 196612
  0.0 2.9 %copy-start = (bf16[8,7,128,128]{3,2,1,0:T(8,128)(2,1)S(1)}, bf16[8,7,128,128]{3,2,1,0:T(8,128)(2,1)}, u32[]{:S(2)}) copy-start(bf16[8,7,128,128]{3,2,1,0:T(8,128)(2,1)} %refs_2_.3) | copy-start | bytes 5505028
  0.0 9.3 %copy-start.11 = (f32[8,128]{1,0:T(8,128)S(1)}, f32[8,128]{1,0:T(8,128)}, u32[]{:S(2)}) copy-start(f32[8,128]{1,0:T(8,128)} %refs_5_.1) | copy-start | bytes 12292
  0.0 9.3 %copy-start.12 = (s32[8,4]{0,1:T(4,128)S(1)}, s32[8,4]{0,1:T(4,128)}, u32[]{:S(2)}) copy-start(s32[8,4]{0,1:T(4,128)} %param.21) | copy-start | bytes 388
  1.2 1.3 %collective-permute-start = (bf16[4,64,128]{2,1,0:T(8,128)(2,1)S(1)}, bf16[4,64,128]{2,1,0:T(8,128)(2,1)S(1)}, u32[]{:S(2)}, u32[]{:S(2)}) collective-permute-start(bf16[4,64,128]{2,1,0:T(8,128)(2,1)S(1)} %bitcast.28), channel_id=1, source_target_pairs={{0,1},{1,0},{2,3},{3,2},{4,5},{5,4},{6,7},{7,6},{8,9},{9,8},{10,11... | collective-permute-start | bytes 196616 | tf_op jit(solution)/shard_map/ppermute | solution.py:389
  2.7 24.1 %copy-start.4 = (bf16[224,224]{1,0:T(8,128)(2,1)S(1)}, bf16[224,224]{1,0:T(8,128)(2,1)}, u32[]{:S(2)}) copy-start(bf16[224,224]{1,0:T(8,128)(2,1)} %constant.119.clone.refs_11_) | copy-start | bytes 301060
  2.7 24.1 %copy-start.5 = (bf16[192,192]{1,0:T(8,128)(2,1)S(1)}, bf16[192,192]{1,0:T(8,128)(2,1)}, u32[]{:S(2)}) copy-start(bf16[192,192]{1,0:T(8,128)(2,1)} %constant.120.clone.refs_12_) | copy-start | bytes 221188
  2.7 6.6 %collective-permute-start.1 = (f32[3,16,8,128]{3,2,1,0:T(8,128)S(1)}, f32[3,16,8,128]{3,2,1,0:T(8,128)S(1)}, u32[]{:S(2)}, u32[]{:S(2)}) collective-permute-start(f32[3,16,8,128]{3,2,1,0:T(8,128)S(1)} %shard_map.145.fields), channel_id=1, source_target_pairs={{0,1},{1,0},{2,3},{3,2},{4,5},{5,4},{6,7},{7,6},{8,9},{9,8},{10,11... | collective-permute-start | bytes 589832 | tf_op jit(solution)/shard_map/ppermute | solution.py:389
  3.0 13.6 %collective-permute-start.10 = (bf16[7,128,128]{2,1,0:T(8,128)(2,1)S(1)}, bf16[7,128,128]{2,1,0:T(8,128)(2,1)S(1)}, u32[]{:S(2)}, u32[]{:S(2)}) collective-permute-start(bf16[7,128,128]{2,1,0:T(8,128)(2,1)S(1)} %dynamic-slice_bitcast_fusion), channel_id=1, source_target_pairs={{1,2},{2,1},{3,0},{0,3},{5,6},{6,5},{7,4},{4,7},{9,10},{10,9},{11,... | collective-permute-start | bytes 688136 | tf_op jit(solution)/shard_map/ppermute | solution.py:392
  5.6 3.7 %collective-permute-start.2 = (bf16[4,64,128]{2,1,0:T(8,128)(2,1)S(1)}, bf16[4,64,128]{2,1,0:T(8,128)(2,1)S(1)}, u32[]{:S(2)}, u32[]{:S(2)}) collective-permute-start(bf16[4,64,128]{2,1,0:T(8,128)(2,1)S(1)} %get-tuple-element.32._), channel_id=1, source_target_pairs={{0,4},{4,0},{8,12},{12,8},{1,5},{5,1},{9,13},{13,9},{2,6},{6,2},{1... | collective-permute-start | bytes 196616 | tf_op jit(solution)/shard_map/ppermute | solution.py:396
  6.9 5.7 %collective-permute-start.5 = (bf16[4,64,128]{2,1,0:T(8,128)(2,1)S(1)}, bf16[4,64,128]{2,1,0:T(8,128)(2,1)S(1)}, u32[]{:S(2)}, u32[]{:S(2)}) collective-permute-start(bf16[4,64,128]{2,1,0:T(8,128)(2,1)S(1)} %get-tuple-element.29), channel_id=1, source_target_pairs={{0,12},{4,8},{8,4},{12,0},{1,13},{5,9},{9,5},{13,1},{2,14},{6,10},... | collective-permute-start | bytes 196616 | tf_op jit(solution)/shard_map/ppermute | solution.py:396
  9.1 7.0 %collective-permute-start.4 = (bf16[4,64,128]{2,1,0:T(8,128)(2,1)S(1)}, bf16[4,64,128]{2,1,0:T(8,128)(2,1)S(1)}, u32[]{:S(2)}, u32[]{:S(2)}) collective-permute-start(bf16[4,64,128]{2,1,0:T(8,128)(2,1)S(1)} %get-tuple-element.30), channel_id=1, source_target_pairs={{0,8},{4,12},{8,0},{12,4},{1,9},{5,13},{9,1},{13,5},{2,10},{6,14},... | collective-permute-start | bytes 196616 | tf_op jit(solution)/shard_map/ppermute | solution.py:396
  10.0 6.7 %collective-permute-start.3 = (f32[51,2,128]{2,1,0:T(2,128)S(1)}, f32[51,2,128]{2,1,0:T(2,128)S(1)}, u32[]{:S(2)}, u32[]{:S(2)}) collective-permute-start(f32[51,2,128]{2,1,0:T(2,128)S(1)} %get-tuple-element.17), channel_id=1, source_target_pairs={{1,2},{2,1},{3,0},{0,3},{5,6},{6,5},{7,4},{4,7},{9,10},{10,9},{11,... | collective-permute-start | bytes 156680 | tf_op jit(solution)/shard_map/ppermute | solution.py:392
  11.1 6.8 %collective-permute-start.6 = (bf16[4,64,128]{2,1,0:T(8,128)(2,1)S(1)}, bf16[4,64,128]{2,1,0:T(8,128)(2,1)S(1)}, u32[]{:S(2)}, u32[]{:S(2)}) collective-permute-start(bf16[4,64,128]{2,1,0:T(8,128)(2,1)S(1)} %get-tuple-element.31.refs_6_), channel_id=1, source_target_pairs={{0,1},{1,0},{2,3},{3,2},{4,5},{5,4},{6,7},{7,6},{8,9},{9,8},{10,11... | collective-permute-start | bytes 196616 | tf_op jit(solution)/shard_map/ppermute | solution.py:389
  12.6 7.9 %collective-permute-start.7 = (bf16[4,64,128]{2,1,0:T(8,128)(2,1)S(1)}, bf16[4,64,128]{2,1,0:T(8,128)(2,1)S(1)}, u32[]{:S(2)}, u32[]{:S(2)}) collective-permute-start(bf16[4,64,128]{2,1,0:T(8,128)(2,1)S(1)} %collective-permute-done.2._.refs_7_), channel_id=1, source_target_pairs={{0,1},{1,0},{2,3},{3,2},{4,5},{5,4},{6,7},{7,6},{8,9},{9,8},{10,11... | collective-permute-start | bytes 196616 | tf_op jit(solution)/shard_map/ppermute | solution.py:389
  16.2 2.6 %collective-permute-start.9 = (bf16[4,64,128]{2,1,0:T(8,128)(2,1)S(1)}, bf16[4,64,128]{2,1,0:T(8,128)(2,1)S(1)}, u32[]{:S(2)}, u32[]{:S(2)}) collective-permute-start(bf16[4,64,128]{2,1,0:T(8,128)(2,1)S(1)} %collective-permute-done.5.refs_9_), channel_id=1, source_target_pairs={{0,1},{1,0},{2,3},{3,2},{4,5},{5,4},{6,7},{7,6},{8,9},{9,8},{10,11... | collective-permute-start | bytes 196616 | tf_op jit(solution)/shard_map/ppermute | solution.py:389
  16.6 3.1 %collective-permute-start.8 = (bf16[4,64,128]{2,1,0:T(8,128)(2,1)S(1)}, bf16[4,64,128]{2,1,0:T(8,128)(2,1)S(1)}, u32[]{:S(2)}, u32[]{:S(2)}) collective-permute-start(bf16[4,64,128]{2,1,0:T(8,128)(2,1)S(1)} %collective-permute-done.4.refs_8_), channel_id=1, source_target_pairs={{0,1},{1,0},{2,3},{3,2},{4,5},{5,4},{6,7},{7,6},{8,9},{9,8},{10,11... | collective-permute-start | bytes 196616 | tf_op jit(solution)/shard_map/ppermute | solution.py:389
  16.7 10.1 %collective-permute-start.11 = (bf16[7,128,128]{2,1,0:T(8,128)(2,1)S(1)}, bf16[7,128,128]{2,1,0:T(8,128)(2,1)S(1)}, u32[]{:S(2)}, u32[]{:S(2)}) collective-permute-start(bf16[7,128,128]{2,1,0:T(8,128)(2,1)S(1)} %collective-permute-done.10.refs_3_), channel_id=1, source_target_pairs={{0,16},{16,0},{1,17},{17,1},{2,18},{18,2},{3,19},{19,3},{4,20},{20... | collective-permute-start | bytes 688136 | tf_op jit(solution)/shard_map/ppermute | solution.py:432
  17.9 4.9 %collective-permute-start.12 = (bf16[4,64,128]{2,1,0:T(8,128)(2,1)S(1)}, bf16[4,64,128]{2,1,0:T(8,128)(2,1)S(1)}, u32[]{:S(2)}, u32[]{:S(2)}) collective-permute-start(bf16[4,64,128]{2,1,0:T(8,128)(2,1)S(1)} %get-tuple-element.31.refs_6_), channel_id=1, source_target_pairs={{1,2},{2,1},{3,0},{0,3},{5,6},{6,5},{7,4},{4,7},{9,10},{10,9},{11,... | collective-permute-start | bytes 196616 | tf_op jit(solution)/shard_map/ppermute | solution.py:392
  18.8 5.3 %collective-permute-start.15 = (bf16[4,64,128]{2,1,0:T(8,128)(2,1)S(1)}, bf16[4,64,128]{2,1,0:T(8,128)(2,1)S(1)}, u32[]{:S(2)}, u32[]{:S(2)}) collective-permute-start(bf16[4,64,128]{2,1,0:T(8,128)(2,1)S(1)} %collective-permute-done.5.refs_9_), channel_id=1, source_target_pairs={{1,2},{2,1},{3,0},{0,3},{5,6},{6,5},{7,4},{4,7},{9,10},{10,9},{11,... | collective-permute-start | bytes 196616 | tf_op jit(solution)/shard_map/ppermute | solution.py:392
  19.7 5.7 %collective-permute-start.14 = (bf16[4,64,128]{2,1,0:T(8,128)(2,1)S(1)}, bf16[4,64,128]{2,1,0:T(8,128)(2,1)S(1)}, u32[]{:S(2)}, u32[]{:S(2)}) collective-permute-start(bf16[4,64,128]{2,1,0:T(8,128)(2,1)S(1)} %collective-permute-done.4.refs_8_), channel_id=1, source_target_pairs={{1,2},{2,1},{3,0},{0,3},{5,6},{6,5},{7,4},{4,7},{9,10},{10,9},{11,... | collective-permute-start | bytes 196616 | tf_op jit(solution)/shard_map/ppermute | solution.py:392
  20.5 6.3 %collective-permute-start.13 = (bf16[4,64,128]{2,1,0:T(8,128)(2,1)S(1)}, bf16[4,64,128]{2,1,0:T(8,128)(2,1)S(1)}, u32[]{:S(2)}, u32[]{:S(2)}) collective-permute-start(bf16[4,64,128]{2,1,0:T(8,128)(2,1)S(1)} %collective-permute-done.2._.refs_7_), channel_id=1, source_target_pairs={{1,2},{2,1},{3,0},{0,3},{5,6},{6,5},{7,4},{4,7},{9,10},{10,9},{11,... | collective-permute-start | bytes 196616 | tf_op jit(solution)/shard_map/ppermute | solution.py:392
  26.8 9.2 %copy-start.3 = (bf16[256,256]{1,0:T(8,128)(2,1)S(1)}, bf16[256,256]{1,0:T(8,128)(2,1)}, u32[]{:S(2)}) copy-start(bf16[256,256]{1,0:T(8,128)(2,1)} %constant.121.clone.refs_1_) | copy-start | bytes 393220
  26.8 9.2 %copy-start.6 = (bf16[160,160]{1,0:T(8,128)(2,1)S(1)}, bf16[160,160]{1,0:T(8,128)(2,1)}, u32[]{:S(2)}) copy-start(bf16[160,160]{1,0:T(8,128)(2,1)} %constant.122.clone.refs_9_) | copy-start | bytes 153604
  26.9 9.2 %copy-start.10 = (bf16[128,128]{1,0:T(8,128)(2,1)S(1)}, bf16[128,128]{1,0:T(8,128)(2,1)}, u32[]{:S(2)}) copy-start(bf16[128,128]{1,0:T(8,128)(2,1)} %constant.123.clone.refs_10_) | copy-start | bytes 98308
  29.9 6.1 %collective-permute-start.16 = (bf16[4,12,16,128]{3,2,1,0:T(8,128)(2,1)S(1)}, bf16[4,12,16,128]{3,2,1,0:T(8,128)(2,1)S(1)}, u32[]{:S(2)}, u32[]{:S(2)}) collective-permute-start(bf16[4,12,16,128]{3,2,1,0:T(8,128)(2,1)S(1)} %get-tuple-element.27.refs_11_), channel_id=1, source_target_pairs={{0,1},{1,0},{2,3},{3,2},{4,5},{5,4},{6,7},{7,6},{8,9},{9,8},{10,11... | collective-permute-start | bytes 589832 | tf_op jit(solution)/shard_map/ppermute | solution.py:389
  30.4 5.6 %collective-permute-start.17 = (bf16[36,16,128]{2,1,0:T(8,128)(2,1)S(1)}, bf16[36,16,128]{2,1,0:T(8,128)(2,1)S(1)}, u32[]{:S(2)}, u32[]{:S(2)}) collective-permute-start(bf16[36,16,128]{2,1,0:T(8,128)(2,1)S(1)} %get-tuple-element.28), channel_id=1, source_target_pairs={{1,2},{2,1},{3,0},{0,3},{5,6},{6,5},{7,4},{4,7},{9,10},{10,9},{11,... | collective-permute-start | bytes 442376 | tf_op jit(solution)/shard_map/ppermute | solution.py:392
  36.0 11.5 %copy-start.2 = (bf16[256,256]{1,0:T(8,128)(2,1)S(1)}, bf16[256,256]{1,0:T(8,128)(2,1)}, u32[]{:S(2)}) copy-start(bf16[256,256]{1,0:T(8,128)(2,1)} %constant.124.clone.refs_1_) | copy-start | bytes 393220
  38.7 1.3 %collective-permute-start.18 = (bf16[8,32,128]{2,1,0:T(8,128)(2,1)S(1)}, bf16[8,32,128]{2,1,0:T(8,128)(2,1)S(1)}, u32[]{:S(2)}, u32[]{:S(2)}) collective-permute-start(bf16[8,32,128]{2,1,0:T(8,128)(2,1)S(1)} %slice_bitcast_fusion), channel_id=1, source_target_pairs={{0,1},{1,0},{2,3},{3,2},{4,5},{5,4},{6,7},{7,6},{8,9},{9,8},{10,11... | collective-permute-start | bytes 196616 | tf_op jit(solution)/shard_map/ppermute | solution.py:389
  40.0 6.2 %collective-permute-start.19 = (bf16[2,4,32,128]{3,2,1,0:T(8,128)(2,1)S(1)}, bf16[2,4,32,128]{3,2,1,0:T(8,128)(2,1)S(1)}, u32[]{:S(2)}, u32[]{:S(2)}) collective-permute-start(bf16[2,4,32,128]{3,2,1,0:T(8,128)(2,1)S(1)} %pad_maximum_fusion.1), channel_id=1, source_target_pairs={{0,0},{1,4},{4,1},{5,5},{8,8},{9,12},{12,9},{13,13},{2,2},{3,6},{6... | collective-permute-start | bytes 196616 | tf_op jit(solution)/shard_map/ppermute | solution.py:537
  41.9 5.6 %collective-permute-start.20 = (bf16[2,4,32,128]{3,2,1,0:T(8,128)(2,1)S(1)}, bf16[2,4,32,128]{3,2,1,0:T(8,128)(2,1)S(1)}, u32[]{:S(2)}, u32[]{:S(2)}) collective-permute-start(bf16[2,4,32,128]{3,2,1,0:T(8,128)(2,1)S(1)} %pad_maximum_fusion.2), channel_id=1, source_target_pairs={{0,8},{1,12},{4,9},{5,13},{8,0},{9,4},{12,1},{13,5},{2,10},{3,14},... | collective-permute-start | bytes 196616 | tf_op jit(solution)/shard_map/ppermute | solution.py:537

commit v4 on v3

--- a/solution.py
+++ b/solution.py
@@ -12,8 +12,13 @@
 APPLICATIONS = 2 * NEWTON
 OFFSETS = (-2, -1, 1, 2)
 GROUP = 4
+OVER_GROUP = 3
 
 corner_weight = 0.25
+
+
+def chip_rank(device, count):
+    return device % 2 * (count // 2) + device // 2
 
 
 def transform_tables(steps):
@@ -134,30 +139,15 @@
             write(element - 2, state.astype(jnp.bfloat16))
 
 
-def chooser(where, tiles, edge_tiles, total):
-    core, first = where[0, 0], where[0, 2]
-
-    def blocks(table, ids, at, element, row):
-        places = [0]
-        for offset in OFFSETS:
-            wanted = lax.rem(element + (offset + total), total)
-            slot = jnp.int32(1)
-            for column in range(1, 4):
-                slot = jnp.where(where[ids + column, at] == wanted, column + 1, slot)
-            places.append(slot)
-        return [table[row, place] for place in places + [5, 6]]
-
+def chooser(core, slots, tiles):
     def weights_of(element):
-        local = element - 2 + 4 * core
-        number = first + local + total
-        if 2 <= element < 6:
-            return blocks(tiles, 1, local, number, local)
-        outer = element if element < 2 else element - 6
-        inside = element + 2 if element < 2 else element - 2
-        here = blocks(tiles, 1, inside, number, inside)
-        there = blocks(edge_tiles, 5, 6 - 6 * core + outer, number, outer)
-        away = core == (0 if element < 2 else 1)
-        return [jnp.where(away, two, one) for one, two in zip(here, there)]
+        row = element - 2 + 4 * core
+        if element < 2:
+            row = element + 2
+        elif element > 5:
+            row = element - 2
+        places = [0] + [slots[at, row] for at in range(4)] + [5, 6]
+        return [tiles[row, place] for place in places]
 
     return weights_of
 
@@ -175,14 +165,33 @@
         along[to_along + k, width:] = above
 
 
+def trim_kernel(count, *rest):
+    out = rest[-1]
+    for k, piece in enumerate(rest[:count]):
+        local, rows, _ = piece.shape
+        out[k * local : (k + 1) * local] = piece[:, 4 : rows - 4]
+
+
+def gather_kernel(*rest):
+    parts, out = rest[:-1], rest[-1]
+    local = parts[0].shape[0]
+    mine = lax.axis_index("tm")
+    for k, part in enumerate(parts):
+        out[pl.ds(lax.bitwise_xor(mine, k) * local, local)] = part[...]
+
+
 def pack_kernel(start, reaction, source, _, fields):
     for at, field in enumerate((start, reaction, source)):
         fields[at] = field[...]
 
 
-def fields_kernel(where, fields, others, diag, ids, _, bundle, edge):
+def first_layer(count, all_layers):
+    return chip_rank(lax.axis_index("tm"), count) * (all_layers // count) - APPLICATIONS
+
+
+def fields_kernel(count, fields, others, diag, slots, _, bundle, edge):
     layers = fields.shape[1]
-    core, base = where[0], where[1]
+    core, base = lax.axis_index("layer"), first_layer(count, 2 * layers)
     window = bundle.shape[0] // 3
     for at in range(3):
         for place in range(window):
@@ -194,15 +203,11 @@
             edge[at * window + place] = jnp.where(core == 0, row[0:2], row[6:8])
     edge[3 * window] = jnp.where(core == 0, diag[0:2], diag[6:8])
     for at in range(2):
-        edge[3 * window + 1 + at, :, 0:8] = ids[2 * at : 2 * at + 2].astype(jnp.float32)
-
-
-def arrive(where, count, chunks, order, arrived, values, at_elements):
-    core, mine = where[0, 0], where[0, 3]
+        edge[3 * window + 1 + at, :, 0:8] = slots[2 * at : 2 * at + 2].astype(jnp.float32)
+
+
+def arrive(arrived, order, values, at_elements):
     steps, rows, width = arrived.shape
-    local = steps // count
-    for k, part in enumerate(chunks):
-        arrived[pl.ds(lax.bitwise_xor(mine, k) * local, local)] = part[...]
     size = steps * GROUP * 4
     groups = rows // (GROUP * 4)
     for group in range(0, groups, 2):
@@ -219,13 +224,18 @@
             ].reshape(4, GROUP, steps, width)
 
 
-def ready_kernel(all_layers, total, count, where, order, tiles, bundle, bundle_edge, diag_own,
-                 *rest):
-    own, beside = rest[:count], rest[count : 2 * count]
-    coef, diag, inverse, values, across, along, arrived = rest[2 * count :]
-    core, base = where[0, 0], where[0, 1]
-    arrive(where, count, own, order, arrived, values, 4)
-    arrive(where, count, beside, order, arrived, values, 8 - 8 * core)
+def edge_tiles_kernel(tiles, out):
+    at, group = 6 * lax.axis_index("layer"), lax.axis_index("group")
+    count = tiles.shape[1]
+    out[:count] = tiles[at + group]
+    out[count:] = tiles[at + 1 - group, : out.shape[0] - count]
+
+
+def ready_kernel(all_layers, count, slots, order, tiles, bundle, bundle_edge, diag_own, own, beside,
+                 coef, diag, inverse, values, across, along, picks):
+    core, base = lax.axis_index("layer"), first_layer(count, all_layers)
+    arrive(own, order, values, 4)
+    arrive(beside, order, values, 8 - 8 * core)
     window = bundle.shape[0] // 3
     width = bundle.shape[2]
     sublane = lax.broadcasted_iota(jnp.int32, (8, width), 0)
@@ -263,39 +273,53 @@
         inverse[element, 0] = near * near_over
         inverse[element, 1] = -imag * near_over
         inverse[element, 2] = far * (inside / (far * far + imag * imag))
-    weights_of = chooser(where, tiles, None, total)
-    for pair in (1, 2):
-        lay_tiles(weights_of, pair, across, along, pair - 1, 2 * pair - 2)
-
-
-class Joined:
-    def __init__(self, outer, inner, each):
-        self.outer, self.inner, self.each = outer, inner, each
-
-    def __getitem__(self, at):
-        if self.each <= at < 3 * self.each:
-            return self.inner.at[at - self.each]
-        return self.outer.at[at if at < self.each else at - 2 * self.each]
-
-
-def first_kernel(total, count, where, order, tiles, edge_one, edge_two, coef, diag, inverse, ready,
-                 inner_across, inner_along, forward, backward, *rest):
-    chunks = rest[:count]
-    out, message, across, along, edge_tiles, arrived, values, packed, spec = rest[count:]
-    core, group = where[0, 0], where[0, 4]
-    edge_tiles[group] = edge_one[...]
-    edge_tiles[1 - group] = edge_two[...]
-    weights_of = chooser(where, tiles, edge_tiles, total)
-    lay_tiles(weights_of, 0, across, along, 0, 0)
-    lay_tiles(weights_of, 3, across, along, 1, 2)
+    weights_of = chooser(core, slots, tiles)
+    for pair in range(4):
+        lay_tiles(weights_of, pair, across, along, pair, 2 * pair)
+    for k in range(2):
+        for at in range(4):
+            for slot in range(4):
+                hit = jnp.where(slots[4 + at, 6 - 6 * core + k] == slot + 1, 1.0, 0.0)
+                picks[4 * (4 * k + at) + slot] = jnp.full((8, width), hit, jnp.float32)
+
+
+def first_kernel(count, order, coef, diag, inverse, ready, near_across, near_along, picks, edge_one,
+                 edge_two, forward, backward, first, others, out, message, across, along, edge_tiles,
+                 arrived, values, packed, spec):
+    core, mine, group = lax.axis_index("layer"), lax.axis_index("tm"), lax.axis_index("group")
+    rest = 7 - edge_two.shape[0]
+    edge_tiles[group] = edge_one[0:7]
+    edge_tiles[1 - group, 0:rest] = edge_one[7 : 7 + rest]
+    edge_tiles[1 - group, rest:7] = edge_two[...]
+    across[...] = near_across[...]
+    along[...] = near_along[...]
+
+    def weights_of(element):
+        blocks = [edge_tiles[element, 0]]
+        for at in range(4):
+            block = 0.0
+            for slot in range(4):
+                pick = picks[4 * (4 * element + at) + slot, 0:1].astype(jnp.bfloat16)
+                block = block + edge_tiles[element, 1 + slot] * pick
+            blocks.append(block)
+        return blocks + [edge_tiles[element, 5], edge_tiles[element, 6]]
+
+    lay_tiles(weights_of, 0, across, along, 3 * core, 6 * core)
     values[4:8] = ready[4:8]
     values[pl.ds(8 - 8 * core, 4)] = ready[pl.ds(8 - 8 * core, 4)]
-    arrive(where, count, chunks, order, arrived, values, 8 * core)
+    steps, rows, width = arrived.shape
+    local = steps // count
+    arrived[:, :4] = jnp.zeros((steps, 4, width), jnp.bfloat16)
+    arrived[:, rows - 4 :] = jnp.zeros((steps, 4, width), jnp.bfloat16)
+    for k in range(count):
+        part = first[...] if k == 0 else others[(k - 1) * local : k * local]
+        arrived[pl.ds(lax.bitwise_xor(mine, k) * local, local), 4 : rows - 4] = part
+    arrive(arrived, order, values, 8 * core)
 
     def write(element, state):
         out[element] = state
 
-    newton(values, Joined(across, inner_across, 1), Joined(along, inner_along, 2), coef, diag,
+    newton(values, [across.at[k] for k in range(4)], [along.at[k] for k in range(8)], coef, diag,
            inverse, forward, backward, packed, spec, 0, write)
     layers = out.shape[1]
     for at in range(2):
@@ -304,10 +328,9 @@
         message[begin : begin + layers - 4] = out[2 - 2 * core + at, 2 : layers - 2]
 
 
-def second_kernel(count, where, order, coef, diag, inverse, across, along, inner_across,
-                  inner_along, forward, backward, own, beside, far, out, values, packed, spec,
-                  solved):
-    core, mine = where[0, 0], where[0, 3]
+def second_kernel(count, order, coef, diag, inverse, across, along, forward, backward, own, beside,
+                  far, out, values, packed, spec, solved):
+    core, mine = lax.axis_index("layer"), lax.axis_index("tm")
     layers, steps, width = own.shape[1:]
     values[4:8] = own[...]
     values[pl.ds(8 - 8 * core, 4)] = beside[...]
@@ -321,7 +344,7 @@
     def write(element, state):
         solved[element] = state
 
-    newton(values, Joined(across, inner_across, 1), Joined(along, inner_along, 2), coef, diag,
+    newton(values, [across.at[k] for k in range(4)], [along.at[k] for k in range(8)], coef, diag,
            inverse, forward, backward, packed, spec, 2, write)
     size = steps * GROUP * 4
     local = steps // count
@@ -336,12 +359,12 @@
             out[side, pl.ds(place * local, local), cut] = moved[goal * local : (goal + 1) * local]
 
 
-def last_kernel(count, where, order, *rest):
+def last_kernel(count, order, *rest):
     parts, out = rest[:-1], rest[-1]
     steps, layers, elems, width = out.shape
     half = count // 2
     layers //= half
-    mine = where[3]
+    mine = lax.axis_index("tm")
     for k, part in enumerate(parts):
         both = [part[lax.bitwise_xor(lax.rem(mine, 2), side)].reshape(-1, width) for side in range(2)]
         moved = jnp.dot(
@@ -374,9 +397,6 @@
     all_layers = local_layers * 2
     chip_layers = all_layers // count
 
-    def rank(device):
-        return device % 2 * (count // 2) + device // 2
-
     window = -(-(chip_layers + 2 * APPLICATIONS) // GROUP) * GROUP
     half = local_elems // 2
     swap = [(0, 1), (1, 0)]
@@ -414,22 +434,38 @@
     )
     pieces = [
         lax.dynamic_slice_in_dim(
-            whole, rank(lax.bitwise_xor(mine, k)) * (chip_layers * half), window * half, 1
+            whole, chip_rank(lax.bitwise_xor(mine, k), count) * (chip_layers * half), window * half, 1
         )
         for k in range(count)
     ]
     chunks = exchanged(pieces)
-    across = [over_circle(chunk) for chunk in chunks]
-    beside = [over_core(chunk) for chunk in chunks]
-
-    section = lax.axis_index("space") * local_elems
-    place = jnp.stack(
-        [core, rank(mine) * chip_layers - APPLICATIONS, section, mine, lax.axis_index("group")]
-    ).astype(jnp.int32)
-    edge_one = over_circle(
-        lax.dynamic_index_in_dim(tiles, 6 * core + lax.axis_index("group"), 0, keepdims=False)
-    )
-    edge_two = lax.ppermute(edge_one, "group", swap)
+    rest = tiles.shape[1] - OVER_GROUP
+    edge_one = call(
+        edge_tiles_kernel,
+        held((tiles.shape[1] + rest,) + tiles.shape[2:]),
+        [],
+        [],
+        [tiles],
+    )
+    edge_one = over_circle(edge_one)
+    edge_two = lax.ppermute(edge_one[rest : tiles.shape[1]], "group", swap)
+    def trimmed(parts, later_than):
+        return call(
+            lambda *refs: trim_kernel(len(parts), *refs),
+            held((local_steps * len(parts), (window - 2) * half, width)),
+            [],
+            [],
+            parts,
+            later_than,
+        )
+
+    across = [over_circle(trimmed(chunks[:1], []))]
+    across.append(over_circle(trimmed(chunks[1:], [across[0], edge_one])))
+
+    own = call(
+        gather_kernel, held((steps, window * half, width)), [], [], list(chunks)
+    )
+
     fields = call(
         pack_kernel,
         held((3,) + start_state.shape, jnp.float32),
@@ -438,23 +474,25 @@
         [start_state, reaction, source],
         [pieces[1]],
     )
+    total = local_elems * sections
+    number = local_elems * lax.axis_index("space") + jnp.arange(local_elems, dtype=jnp.int32)
+    wanted = (number[None] + jnp.array(OFFSETS, jnp.int32)[:, None] + total) % total
     ids = neighbors.T
+    slots = 1 + sum(at * (ids[at : at + 1] == wanted).astype(jnp.int32) for at in range(1, 4))
     bundle, bundle_edge = call(
-        fields_kernel,
+        lambda *refs: fields_kernel(count, *refs),
         (
             held((3 * window, local_elems, width), jnp.float32),
             held((3 * window + 3, 2, width), jnp.float32),
         ),
         [],
-        [place],
-        [fields, over_core(fields), self_diag, ids],
+        [],
+        [fields, over_core(fields), self_diag, slots],
         [chunks[1]],
     )
     bundle_edge = over_circle(bundle_edge)
-    edge_ids = bundle_edge[3 * window + 1 :, :, :local_elems].reshape(4, local_elems)
-    where = jnp.concatenate(
-        [jnp.pad(place[None], ((0, 0), (0, local_elems - 5))), ids, edge_ids.astype(jnp.int32)], 0
-    )
+    edge_slots = bundle_edge[3 * window + 1 :, :, :local_elems].reshape(4, local_elems)
+    slots = jnp.concatenate([slots, edge_slots.astype(jnp.int32)], 0)
 
     forward, backward, _ = transform_tables(steps)
     order = np.zeros((4, GROUP, steps, steps, GROUP, 4), np.float32)
@@ -486,42 +524,41 @@
         ]
 
     total = local_elems * sections
-    two_across, four_along = held((2, 6 * width, 2 * width)), held((4, 2 * width, width))
     arrived = pltpu.VMEM((steps, window * half, width), jnp.bfloat16)
-    coef, diag, inverse, ready, inner_across, inner_along = call(
-        lambda *refs: ready_kernel(all_layers, total, count, *refs),
+    laid = (held((4, 6 * width, 2 * width)), held((8, 2 * width, width)))
+    coef, diag, inverse, ready, near_across, near_along, picks = call(
+        lambda *refs: ready_kernel(all_layers, count, *refs),
         (
             held((3, window, 8, width), jnp.float32),
             held((8, width), jnp.float32),
             held((8, 3, window - 2, steps // 2, width), jnp.float32),
             held((12, window, steps, width)),
-            two_across,
-            four_along,
+            *laid,
+            held((32, 8, width), jnp.float32),
         ),
-        [arrived],
-        [where],
-        [constant(order), tiles, bundle, bundle_edge, self_diag, *chunks, *beside],
-    )
-    state, edge, outer_across, outer_along = call(
-        lambda *refs: first_kernel(total, count, *refs),
+        [],
+        [slots],
+        [constant(order), tiles, bundle, bundle_edge, self_diag, own, over_core(own)],
+    )
+    state, edge, *laid = call(
+        lambda *refs: first_kernel(count, *refs),
         (
             held((4, window - 4, steps, width)),
             held((2 * (window - 6) + 2 * (window - 8), steps, width)),
-            two_across,
-            four_along,
+            *laid,
         ),
         [pltpu.VMEM((2,) + tiles.shape[1:], jnp.bfloat16), arrived] + scratch(window),
-        [where],
-        [constant(order), tiles, edge_one, edge_two, coef, diag, inverse, ready, inner_across,
-         inner_along, table(forward, window - 2), table(backward, window - 4), *across],
+        [],
+        [constant(order), coef, diag, inverse, ready, near_across, near_along, picks, edge_one,
+         edge_two, table(forward, window - 2), table(backward, window - 4), *across],
     )
     solved = call(
         lambda *refs: second_kernel(count, *refs),
         held((2, steps // 2, last * half, width)),
         scratch(window - 4) + [pltpu.VMEM((4, last, steps, width), jnp.bfloat16)],
-        [where],
-        [constant(order.T), coef, diag, inverse, outer_across, outer_along, inner_across,
-         inner_along, table(forward, window - 6), table(backward, last),
+        [],
+        [constant(order.T), coef, diag, inverse, *laid,
+         table(forward, window - 6), table(backward, last),
          state, over_core(state), over_circle(edge)],
     )
 
@@ -539,7 +576,7 @@
         lambda *refs: last_kernel(count, *refs),
         held(state_guess.shape, jnp.float32),
         [],
-        [place],
+        [],
         [constant(order_last), *parts],
     )
 

time: 49.1 us -> 44.3 us (0.902)
  waiting for transfers between devices: 18.3 us -> 15.6 us
  Pallas kernels: 9.2 us -> 7.08 us
  local copies, waits for them, and re-layouts: 0.28 us -> 1.7 us
  starting transfers between devices: 19.6 us -> 18.4 us
    ppermute x7 -> x5, waiting for transfers between devices: 9.53 us -> 5.28 us  [over_circle(): return lax.ppermute(array, ('space', 'layer'), circle)]
    pallas_call x6 -> x10, Pallas kernels: 9.2 us -> 7.08 us  [call(): pl.pallas_call(kernel, out_shape=out_shape, in_specs=[pl.BlockSpec(memory...]
    unnamed x26 -> x30, local copies, waits for them, and re-layouts: 0.07 us -> 1.57 us
    ppermute x8 -> x5, starting transfers between devices: 3.18 us -> 1.79 us  [over_core(): return lax.ppermute(array, 'layer', swap)]
    ppermute x1, waiting for transfers between devices: 0.01 us -> 1.31 us  [shards(): edge_two = lax.ppermute(edge_one[rest:tiles.shape[1]], 'group', swap)]
    ppermute x7 -> x5, starting transfers between devices: 7.28 us -> 7.23 us  [over_circle(): return lax.ppermute(array, ('space', 'layer'), circle)]
    ppermute x8 -> x5, waiting for transfers between devices: 2.14 us -> 2.11 us  [over_core(): return lax.ppermute(array, 'layer', swap)]
  transfers between devices with their start and end apart: 21 -> 16, of which waited for: 10 -> 9; matrix products, arithmetic and copies ran while one was open for 0% -> 0% of each run, Pallas kernels for 4% -> 4%
where the time goes in v4:
time: 44.3 us; the launch traced here: 44.1 us
  starting transfers between devices  18.4 us (42%)
  waiting for transfers between devices  15.6 us (35%)
  Pallas kernels  7.08 us (16%)
  local copies, waits for them, and re-layouts  1.7 us (4%)
  other arithmetic  1.13 us (3%)
    ppermute x5, starting transfers between devices, over_circle(): return lax.ppermute(array, ('space', 'layer'), circle)  7.23 us
    pallas_call x10, Pallas kernels, call(): pl.pallas_call(kernel, out_shape=out_shape, in_specs=[pl.BlockSpec(memory...  7.08 us
    ppermute x5, waiting for transfers between devices, over_circle(): return lax.ppermute(array, ('space', 'layer'), circle)  5.28 us
    ppermute x2, starting transfers between devices, shards(): lax.ppermute(jnp.stack([keep[cut], got[cut]]), ('tm', 'layer'), pairs)  4.39 us
    ppermute x3, waiting for transfers between devices, exchanged(): lax.ppermute(parts[k], 'tm', [(i, i ^ k) for i in range(count)])  3.77 us
    ppermute x3, starting transfers between devices, exchanged(): lax.ppermute(parts[k], 'tm', [(i, i ^ k) for i in range(count)])  3.67 us
    ppermute x2, waiting for transfers between devices, shards(): lax.ppermute(jnp.stack([keep[cut], got[cut]]), ('tm', 'layer'), pairs)  3.09 us
    ppermute x5, waiting for transfers between devices, over_core(): return lax.ppermute(array, 'layer', swap)  2.11 us
  transfers between devices with their start and end apart: 16, of which 9 were waited for; matrix products, arithmetic and copies ran while one was open for 0% of the time, Pallas kernels for 4%

profile of v4, /device:TPU:1, one launch (start us, length us, event | category | flops | bytes accessed | tf_op | source)
XLA Modules:
  0.0 44.1 jit_solution(10151685444849900393)
XLA Ops:
  0.0 1.0 %convert_element_type.15 = bf16[4,16,8,128]{3,2,1,0:T(8,128)(2,1)S(1)} convert(f32[4,16,8,128]{3,2,1,0:T(8,128)} %param.16) | non-fusion elementwise | flops 65536 | bytes 393216 | tf_op jit(solution)/shard_map/convert_element_type | solution.py:423
  1.0 0.1 constant_dynamic-slice_fusion.5
  1.1 0.1 collective-permute-start
  1.2 1.5 %copy-done = bf16[8,7,128,128]{3,2,1,0:T(8,128)(2,1)S(1)} copy-done((bf16[8,7,128,128]{3,2,1,0:T(8,128)(2,1)S(1)}, bf16[8,7,128,128]{3,2,1,0:T(8,128)(2,1)}, u32[]{:S(2)}) %copy-start) | copy-done | bytes 1835032
  2.7 0.0 copy-start.12
  2.7 2.6 %collective-permute-start.7 = (bf16[11,128,128]{2,1,0:T(8,128)(2,1)S(1)}, bf16[11,128,128]{2,1,0:T(8,128)(2,1)S(1)}, u32[]{:S(2)}, u32[]{:S(2)}) collective-permute-start(bf16[11,128,128]{2,1,0:T(8,128)(2,1)S(1)} %shard_map.158), channel_id=1, source_target_pairs={{1,2},{2,1},{3,0},{0,3},{5,6},{6,5},{7,4},{4,7},{9,10},{10,9},{11,... | collective-permute-start | bytes 1081352 | tf_op jit(solution)/shard_map/ppermute | solution.py:412
  5.4 0.0 collective-permute-done
  5.4 0.0 copy-start.1
  5.5 0.0 copy-start.2
  5.5 1.4 %collective-permute-start.2 = (bf16[4,64,128]{2,1,0:T(8,128)(2,1)S(1)}, bf16[4,64,128]{2,1,0:T(8,128)(2,1)S(1)}, u32[]{:S(2)}, u32[]{:S(2)}) collective-permute-start(bf16[4,64,128]{2,1,0:T(8,128)(2,1)S(1)} %get-tuple-element.34._), channel_id=1, source_target_pairs={{0,4},{4,0},{8,12},{12,8},{1,5},{5,1},{9,13},{13,9},{2,6},{6,2},{1... | collective-permute-start | bytes 196616 | tf_op jit(solution)/shard_map/ppermute | solution.py:416
  6.9 1.0 %collective-permute-start.9 = (bf16[4,56,128]{2,1,0:T(8,128)(2,1)S(1)}, bf16[4,56,128]{2,1,0:T(8,128)(2,1)S(1)}, u32[]{:S(2)}, u32[]{:S(2)}) collective-permute-start(bf16[4,56,128]{2,1,0:T(8,128)(2,1)S(1)} %shard_map.159), channel_id=1, source_target_pairs={{1,2},{2,1},{3,0},{0,3},{5,6},{6,5},{7,4},{4,7},{9,10},{10,9},{11,... | collective-permute-start | bytes 172040 | tf_op jit(solution)/shard_map/ppermute | solution.py:412
  7.9 2.2 %collective-permute-start.5 = (bf16[4,64,128]{2,1,0:T(8,128)(2,1)S(1)}, bf16[4,64,128]{2,1,0:T(8,128)(2,1)S(1)}, u32[]{:S(2)}, u32[]{:S(2)}) collective-permute-start(bf16[4,64,128]{2,1,0:T(8,128)(2,1)S(1)} %get-tuple-element.31), channel_id=1, source_target_pairs={{0,12},{4,8},{8,4},{12,0},{1,13},{5,9},{9,5},{13,1},{2,14},{6,10},... | collective-permute-start | bytes 196616 | tf_op jit(solution)/shard_map/ppermute | solution.py:416
  10.1 0.1 collective-permute-start.4
  10.2 0.0 collective-permute-done.2.refs_4_.rest_1_.refs_0_
  10.2 0.4 collective-permute-start.1
  10.6 0.1 add_add_fusion.refs_3_
  10.7 1.1 %collective-permute-done.1.refs_1_ = f32[3,16,8,128]{3,2,1,0:T(8,128)S(1)} collective-permute-done((f32[3,16,8,128]{3,2,1,0:T(8,128)S(1)}, f32[3,16,8,128]{3,2,1,0:T(8,128)S(1)}, u32[]{:S(2)}, u32[]{:S(2)}) %collective-permute-start.1) | collective-permute-done | bytes 196640 | tf_op jit(solution)/shard_map/ppermute | solution.py:409
  11.7 0.1 shard_map.155
  11.8 1.3 %collective-permute-start.3 = (f32[51,2,128]{2,1,0:T(2,128)S(1)}, f32[51,2,128]{2,1,0:T(2,128)S(1)}, u32[]{:S(2)}, u32[]{:S(2)}) collective-permute-start(f32[51,2,128]{2,1,0:T(2,128)S(1)} %get-tuple-element.18), channel_id=1, source_target_pairs={{1,2},{2,1},{3,0},{0,3},{5,6},{6,5},{7,4},{4,7},{9,10},{10,9},{11,... | collective-permute-start | bytes 156680 | tf_op jit(solution)/shard_map/ppermute | solution.py:412
  13.1 0.4 collective-permute-done.5.rest_3_.refs_2_
  13.5 3.4 %collective-permute-done.4.rest_2_.refs_1_ = bf16[4,64,128]{2,1,0:T(8,128)(2,1)S(1)} collective-permute-done((bf16[4,64,128]{2,1,0:T(8,128)(2,1)S(1)}, bf16[4,64,128]{2,1,0:T(8,128)(2,1)S(1)}, u32[]{:S(2)}, u32[]{:S(2)}) %collective-permute-start.4) | collective-permute-done | bytes 65568 | tf_op jit(solution)/shard_map/ppermute | solution.py:416
  16.9 0.6 %collective-permute-start.6 = (bf16[16,64,128]{2,1,0:T(8,128)(2,1)S(1)}, bf16[16,64,128]{2,1,0:T(8,128)(2,1)S(1)}, u32[]{:S(2)}, u32[]{:S(2)}) collective-permute-start(bf16[16,64,128]{2,1,0:T(8,128)(2,1)S(1)} %shard_map.156.refs_6_), channel_id=1, source_target_pairs={{0,1},{1,0},{2,3},{3,2},{4,5},{5,4},{6,7},{7,6},{8,9},{9,8},{10,11... | collective-permute-start | bytes 786440 | tf_op jit(solution)/shard_map/ppermute | solution.py:409
  17.5 0.0 collective-permute-done.9.refs_3_.refs_12_
  17.5 0.0 collective-permute-done.7.refs_4_.refs_8_
  17.5 0.1 shard_map.160
  17.6 0.0 copy-start.5
  17.6 0.0 copy-start.6
  17.6 1.1 %collective-permute-start.10 = (bf16[12,56,128]{2,1,0:T(8,128)(2,1)S(1)}, bf16[12,56,128]{2,1,0:T(8,128)(2,1)S(1)}, u32[]{:S(2)}, u32[]{:S(2)}) collective-permute-start(bf16[12,56,128]{2,1,0:T(8,128)(2,1)S(1)} %shard_map.160), channel_id=1, source_target_pairs={{1,2},{2,1},{3,0},{0,3},{5,6},{6,5},{7,4},{4,7},{9,10},{10,9},{11,... | collective-permute-start | bytes 516104 | tf_op jit(solution)/shard_map/ppermute | solution.py:412
  18.8 0.0 collective-permute-done.3.refs_4_
  18.8 1.3 %collective-permute-start.8 = (bf16[3,128,128]{2,1,0:T(8,128)(2,1)S(1)}, bf16[3,128,128]{2,1,0:T(8,128)(2,1)S(1)}, u32[]{:S(2)}, u32[]{:S(2)}) collective-permute-start(bf16[3,128,128]{2,1,0:T(8,128)(2,1)S(1)} %slice.46), channel_id=1, source_target_pairs={{0,16},{16,0},{1,17},{17,1},{2,18},{18,2},{3,19},{19,3},{4,20},{20... | collective-permute-start | bytes 294920 | tf_op jit(solution)/shard_map/ppermute | solution.py:451
  20.1 0.0 collective-permute-done.6.refs_7_
  20.1 1.4 %shard_map.157 = (f32[3,16,8,128]{3,2,1,0:T(8,128)S(1)}, f32[8,128]{1,0:T(8,128)S(1)}, f32[8,3,14,8,128]{4,3,2,1,0:T(8,128)S(1)}, bf16[12,16,16,128]{3,2,1,0:T(8...) custom-call(s32[8,8]{1,0:T(8,128)S(1)} %pad_add_fusion.refs_0_, ...), custom_call_target="tpu_custom_call" | custom-call | tf_op jit(solution)/shard_map/pallas_call | solution.py:379
  21.6 1.3 %collective-permute-done.8.refs_9_ = bf16[3,128,128]{2,1,0:T(8,128)(2,1)S(1)} collective-permute-done((bf16[3,128,128]{2,1,0:T(8,128)(2,1)S(1)}, bf16[3,128,128]{2,1,0:T(8,128)(2,1)S(1)}, u32[]{:S(2)}, u32[]{:S(2)}) %collective-permute-start.8) | collective-permute-done | bytes 98336 | tf_op jit(solution)/shard_map/ppermute | solution.py:451
  22.9 0.8 %collective-permute-done.10.refs_13_ = bf16[12,56,128]{2,1,0:T(8,128)(2,1)S(1)} collective-permute-done((bf16[12,56,128]{2,1,0:T(8,128)(2,1)S(1)}, bf16[12,56,128]{2,1,0:T(8,128)(2,1)S(1)}, u32[]{:S(2)}, u32[]{:S(2)}) %collective-permute-start.10) | collective-permute-done | bytes 172064 | tf_op jit(solution)/shard_map/ppermute | solution.py:412
  23.7 0.0 copy-start.11
  23.7 2.5 %shard_map.161 = (bf16[4,12,16,128]{3,2,1,0:T(8,128)(2,1)S(1)}, bf16[36,16,128]{2,1,0:T(8,128)(2,1)S(1)}, bf16[4,768,256]{2,1,0:T(8,128)(2,1)S(1)}, bf16[8,256,128]{2,1,0:T(8,128)(2,1)S(1)}) custom-call(bf16[256,256]{1,0:T(8,128)(2,1)S(1)} %copy-done.2, f32[3,16,8,128]{3,2,1,0:T(8,128)S(1)} %get-tuple-element.20.refs_1_, ...), custom_call_target="tpu_custom_call" | custom-call | tf_op jit(solution)/shard_map/pallas_call | solution.py:379
  26.3 0.4 %collective-permute-start.11 = (bf16[4,12,16,128]{3,2,1,0:T(8,128)(2,1)S(1)}, bf16[4,12,16,128]{3,2,1,0:T(8,128)(2,1)S(1)}, u32[]{:S(2)}, u32[]{:S(2)}) collective-permute-start(bf16[4,12,16,128]{3,2,1,0:T(8,128)(2,1)S(1)} %get-tuple-element.29.refs_8_), channel_id=1, source_target_pairs={{0,1},{1,0},{2,3},{3,2},{4,5},{5,4},{6,7},{7,6},{8,9},{9,8},{10,11... | collective-permute-start | bytes 589832 | tf_op jit(solution)/shard_map/ppermute | solution.py:409
  26.7 1.2 %collective-permute-start.12 = (bf16[36,16,128]{2,1,0:T(8,128)(2,1)S(1)}, bf16[36,16,128]{2,1,0:T(8,128)(2,1)S(1)}, u32[]{:S(2)}, u32[]{:S(2)}) collective-permute-start(bf16[36,16,128]{2,1,0:T(8,128)(2,1)S(1)} %get-tuple-element.30), channel_id=1, source_target_pairs={{1,2},{2,1},{3,0},{0,3},{5,6},{6,5},{7,4},{4,7},{9,10},{10,9},{11,... | collective-permute-start | bytes 442376 | tf_op jit(solution)/shard_map/ppermute | solution.py:412
  27.9 4.4 %collective-permute-done.12.refs_10_ = bf16[36,16,128]{2,1,0:T(8,128)(2,1)S(1)} collective-permute-done((bf16[36,16,128]{2,1,0:T(8,128)(2,1)S(1)}, bf16[36,16,128]{2,1,0:T(8,128)(2,1)S(1)}, u32[]{:S(2)}, u32[]{:S(2)}) %collective-permute-start.12) | collective-permute-done | bytes 147488 | tf_op jit(solution)/shard_map/ppermute | solution.py:412
  32.4 0.0 copy-start.3
  32.4 1.9 %shard_map.162 = bf16[2,8,32,128]{3,2,1,0:T(8,128)(2,1)S(1)} custom-call(bf16[256,256]{1,0:T(8,128)(2,1)S(1)} %copy-done.4, f32[3,16,8,128]{3,2,1,0:T(8,128)S(1)} %get-tuple-element.20.refs_1_, f32[8,128]{1,0:T(8,128)S(1)} %get-tuple-element.21.refs_2_, f32[8,3,14,8,128]{4,3,2,1,0:T(8,128)S(1)} %get-tuple-element.22.refs_3_, ...), custom_call_target="tpu_custom_call" | custom-call | tf_op jit(solution)/shard_map/pallas_call | solution.py:379
  34.3 0.3 collective-permute-start.13
  34.6 1.0 %collective-permute-done.13 = bf16[8,32,128]{2,1,0:T(8,128)(2,1)S(1)} collective-permute-done((bf16[8,32,128]{2,1,0:T(8,128)(2,1)S(1)}, bf16[8,32,128]{2,1,0:T(8,128)(2,1)S(1)}, u32[]{:S(2)}, u32[]{:S(2)}) %collective-permute-start.13) | collective-permute-done | bytes 65568 | tf_op jit(solution)/shard_map/ppermute | solution.py:409
  35.7 1.9 %collective-permute-start.14 = (bf16[2,4,32,128]{3,2,1,0:T(8,128)(2,1)S(1)}, bf16[2,4,32,128]{3,2,1,0:T(8,128)(2,1)S(1)}, u32[]{:S(2)}, u32[]{:S(2)}) collective-permute-start(bf16[2,4,32,128]{3,2,1,0:T(8,128)(2,1)S(1)} %pad_maximum_fusion.1), channel_id=1, source_target_pairs={{0,0},{1,4},{4,1},{5,5},{8,8},{9,12},{12,9},{13,13},{2,2},{3,6},{6... | collective-permute-start | bytes 196616 | tf_op jit(solution)/shard_map/ppermute | solution.py:574
  37.6 2.5 %collective-permute-start.15 = (bf16[2,4,32,128]{3,2,1,0:T(8,128)(2,1)S(1)}, bf16[2,4,32,128]{3,2,1,0:T(8,128)(2,1)S(1)}, u32[]{:S(2)}, u32[]{:S(2)}) collective-permute-start(bf16[2,4,32,128]{3,2,1,0:T(8,128)(2,1)S(1)} %pad_maximum_fusion.2), channel_id=1, source_target_pairs={{0,8},{1,12},{4,9},{5,13},{8,0},{9,4},{12,1},{13,5},{2,10},{3,14},... | collective-permute-start | bytes 196616 | tf_op jit(solution)/shard_map/ppermute | solution.py:574
  40.1 1.8 %collective-permute-done.14.refs_1_ = bf16[2,4,32,128]{3,2,1,0:T(8,128)(2,1)S(1)} collective-permute-done((bf16[2,4,32,128]{3,2,1,0:T(8,128)(2,1)S(1)}, bf16[2,4,32,128]{3,2,1,0:T(8,128)(2,1)S(1)}, u32[]{:S(2)}, u32[]{:S(2)}) %collective-permute-start.14) | collective-permute-done | bytes 65568 | tf_op jit(solution)/shard_map/ppermute | solution.py:574
  41.8 1.3 %collective-permute-done.15.refs_2_ = bf16[2,4,32,128]{3,2,1,0:T(8,128)(2,1)S(1)} collective-permute-done((bf16[2,4,32,128]{3,2,1,0:T(8,128)(2,1)S(1)}, bf16[2,4,32,128]{3,2,1,0:T(8,128)(2,1)S(1)}, u32[]{:S(2)}, u32[]{:S(2)}) %collective-permute-start.15) | collective-permute-done | bytes 65568 | tf_op jit(solution)/shard_map/ppermute | solution.py:574
  43.2 0.9 %shard_map.163 = f32[4,16,8,128]{3,2,1,0:T(8,128)} custom-call(bf16[256,256]{1,0:T(8,128)(2,1)S(1)} %copy-done.3, bf16[2,4,32,128]{3,2,1,0:T(8,128)(2,1)S(1)} %collective-permute-done.14.refs_1_, bf16[2,4,32,128]{3,2,1,0:T(8,128)(2,1)S(1)} %collective-permute-done.15.refs_2_), custom_call_target="tpu_custom_call" | custom-call | tf_op jit(solution)/shard_map/pallas_call | solution.py:379
  (41 shorter events, 0.3 us)
Async XLA Ops:
  0.0 5.4 %copy-start.13 = (s32[8,4]{0,1:T(4,128)S(1)}, s32[8,4]{0,1:T(4,128)}, u32[]{:S(2)}) copy-start(s32[8,4]{0,1:T(4,128)} %param.22) | copy-start | bytes 388
  1.1 4.3 %collective-permute-start = (bf16[4,64,128]{2,1,0:T(8,128)(2,1)S(1)}, bf16[4,64,128]{2,1,0:T(8,128)(2,1)S(1)}, u32[]{:S(2)}, u32[]{:S(2)}) collective-permute-start(bf16[4,64,128]{2,1,0:T(8,128)(2,1)S(1)} %bitcast.23), channel_id=1, source_target_pairs={{0,1},{1,0},{2,3},{3,2},{4,5},{5,4},{6,7},{7,6},{8,9},{9,8},{10,11... | collective-permute-start | bytes 196616 | tf_op jit(solution)/shard_map/ppermute | solution.py:409
  1.2 1.5 %copy-start = (bf16[8,7,128,128]{3,2,1,0:T(8,128)(2,1)S(1)}, bf16[8,7,128,128]{3,2,1,0:T(8,128)(2,1)}, u32[]{:S(2)}) copy-start(bf16[8,7,128,128]{3,2,1,0:T(8,128)(2,1)} %tiles.1) | copy-start | bytes 5505028
  2.7 7.5 %copy-start.8 = (f32[16,8,128]{2,1,0:T(8,128)S(1)}, f32[16,8,128]{2,1,0:T(8,128)}, u32[]{:S(2)}) copy-start(f32[16,8,128]{2,1,0:T(8,128)} %start.1) | copy-start | bytes 196612
  2.7 7.5 %copy-start.9 = (f32[16,8,128]{2,1,0:T(8,128)S(1)}, f32[16,8,128]{2,1,0:T(8,128)}, u32[]{:S(2)}) copy-start(f32[16,8,128]{2,1,0:T(8,128)} %reaction.1) | copy-start | bytes 196612
  2.7 7.5 %copy-start.10 = (f32[16,8,128]{2,1,0:T(8,128)S(1)}, f32[16,8,128]{2,1,0:T(8,128)}, u32[]{:S(2)}) copy-start(f32[16,8,128]{2,1,0:T(8,128)} %source.1) | copy-start | bytes 196612
  2.7 7.9 %copy-start.14 = (s32[4]{0:T(128)S(1)}, s32[4]{0:T(128)}, u32[]{:S(2)}) copy-start(s32[4]{0:T(128)} %constant.123.clone) | copy-start | bytes 52
  2.7 9.0 %copy-start.12 = (f32[8,128]{1,0:T(8,128)S(1)}, f32[8,128]{1,0:T(8,128)}, u32[]{:S(2)}) copy-start(f32[8,128]{1,0:T(8,128)} %refs_5_.1) | copy-start | bytes 12292
  2.7 14.8 %collective-permute-start.7 = (bf16[11,128,128]{2,1,0:T(8,128)(2,1)S(1)}, bf16[11,128,128]{2,1,0:T(8,128)(2,1)S(1)}, u32[]{:S(2)}, u32[]{:S(2)}) collective-permute-start(bf16[11,128,128]{2,1,0:T(8,128)(2,1)S(1)} %shard_map.158), channel_id=1, source_target_pairs={{1,2},{2,1},{3,0},{0,3},{5,6},{6,5},{7,4},{4,7},{9,10},{10,9},{11,... | collective-permute-start | bytes 1081352 | tf_op jit(solution)/shard_map/ppermute | solution.py:412
  5.4 14.7 %copy-start.1 = (bf16[8,7,128,128]{3,2,1,0:T(8,128)(2,1)S(1)}, bf16[8,7,128,128]{3,2,1,0:T(8,128)(2,1)}, u32[]{:S(2)}) copy-start(bf16[8,7,128,128]{3,2,1,0:T(8,128)(2,1)} %tiles.1) | copy-start | bytes 5505028
  5.5 14.7 %copy-start.2 = (bf16[256,256]{1,0:T(8,128)(2,1)S(1)}, bf16[256,256]{1,0:T(8,128)(2,1)}, u32[]{:S(2)}) copy-start(bf16[256,256]{1,0:T(8,128)(2,1)} %constant.124.clone.refs_1_.refs_0_) | copy-start | bytes 393220
  5.5 4.7 %collective-permute-start.2 = (bf16[4,64,128]{2,1,0:T(8,128)(2,1)S(1)}, bf16[4,64,128]{2,1,0:T(8,128)(2,1)S(1)}, u32[]{:S(2)}, u32[]{:S(2)}) collective-permute-start(bf16[4,64,128]{2,1,0:T(8,128)(2,1)S(1)} %get-tuple-element.34._), channel_id=1, source_target_pairs={{0,4},{4,0},{8,12},{12,8},{1,5},{5,1},{9,13},{13,9},{2,6},{6,2},{1... | collective-permute-start | bytes 196616 | tf_op jit(solution)/shard_map/ppermute | solution.py:416
  6.9 10.6 %collective-permute-start.9 = (bf16[4,56,128]{2,1,0:T(8,128)(2,1)S(1)}, bf16[4,56,128]{2,1,0:T(8,128)(2,1)S(1)}, u32[]{:S(2)}, u32[]{:S(2)}) collective-permute-start(bf16[4,56,128]{2,1,0:T(8,128)(2,1)S(1)} %shard_map.159), channel_id=1, source_target_pairs={{1,2},{2,1},{3,0},{0,3},{5,6},{6,5},{7,4},{4,7},{9,10},{10,9},{11,... | collective-permute-start | bytes 172040 | tf_op jit(solution)/shard_map/ppermute | solution.py:412
  7.9 5.6 %collective-permute-start.5 = (bf16[4,64,128]{2,1,0:T(8,128)(2,1)S(1)}, bf16[4,64,128]{2,1,0:T(8,128)(2,1)S(1)}, u32[]{:S(2)}, u32[]{:S(2)}) collective-permute-start(bf16[4,64,128]{2,1,0:T(8,128)(2,1)S(1)} %get-tuple-element.31), channel_id=1, source_target_pairs={{0,12},{4,8},{8,4},{12,0},{1,13},{5,9},{9,5},{13,1},{2,14},{6,10},... | collective-permute-start | bytes 196616 | tf_op jit(solution)/shard_map/ppermute | solution.py:416
  10.1 6.9 %collective-permute-start.4 = (bf16[4,64,128]{2,1,0:T(8,128)(2,1)S(1)}, bf16[4,64,128]{2,1,0:T(8,128)(2,1)S(1)}, u32[]{:S(2)}, u32[]{:S(2)}) collective-permute-start(bf16[4,64,128]{2,1,0:T(8,128)(2,1)S(1)} %get-tuple-element.32), channel_id=1, source_target_pairs={{0,8},{4,12},{8,0},{12,4},{1,9},{5,13},{9,1},{13,5},{2,10},{6,14},... | collective-permute-start | bytes 196616 | tf_op jit(solution)/shard_map/ppermute | solution.py:416
  10.2 1.5 %collective-permute-start.1 = (f32[3,16,8,128]{3,2,1,0:T(8,128)S(1)}, f32[3,16,8,128]{3,2,1,0:T(8,128)S(1)}, u32[]{:S(2)}, u32[]{:S(2)}) collective-permute-start(f32[3,16,8,128]{3,2,1,0:T(8,128)S(1)} %shard_map.154.refs_0_), channel_id=1, source_target_pairs={{0,1},{1,0},{2,3},{3,2},{4,5},{5,4},{6,7},{7,6},{8,9},{9,8},{10,11... | collective-permute-start | bytes 589832 | tf_op jit(solution)/shard_map/ppermute | solution.py:409
  11.8 6.9 %collective-permute-start.3 = (f32[51,2,128]{2,1,0:T(2,128)S(1)}, f32[51,2,128]{2,1,0:T(2,128)S(1)}, u32[]{:S(2)}, u32[]{:S(2)}) collective-permute-start(f32[51,2,128]{2,1,0:T(2,128)S(1)} %get-tuple-element.18), channel_id=1, source_target_pairs={{1,2},{2,1},{3,0},{0,3},{5,6},{6,5},{7,4},{4,7},{9,10},{10,9},{11,... | collective-permute-start | bytes 156680 | tf_op jit(solution)/shard_map/ppermute | solution.py:412
  16.9 3.2 %collective-permute-start.6 = (bf16[16,64,128]{2,1,0:T(8,128)(2,1)S(1)}, bf16[16,64,128]{2,1,0:T(8,128)(2,1)S(1)}, u32[]{:S(2)}, u32[]{:S(2)}) collective-permute-start(bf16[16,64,128]{2,1,0:T(8,128)(2,1)S(1)} %shard_map.156.refs_6_), channel_id=1, source_target_pairs={{0,1},{1,0},{2,3},{3,2},{4,5},{5,4},{6,7},{7,6},{8,9},{9,8},{10,11... | collective-permute-start | bytes 786440 | tf_op jit(solution)/shard_map/ppermute | solution.py:409
  17.6 6.1 %copy-start.5 = (bf16[224,224]{1,0:T(8,128)(2,1)S(1)}, bf16[224,224]{1,0:T(8,128)(2,1)}, u32[]{:S(2)}) copy-start(bf16[224,224]{1,0:T(8,128)(2,1)} %constant.125.clone.refs_10_) | copy-start | bytes 301060
  17.6 6.1 %copy-start.6 = (bf16[192,192]{1,0:T(8,128)(2,1)S(1)}, bf16[192,192]{1,0:T(8,128)(2,1)}, u32[]{:S(2)}) copy-start(bf16[192,192]{1,0:T(8,128)(2,1)} %constant.126.clone.refs_11_) | copy-start | bytes 221188
  17.6 6.1 %collective-permute-start.10 = (bf16[12,56,128]{2,1,0:T(8,128)(2,1)S(1)}, bf16[12,56,128]{2,1,0:T(8,128)(2,1)S(1)}, u32[]{:S(2)}, u32[]{:S(2)}) collective-permute-start(bf16[12,56,128]{2,1,0:T(8,128)(2,1)S(1)} %shard_map.160), channel_id=1, source_target_pairs={{1,2},{2,1},{3,0},{0,3},{5,6},{6,5},{7,4},{4,7},{9,10},{10,9},{11,... | collective-permute-start | bytes 516104 | tf_op jit(solution)/shard_map/ppermute | solution.py:412
  18.8 4.1 %collective-permute-start.8 = (bf16[3,128,128]{2,1,0:T(8,128)(2,1)S(1)}, bf16[3,128,128]{2,1,0:T(8,128)(2,1)S(1)}, u32[]{:S(2)}, u32[]{:S(2)}) collective-permute-start(bf16[3,128,128]{2,1,0:T(8,128)(2,1)S(1)} %slice.46), channel_id=1, source_target_pairs={{0,16},{16,0},{1,17},{17,1},{2,18},{18,2},{3,19},{19,3},{4,20},{20... | collective-permute-start | bytes 294920 | tf_op jit(solution)/shard_map/ppermute | solution.py:451
  23.7 8.6 %copy-start.4 = (bf16[256,256]{1,0:T(8,128)(2,1)S(1)}, bf16[256,256]{1,0:T(8,128)(2,1)}, u32[]{:S(2)}) copy-start(bf16[256,256]{1,0:T(8,128)(2,1)} %constant.127.clone.refs_0_) | copy-start | bytes 393220
  23.7 8.6 %copy-start.7 = (bf16[160,160]{1,0:T(8,128)(2,1)S(1)}, bf16[160,160]{1,0:T(8,128)(2,1)}, u32[]{:S(2)}) copy-start(bf16[160,160]{1,0:T(8,128)(2,1)} %constant.128.clone.refs_6_) | copy-start | bytes 153604
  23.7 8.6 %copy-start.11 = (bf16[128,128]{1,0:T(8,128)(2,1)S(1)}, bf16[128,128]{1,0:T(8,128)(2,1)}, u32[]{:S(2)}) copy-start(bf16[128,128]{1,0:T(8,128)(2,1)} %constant.129.clone.refs_7_) | copy-start | bytes 98308
  26.3 6.1 %collective-permute-start.11 = (bf16[4,12,16,128]{3,2,1,0:T(8,128)(2,1)S(1)}, bf16[4,12,16,128]{3,2,1,0:T(8,128)(2,1)S(1)}, u32[]{:S(2)}, u32[]{:S(2)}) collective-permute-start(bf16[4,12,16,128]{3,2,1,0:T(8,128)(2,1)S(1)} %get-tuple-element.29.refs_8_), channel_id=1, source_target_pairs={{0,1},{1,0},{2,3},{3,2},{4,5},{5,4},{6,7},{7,6},{8,9},{9,8},{10,11... | collective-permute-start | bytes 589832 | tf_op jit(solution)/shard_map/ppermute | solution.py:409
  26.7 5.6 %collective-permute-start.12 = (bf16[36,16,128]{2,1,0:T(8,128)(2,1)S(1)}, bf16[36,16,128]{2,1,0:T(8,128)(2,1)S(1)}, u32[]{:S(2)}, u32[]{:S(2)}) collective-permute-start(bf16[36,16,128]{2,1,0:T(8,128)(2,1)S(1)} %get-tuple-element.30), channel_id=1, source_target_pairs={{1,2},{2,1},{3,0},{0,3},{5,6},{6,5},{7,4},{4,7},{9,10},{10,9},{11,... | collective-permute-start | bytes 442376 | tf_op jit(solution)/shard_map/ppermute | solution.py:412
  32.4 10.8 %copy-start.3 = (bf16[256,256]{1,0:T(8,128)(2,1)S(1)}, bf16[256,256]{1,0:T(8,128)(2,1)}, u32[]{:S(2)}) copy-start(bf16[256,256]{1,0:T(8,128)(2,1)} %constant.130.clone.refs_0_) | copy-start | bytes 393220
  34.3 1.3 %collective-permute-start.13 = (bf16[8,32,128]{2,1,0:T(8,128)(2,1)S(1)}, bf16[8,32,128]{2,1,0:T(8,128)(2,1)S(1)}, u32[]{:S(2)}, u32[]{:S(2)}) collective-permute-start(bf16[8,32,128]{2,1,0:T(8,128)(2,1)S(1)} %slice_bitcast_fusion), channel_id=1, source_target_pairs={{0,1},{1,0},{2,3},{3,2},{4,5},{5,4},{6,7},{7,6},{8,9},{9,8},{10,11... | collective-permute-start | bytes 196616 | tf_op jit(solution)/shard_map/ppermute | solution.py:409
  35.7 6.2 %collective-permute-start.14 = (bf16[2,4,32,128]{3,2,1,0:T(8,128)(2,1)S(1)}, bf16[2,4,32,128]{3,2,1,0:T(8,128)(2,1)S(1)}, u32[]{:S(2)}, u32[]{:S(2)}) collective-permute-start(bf16[2,4,32,128]{3,2,1,0:T(8,128)(2,1)S(1)} %pad_maximum_fusion.1), channel_id=1, source_target_pairs={{0,0},{1,4},{4,1},{5,5},{8,8},{9,12},{12,9},{13,13},{2,2},{3,6},{6... | collective-permute-start | bytes 196616 | tf_op jit(solution)/shard_map/ppermute | solution.py:574
  37.6 5.6 %collective-permute-start.15 = (bf16[2,4,32,128]{3,2,1,0:T(8,128)(2,1)S(1)}, bf16[2,4,32,128]{3,2,1,0:T(8,128)(2,1)S(1)}, u32[]{:S(2)}, u32[]{:S(2)}) collective-permute-start(bf16[2,4,32,128]{3,2,1,0:T(8,128)(2,1)S(1)} %pad_maximum_fusion.2), channel_id=1, source_target_pairs={{0,8},{1,12},{4,9},{5,13},{8,0},{9,4},{12,1},{13,5},{2,10},{3,14},... | collective-permute-start | bytes 196616 | tf_op jit(solution)/shard_map/ppermute | solution.py:574

commit v5 on v4

--- a/solution.py
+++ b/solution.py
@@ -225,10 +225,10 @@
 
 
 def edge_tiles_kernel(tiles, out):
-    at, group = 6 * lax.axis_index("layer"), lax.axis_index("group")
+    group = lax.axis_index("group")
     count = tiles.shape[1]
-    out[:count] = tiles[at + group]
-    out[count:] = tiles[at + 1 - group, : out.shape[0] - count]
+    out[:count] = tiles[group]
+    out[count:] = tiles[1 - group, : out.shape[0] - count]
 
 
 def ready_kernel(all_layers, count, slots, order, tiles, bundle, bundle_edge, diag_own, own, beside,
@@ -283,6 +283,12 @@
                 picks[4 * (4 * k + at) + slot] = jnp.full((8, width), hit, jnp.float32)
 
 
+def joined(outer, every, each):
+    inner = [every.at[k] for k in range(each, 3 * each)]
+    outer = [outer.at[k] for k in range(2 * each)]
+    return outer[:each] + inner + outer[each:]
+
+
 def first_kernel(count, order, coef, diag, inverse, ready, near_across, near_along, picks, edge_one,
                  edge_two, forward, backward, first, others, out, message, across, along, edge_tiles,
                  arrived, values, packed, spec):
@@ -291,8 +297,8 @@
     edge_tiles[group] = edge_one[0:7]
     edge_tiles[1 - group, 0:rest] = edge_one[7 : 7 + rest]
     edge_tiles[1 - group, rest:7] = edge_two[...]
-    across[...] = near_across[...]
-    along[...] = near_along[...]
+    across[1 - core] = near_across[3 - 3 * core]
+    along[pl.ds(2 - 2 * core, 2)] = near_along[pl.ds(6 - 6 * core, 2)]
 
     def weights_of(element):
         blocks = [edge_tiles[element, 0]]
@@ -304,7 +310,7 @@
             blocks.append(block)
         return blocks + [edge_tiles[element, 5], edge_tiles[element, 6]]
 
-    lay_tiles(weights_of, 0, across, along, 3 * core, 6 * core)
+    lay_tiles(weights_of, 0, across, along, core, 2 * core)
     values[4:8] = ready[4:8]
     values[pl.ds(8 - 8 * core, 4)] = ready[pl.ds(8 - 8 * core, 4)]
     steps, rows, width = arrived.shape
@@ -319,8 +325,8 @@
     def write(element, state):
         out[element] = state
 
-    newton(values, [across.at[k] for k in range(4)], [along.at[k] for k in range(8)], coef, diag,
-           inverse, forward, backward, packed, spec, 0, write)
+    newton(values, joined(across, near_across, 1), joined(along, near_along, 2), coef, diag, inverse,
+           forward, backward, packed, spec, 0, write)
     layers = out.shape[1]
     for at in range(2):
         message[at * (layers - 2) : (at + 1) * (layers - 2)] = out[2 * core + at, 1 : layers - 1]
@@ -328,8 +334,8 @@
         message[begin : begin + layers - 4] = out[2 - 2 * core + at, 2 : layers - 2]
 
 
-def second_kernel(count, order, coef, diag, inverse, across, along, forward, backward, own, beside,
-                  far, out, values, packed, spec, solved):
+def second_kernel(count, order, coef, diag, inverse, across, along, near_across, near_along,
+                  forward, backward, own, beside, far, out, values, packed, spec, solved):
     core, mine = lax.axis_index("layer"), lax.axis_index("tm")
     layers, steps, width = own.shape[1:]
     values[4:8] = own[...]
@@ -344,8 +350,8 @@
     def write(element, state):
         solved[element] = state
 
-    newton(values, [across.at[k] for k in range(4)], [along.at[k] for k in range(8)], coef, diag,
-           inverse, forward, backward, packed, spec, 2, write)
+    newton(values, joined(across, near_across, 1), joined(along, near_along, 2), coef, diag, inverse,
+           forward, backward, packed, spec, 2, write)
     size = steps * GROUP * 4
     local = steps // count
     for group in range(solved.shape[1] // GROUP):
@@ -445,7 +451,7 @@
         held((tiles.shape[1] + rest,) + tiles.shape[2:]),
         [],
         [],
-        [tiles],
+        [lax.dynamic_slice_in_dim(tiles, 6 * core, 2, 0)],
     )
     edge_one = over_circle(edge_one)
     edge_two = lax.ppermute(edge_one[rest : tiles.shape[1]], "group", swap)
@@ -540,12 +546,13 @@
         [slots],
         [constant(order), tiles, bundle, bundle_edge, self_diag, own, over_core(own)],
     )
-    state, edge, *laid = call(
+    state, edge, *outer = call(
         lambda *refs: first_kernel(count, *refs),
         (
             held((4, window - 4, steps, width)),
             held((2 * (window - 6) + 2 * (window - 8), steps, width)),
-            *laid,
+            held((2, 6 * width, 2 * width)),
+            held((4, 2 * width, width)),
         ),
         [pltpu.VMEM((2,) + tiles.shape[1:], jnp.bfloat16), arrived] + scratch(window),
         [],
@@ -557,7 +564,7 @@
         held((2, steps // 2, last * half, width)),
         scratch(window - 4) + [pltpu.VMEM((4, last, steps, width), jnp.bfloat16)],
         [],
-        [constant(order.T), coef, diag, inverse, *laid,
+        [constant(order.T), coef, diag, inverse, *outer, near_across, near_along,
          table(forward, window - 6), table(backward, last),
          state, over_core(state), over_circle(edge)],
     )

time: 44.3 us -> 43.8 us (0.989)
    unnamed x30 -> x28, local copies, waits for them, and re-layouts: 1.57 us -> 0.08 us
    dynamic_slice x0 -> x1, local copies, waits for them, and re-layouts: none -> 1.08 us  [shards(): lax.dynamic_slice_in_dim(tiles, 6 * core, 2, 0)]
  transfers between devices with their start and end apart: 16 -> 16, of which waited for: 9 -> 9; matrix products, arithmetic and copies ran while one was open for 0% -> 3% of each run, Pallas kernels for 4% -> 4%
where the time goes in v5:
time: 43.8 us; the launch traced here: 43.6 us
  starting transfers between devices  18.4 us (42%)
  waiting for transfers between devices  15.6 us (36%)
  Pallas kernels  7.01 us (16%)
  local copies, waits for them, and re-layouts  1.28 us (3%)
  other arithmetic  1.13 us (3%)
    ppermute x5, starting transfers between devices, over_circle(): return lax.ppermute(array, ('space', 'layer'), circle)  7.24 us
    pallas_call x10, Pallas kernels, call(): pl.pallas_call(kernel, out_shape=out_shape, in_specs=[pl.BlockSpec(memory...  7.01 us
    ppermute x5, waiting for transfers between devices, over_circle(): return lax.ppermute(array, ('space', 'layer'), circle)  5.27 us
    ppermute x2, starting transfers between devices, shards(): lax.ppermute(jnp.stack([keep[cut], got[cut]]), ('tm', 'layer'), pairs)  4.38 us
    ppermute x3, waiting for transfers between devices, exchanged(): lax.ppermute(parts[k], 'tm', [(i, i ^ k) for i in range(count)])  3.77 us
    ppermute x3, starting transfers between devices, exchanged(): lax.ppermute(parts[k], 'tm', [(i, i ^ k) for i in range(count)])  3.67 us
    ppermute x2, waiting for transfers between devices, shards(): lax.ppermute(jnp.stack([keep[cut], got[cut]]), ('tm', 'layer'), pairs)  3.1 us
    ppermute x5, waiting for transfers between devices, over_core(): return lax.ppermute(array, 'layer', swap)  2.1 us
  transfers between devices with their start and end apart: 16, of which 9 were waited for; matrix products, arithmetic and copies ran while one was open for 3% of the time, Pallas kernels for 4%

profile of v5, /device:TPU:1, one launch (start us, length us, event | category | flops | bytes accessed | tf_op | source)
XLA Modules:
  0.0 43.6 jit_solution(9827614549327203893)
XLA Ops:
  0.0 1.0 %convert_element_type.15 = bf16[4,16,8,128]{3,2,1,0:T(8,128)(2,1)S(1)} convert(f32[4,16,8,128]{3,2,1,0:T(8,128)} %param.16) | non-fusion elementwise | flops 65536 | bytes 393216 | tf_op jit(solution)/shard_map/convert_element_type | solution.py:429
  1.0 0.0 copy-start.7
  1.0 0.0 copy-start.8
  1.0 0.0 copy-start.9
  1.0 0.1 constant_dynamic-slice_fusion.6
  1.1 0.1 collective-permute-start
  1.2 1.1 %constant_dynamic-slice_fusion.tiles = bf16[2,7,128,128]{3,2,1,0:T(8,128)(2,1)S(1)} fusion(bf16[8,7,128,128]{3,2,1,0:T(8,128)(2,1)} %refs_2_.3, s32[]{:T(128)S(6)} %select_n.90), kind=kLoop, calls=%fused_computation.15 | loop fusion | bytes 917508 | tf_op jit(solution)/shard_map/dynamic_slice | solution.py:454
  2.3 2.6 %collective-permute-start.7 = (bf16[11,128,128]{2,1,0:T(8,128)(2,1)S(1)}, bf16[11,128,128]{2,1,0:T(8,128)(2,1)S(1)}, u32[]{:S(2)}, u32[]{:S(2)}) collective-permute-start(bf16[11,128,128]{2,1,0:T(8,128)(2,1)S(1)} %shard_map.158), channel_id=1, source_target_pairs={{1,2},{2,1},{3,0},{0,3},{5,6},{6,5},{7,4},{4,7},{9,10},{10,9},{11,... | collective-permute-start | bytes 1081352 | tf_op jit(solution)/shard_map/ppermute | solution.py:418
  5.0 0.0 collective-permute-done
  5.0 0.0 copy-start
  5.0 0.0 copy-start.1
  5.1 1.4 %collective-permute-start.2 = (bf16[4,64,128]{2,1,0:T(8,128)(2,1)S(1)}, bf16[4,64,128]{2,1,0:T(8,128)(2,1)S(1)}, u32[]{:S(2)}, u32[]{:S(2)}) collective-permute-start(bf16[4,64,128]{2,1,0:T(8,128)(2,1)S(1)} %get-tuple-element.34._), channel_id=1, source_target_pairs={{0,4},{4,0},{8,12},{12,8},{1,5},{5,1},{9,13},{13,9},{2,6},{6,2},{1... | collective-permute-start | bytes 196616 | tf_op jit(solution)/shard_map/ppermute | solution.py:422
  6.5 1.0 %collective-permute-start.9 = (bf16[4,56,128]{2,1,0:T(8,128)(2,1)S(1)}, bf16[4,56,128]{2,1,0:T(8,128)(2,1)S(1)}, u32[]{:S(2)}, u32[]{:S(2)}) collective-permute-start(bf16[4,56,128]{2,1,0:T(8,128)(2,1)S(1)} %shard_map.159), channel_id=1, source_target_pairs={{1,2},{2,1},{3,0},{0,3},{5,6},{6,5},{7,4},{4,7},{9,10},{10,9},{11,... | collective-permute-start | bytes 172040 | tf_op jit(solution)/shard_map/ppermute | solution.py:418
  7.5 2.2 %collective-permute-start.5 = (bf16[4,64,128]{2,1,0:T(8,128)(2,1)S(1)}, bf16[4,64,128]{2,1,0:T(8,128)(2,1)S(1)}, u32[]{:S(2)}, u32[]{:S(2)}) collective-permute-start(bf16[4,64,128]{2,1,0:T(8,128)(2,1)S(1)} %get-tuple-element.31), channel_id=1, source_target_pairs={{0,12},{4,8},{8,4},{12,0},{1,13},{5,9},{9,5},{13,1},{2,14},{6,10},... | collective-permute-start | bytes 196616 | tf_op jit(solution)/shard_map/ppermute | solution.py:422
  9.7 0.1 collective-permute-start.4
  9.8 0.4 collective-permute-start.1
  10.2 0.1 add_add_fusion.refs_3_
  10.3 1.1 %collective-permute-done.1.refs_1_ = f32[3,16,8,128]{3,2,1,0:T(8,128)S(1)} collective-permute-done((f32[3,16,8,128]{3,2,1,0:T(8,128)S(1)}, f32[3,16,8,128]{3,2,1,0:T(8,128)S(1)}, u32[]{:S(2)}, u32[]{:S(2)}) %collective-permute-start.1) | collective-permute-done | bytes 196640 | tf_op jit(solution)/shard_map/ppermute | solution.py:415
  11.3 0.1 shard_map.155
  11.4 1.3 %collective-permute-start.3 = (f32[51,2,128]{2,1,0:T(2,128)S(1)}, f32[51,2,128]{2,1,0:T(2,128)S(1)}, u32[]{:S(2)}, u32[]{:S(2)}) collective-permute-start(f32[51,2,128]{2,1,0:T(2,128)S(1)} %get-tuple-element.18), channel_id=1, source_target_pairs={{1,2},{2,1},{3,0},{0,3},{5,6},{6,5},{7,4},{4,7},{9,10},{10,9},{11,... | collective-permute-start | bytes 156680 | tf_op jit(solution)/shard_map/ppermute | solution.py:418
  12.7 0.4 collective-permute-done.5.rest_3_.refs_2_
  13.1 3.4 %collective-permute-done.4.rest_2_.refs_1_ = bf16[4,64,128]{2,1,0:T(8,128)(2,1)S(1)} collective-permute-done((bf16[4,64,128]{2,1,0:T(8,128)(2,1)S(1)}, bf16[4,64,128]{2,1,0:T(8,128)(2,1)S(1)}, u32[]{:S(2)}, u32[]{:S(2)}) %collective-permute-start.4) | collective-permute-done | bytes 65568 | tf_op jit(solution)/shard_map/ppermute | solution.py:422
  16.5 0.0 copy-start.4
  16.6 0.0 copy-start.5
  16.6 0.6 %collective-permute-start.6 = (bf16[16,64,128]{2,1,0:T(8,128)(2,1)S(1)}, bf16[16,64,128]{2,1,0:T(8,128)(2,1)S(1)}, u32[]{:S(2)}, u32[]{:S(2)}) collective-permute-start(bf16[16,64,128]{2,1,0:T(8,128)(2,1)S(1)} %shard_map.156.refs_6_), channel_id=1, source_target_pairs={{0,1},{1,0},{2,3},{3,2},{4,5},{5,4},{6,7},{7,6},{8,9},{9,8},{10,11... | collective-permute-start | bytes 786440 | tf_op jit(solution)/shard_map/ppermute | solution.py:415
  17.2 0.0 collective-permute-done.7.refs_4_.refs_8_
  17.2 0.1 shard_map.160
  17.2 1.1 %collective-permute-start.10 = (bf16[12,56,128]{2,1,0:T(8,128)(2,1)S(1)}, bf16[12,56,128]{2,1,0:T(8,128)(2,1)S(1)}, u32[]{:S(2)}, u32[]{:S(2)}) collective-permute-start(bf16[12,56,128]{2,1,0:T(8,128)(2,1)S(1)} %shard_map.160), channel_id=1, source_target_pairs={{1,2},{2,1},{3,0},{0,3},{5,6},{6,5},{7,4},{4,7},{9,10},{10,9},{11,... | collective-permute-start | bytes 516104 | tf_op jit(solution)/shard_map/ppermute | solution.py:418
  18.4 1.3 %collective-permute-start.8 = (bf16[3,128,128]{2,1,0:T(8,128)(2,1)S(1)}, bf16[3,128,128]{2,1,0:T(8,128)(2,1)S(1)}, u32[]{:S(2)}, u32[]{:S(2)}) collective-permute-start(bf16[3,128,128]{2,1,0:T(8,128)(2,1)S(1)} %slice.46), channel_id=1, source_target_pairs={{0,16},{16,0},{1,17},{17,1},{2,18},{18,2},{3,19},{19,3},{4,20},{20... | collective-permute-start | bytes 294920 | tf_op jit(solution)/shard_map/ppermute | solution.py:457
  19.7 0.0 collective-permute-done.6.refs_7_
  19.7 1.4 %shard_map.157 = (f32[3,16,8,128]{3,2,1,0:T(8,128)S(1)}, f32[8,128]{1,0:T(8,128)S(1)}, f32[8,3,14,8,128]{4,3,2,1,0:T(8,128)S(1)}, bf16[12,16,16,128]{3,2,1,0:T(8...) custom-call(s32[8,8]{1,0:T(8,128)S(1)} %pad_add_fusion.refs_0_, ...), custom_call_target="tpu_custom_call" | custom-call | tf_op jit(solution)/shard_map/pallas_call | solution.py:385
  21.2 1.3 %collective-permute-done.8.refs_9_ = bf16[3,128,128]{2,1,0:T(8,128)(2,1)S(1)} collective-permute-done((bf16[3,128,128]{2,1,0:T(8,128)(2,1)S(1)}, bf16[3,128,128]{2,1,0:T(8,128)(2,1)S(1)}, u32[]{:S(2)}, u32[]{:S(2)}) %collective-permute-start.8) | collective-permute-done | bytes 98336 | tf_op jit(solution)/shard_map/ppermute | solution.py:457
  22.5 0.8 %collective-permute-done.10.refs_13_ = bf16[12,56,128]{2,1,0:T(8,128)(2,1)S(1)} collective-permute-done((bf16[12,56,128]{2,1,0:T(8,128)(2,1)S(1)}, bf16[12,56,128]{2,1,0:T(8,128)(2,1)S(1)}, u32[]{:S(2)}, u32[]{:S(2)}) %collective-permute-start.10) | collective-permute-done | bytes 172064 | tf_op jit(solution)/shard_map/ppermute | solution.py:418
  23.3 0.0 copy-start.10
  23.3 2.5 %shard_map.161 = (bf16[4,12,16,128]{3,2,1,0:T(8,128)(2,1)S(1)}, bf16[36,16,128]{2,1,0:T(8,128)(2,1)S(1)}, bf16[2,768,256]{2,1,0:T(8,128)(2,1)S(1)}, bf16[4,256,128]{2,1,0:T(8,128)(2,1)S(1)}) custom-call(bf16[256,256]{1,0:T(8,128)(2,1)S(1)} %copy-done.1, f32[3,16,8,128]{3,2,1,0:T(8,128)S(1)} %get-tuple-element.20.refs_1_, ...), custom_call_target="tpu_custom_call" | custom-call | tf_op jit(solution)/shard_map/pallas_call | solution.py:385
  25.8 0.4 %collective-permute-start.11 = (bf16[4,12,16,128]{3,2,1,0:T(8,128)(2,1)S(1)}, bf16[4,12,16,128]{3,2,1,0:T(8,128)(2,1)S(1)}, u32[]{:S(2)}, u32[]{:S(2)}) collective-permute-start(bf16[4,12,16,128]{3,2,1,0:T(8,128)(2,1)S(1)} %get-tuple-element.29.refs_10_), channel_id=1, source_target_pairs={{0,1},{1,0},{2,3},{3,2},{4,5},{5,4},{6,7},{7,6},{8,9},{9,8},{10,11... | collective-permute-start | bytes 589832 | tf_op jit(solution)/shard_map/ppermute | solution.py:415
  26.3 1.2 %collective-permute-start.12 = (bf16[36,16,128]{2,1,0:T(8,128)(2,1)S(1)}, bf16[36,16,128]{2,1,0:T(8,128)(2,1)S(1)}, u32[]{:S(2)}, u32[]{:S(2)}) collective-permute-start(bf16[36,16,128]{2,1,0:T(8,128)(2,1)S(1)} %get-tuple-element.30), channel_id=1, source_target_pairs={{1,2},{2,1},{3,0},{0,3},{5,6},{6,5},{7,4},{4,7},{9,10},{10,9},{11,... | collective-permute-start | bytes 442376 | tf_op jit(solution)/shard_map/ppermute | solution.py:418
  27.4 4.4 %collective-permute-done.12.refs_12_ = bf16[36,16,128]{2,1,0:T(8,128)(2,1)S(1)} collective-permute-done((bf16[36,16,128]{2,1,0:T(8,128)(2,1)S(1)}, bf16[36,16,128]{2,1,0:T(8,128)(2,1)S(1)}, u32[]{:S(2)}, u32[]{:S(2)}) %collective-permute-start.12) | collective-permute-done | bytes 147488 | tf_op jit(solution)/shard_map/ppermute | solution.py:418
  31.9 0.0 collective-permute-done.11.refs_11_
  31.9 0.0 copy-start.3
  31.9 1.9 %shard_map.162 = bf16[2,8,32,128]{3,2,1,0:T(8,128)(2,1)S(1)} custom-call(bf16[256,256]{1,0:T(8,128)(2,1)S(1)} %copy-done.2, f32[3,16,8,128]{3,2,1,0:T(8,128)S(1)} %get-tuple-element.20.refs_1_, f32[8,128]{1,0:T(8,128)S(1)} %get-tuple-element.21.refs_2_, f32[8,3,14,8,128]{4,3,2,1,0:T(8,128)S(1)} %get-tuple-element.22.refs_3_, ...), custom_call_target="tpu_custom_call" | custom-call | tf_op jit(solution)/shard_map/pallas_call | solution.py:385
  33.9 0.3 collective-permute-start.13
  34.1 1.0 %collective-permute-done.13 = bf16[8,32,128]{2,1,0:T(8,128)(2,1)S(1)} collective-permute-done((bf16[8,32,128]{2,1,0:T(8,128)(2,1)S(1)}, bf16[8,32,128]{2,1,0:T(8,128)(2,1)S(1)}, u32[]{:S(2)}, u32[]{:S(2)}) %collective-permute-start.13) | collective-permute-done | bytes 65568 | tf_op jit(solution)/shard_map/ppermute | solution.py:415
  35.2 1.9 %collective-permute-start.14 = (bf16[2,4,32,128]{3,2,1,0:T(8,128)(2,1)S(1)}, bf16[2,4,32,128]{3,2,1,0:T(8,128)(2,1)S(1)}, u32[]{:S(2)}, u32[]{:S(2)}) collective-permute-start(bf16[2,4,32,128]{3,2,1,0:T(8,128)(2,1)S(1)} %pad_maximum_fusion.1), channel_id=1, source_target_pairs={{0,0},{1,4},{4,1},{5,5},{8,8},{9,12},{12,9},{13,13},{2,2},{3,6},{6... | collective-permute-start | bytes 196616 | tf_op jit(solution)/shard_map/ppermute | solution.py:581
  37.1 2.5 %collective-permute-start.15 = (bf16[2,4,32,128]{3,2,1,0:T(8,128)(2,1)S(1)}, bf16[2,4,32,128]{3,2,1,0:T(8,128)(2,1)S(1)}, u32[]{:S(2)}, u32[]{:S(2)}) collective-permute-start(bf16[2,4,32,128]{3,2,1,0:T(8,128)(2,1)S(1)} %pad_maximum_fusion.2), channel_id=1, source_target_pairs={{0,8},{1,12},{4,9},{5,13},{8,0},{9,4},{12,1},{13,5},{2,10},{3,14},... | collective-permute-start | bytes 196616 | tf_op jit(solution)/shard_map/ppermute | solution.py:581
  39.6 1.8 %collective-permute-done.14.refs_1_ = bf16[2,4,32,128]{3,2,1,0:T(8,128)(2,1)S(1)} collective-permute-done((bf16[2,4,32,128]{3,2,1,0:T(8,128)(2,1)S(1)}, bf16[2,4,32,128]{3,2,1,0:T(8,128)(2,1)S(1)}, u32[]{:S(2)}, u32[]{:S(2)}) %collective-permute-start.14) | collective-permute-done | bytes 65568 | tf_op jit(solution)/shard_map/ppermute | solution.py:581
  41.4 1.3 %collective-permute-done.15.refs_2_ = bf16[2,4,32,128]{3,2,1,0:T(8,128)(2,1)S(1)} collective-permute-done((bf16[2,4,32,128]{3,2,1,0:T(8,128)(2,1)S(1)}, bf16[2,4,32,128]{3,2,1,0:T(8,128)(2,1)S(1)}, u32[]{:S(2)}, u32[]{:S(2)}) %collective-permute-start.15) | collective-permute-done | bytes 65568 | tf_op jit(solution)/shard_map/ppermute | solution.py:581
  42.7 0.9 %shard_map.163 = f32[4,16,8,128]{3,2,1,0:T(8,128)} custom-call(bf16[256,256]{1,0:T(8,128)(2,1)S(1)} %copy-done.3, bf16[2,4,32,128]{3,2,1,0:T(8,128)(2,1)S(1)} %collective-permute-done.14.refs_1_, bf16[2,4,32,128]{3,2,1,0:T(8,128)(2,1)S(1)} %collective-permute-done.15.refs_2_), custom_call_target="tpu_custom_call" | custom-call | tf_op jit(solution)/shard_map/pallas_call | solution.py:385
  (40 shorter events, 0.3 us)
Async XLA Ops:
  0.0 5.0 %copy-start.12 = (s32[8,4]{0,1:T(4,128)S(1)}, s32[8,4]{0,1:T(4,128)}, u32[]{:S(2)}) copy-start(s32[8,4]{0,1:T(4,128)} %param.22) | copy-start | bytes 388
  1.0 8.8 %copy-start.7 = (f32[16,8,128]{2,1,0:T(8,128)S(1)}, f32[16,8,128]{2,1,0:T(8,128)}, u32[]{:S(2)}) copy-start(f32[16,8,128]{2,1,0:T(8,128)} %start.1) | copy-start | bytes 196612
  1.0 8.8 %copy-start.8 = (f32[16,8,128]{2,1,0:T(8,128)S(1)}, f32[16,8,128]{2,1,0:T(8,128)}, u32[]{:S(2)}) copy-start(f32[16,8,128]{2,1,0:T(8,128)} %reaction.1) | copy-start | bytes 196612
  1.0 8.8 %copy-start.9 = (f32[16,8,128]{2,1,0:T(8,128)S(1)}, f32[16,8,128]{2,1,0:T(8,128)}, u32[]{:S(2)}) copy-start(f32[16,8,128]{2,1,0:T(8,128)} %source.1) | copy-start | bytes 196612
  1.1 3.9 %collective-permute-start = (bf16[4,64,128]{2,1,0:T(8,128)(2,1)S(1)}, bf16[4,64,128]{2,1,0:T(8,128)(2,1)S(1)}, u32[]{:S(2)}, u32[]{:S(2)}) collective-permute-start(bf16[4,64,128]{2,1,0:T(8,128)(2,1)S(1)} %bitcast.23), channel_id=1, source_target_pairs={{0,1},{1,0},{2,3},{3,2},{4,5},{5,4},{6,7},{7,6},{8,9},{9,8},{10,11... | collective-permute-start | bytes 196616 | tf_op jit(solution)/shard_map/ppermute | solution.py:415
  1.2 9.0 %copy-start.13 = (s32[4]{0:T(128)S(1)}, s32[4]{0:T(128)}, u32[]{:S(2)}) copy-start(s32[4]{0:T(128)} %constant.125.clone) | copy-start | bytes 52
  1.2 10.1 %copy-start.11 = (f32[8,128]{1,0:T(8,128)S(1)}, f32[8,128]{1,0:T(8,128)}, u32[]{:S(2)}) copy-start(f32[8,128]{1,0:T(8,128)} %refs_5_.1) | copy-start | bytes 12292
  2.3 14.8 %collective-permute-start.7 = (bf16[11,128,128]{2,1,0:T(8,128)(2,1)S(1)}, bf16[11,128,128]{2,1,0:T(8,128)(2,1)S(1)}, u32[]{:S(2)}, u32[]{:S(2)}) collective-permute-start(bf16[11,128,128]{2,1,0:T(8,128)(2,1)S(1)} %shard_map.158), channel_id=1, source_target_pairs={{1,2},{2,1},{3,0},{0,3},{5,6},{6,5},{7,4},{4,7},{9,10},{10,9},{11,... | collective-permute-start | bytes 1081352 | tf_op jit(solution)/shard_map/ppermute | solution.py:418
  5.0 14.7 %copy-start = (bf16[8,7,128,128]{3,2,1,0:T(8,128)(2,1)S(1)}, bf16[8,7,128,128]{3,2,1,0:T(8,128)(2,1)}, u32[]{:S(2)}) copy-start(bf16[8,7,128,128]{3,2,1,0:T(8,128)(2,1)} %refs_2_.3) | copy-start | bytes 5505028
  5.0 14.7 %copy-start.1 = (bf16[256,256]{1,0:T(8,128)(2,1)S(1)}, bf16[256,256]{1,0:T(8,128)(2,1)}, u32[]{:S(2)}) copy-start(bf16[256,256]{1,0:T(8,128)(2,1)} %constant.126.clone.refs_1_.refs_0_) | copy-start | bytes 393220
  5.1 4.7 %collective-permute-start.2 = (bf16[4,64,128]{2,1,0:T(8,128)(2,1)S(1)}, bf16[4,64,128]{2,1,0:T(8,128)(2,1)S(1)}, u32[]{:S(2)}, u32[]{:S(2)}) collective-permute-start(bf16[4,64,128]{2,1,0:T(8,128)(2,1)S(1)} %get-tuple-element.34._), channel_id=1, source_target_pairs={{0,4},{4,0},{8,12},{12,8},{1,5},{5,1},{9,13},{13,9},{2,6},{6,2},{1... | collective-permute-start | bytes 196616 | tf_op jit(solution)/shard_map/ppermute | solution.py:422
  6.5 10.7 %collective-permute-start.9 = (bf16[4,56,128]{2,1,0:T(8,128)(2,1)S(1)}, bf16[4,56,128]{2,1,0:T(8,128)(2,1)S(1)}, u32[]{:S(2)}, u32[]{:S(2)}) collective-permute-start(bf16[4,56,128]{2,1,0:T(8,128)(2,1)S(1)} %shard_map.159), channel_id=1, source_target_pairs={{1,2},{2,1},{3,0},{0,3},{5,6},{6,5},{7,4},{4,7},{9,10},{10,9},{11,... | collective-permute-start | bytes 172040 | tf_op jit(solution)/shard_map/ppermute | solution.py:418
  7.5 5.6 %collective-permute-start.5 = (bf16[4,64,128]{2,1,0:T(8,128)(2,1)S(1)}, bf16[4,64,128]{2,1,0:T(8,128)(2,1)S(1)}, u32[]{:S(2)}, u32[]{:S(2)}) collective-permute-start(bf16[4,64,128]{2,1,0:T(8,128)(2,1)S(1)} %get-tuple-element.31), channel_id=1, source_target_pairs={{0,12},{4,8},{8,4},{12,0},{1,13},{5,9},{9,5},{13,1},{2,14},{6,10},... | collective-permute-start | bytes 196616 | tf_op jit(solution)/shard_map/ppermute | solution.py:422
  9.7 6.9 %collective-permute-start.4 = (bf16[4,64,128]{2,1,0:T(8,128)(2,1)S(1)}, bf16[4,64,128]{2,1,0:T(8,128)(2,1)S(1)}, u32[]{:S(2)}, u32[]{:S(2)}) collective-permute-start(bf16[4,64,128]{2,1,0:T(8,128)(2,1)S(1)} %get-tuple-element.32), channel_id=1, source_target_pairs={{0,8},{4,12},{8,0},{12,4},{1,9},{5,13},{9,1},{13,5},{2,10},{6,14},... | collective-permute-start | bytes 196616 | tf_op jit(solution)/shard_map/ppermute | solution.py:422
  9.8 1.5 %collective-permute-start.1 = (f32[3,16,8,128]{3,2,1,0:T(8,128)S(1)}, f32[3,16,8,128]{3,2,1,0:T(8,128)S(1)}, u32[]{:S(2)}, u32[]{:S(2)}) collective-permute-start(f32[3,16,8,128]{3,2,1,0:T(8,128)S(1)} %shard_map.154.refs_0_), channel_id=1, source_target_pairs={{0,1},{1,0},{2,3},{3,2},{4,5},{5,4},{6,7},{7,6},{8,9},{9,8},{10,11... | collective-permute-start | bytes 589832 | tf_op jit(solution)/shard_map/ppermute | solution.py:415
  11.4 6.9 %collective-permute-start.3 = (f32[51,2,128]{2,1,0:T(2,128)S(1)}, f32[51,2,128]{2,1,0:T(2,128)S(1)}, u32[]{:S(2)}, u32[]{:S(2)}) collective-permute-start(f32[51,2,128]{2,1,0:T(2,128)S(1)} %get-tuple-element.18), channel_id=1, source_target_pairs={{1,2},{2,1},{3,0},{0,3},{5,6},{6,5},{7,4},{4,7},{9,10},{10,9},{11,... | collective-permute-start | bytes 156680 | tf_op jit(solution)/shard_map/ppermute | solution.py:418
  16.5 6.8 %copy-start.4 = (bf16[224,224]{1,0:T(8,128)(2,1)S(1)}, bf16[224,224]{1,0:T(8,128)(2,1)}, u32[]{:S(2)}) copy-start(bf16[224,224]{1,0:T(8,128)(2,1)} %constant.127.clone.refs_10_) | copy-start | bytes 301060
  16.6 6.8 %copy-start.5 = (bf16[192,192]{1,0:T(8,128)(2,1)S(1)}, bf16[192,192]{1,0:T(8,128)(2,1)}, u32[]{:S(2)}) copy-start(bf16[192,192]{1,0:T(8,128)(2,1)} %constant.128.clone.refs_11_) | copy-start | bytes 221188
  16.6 3.1 %collective-permute-start.6 = (bf16[16,64,128]{2,1,0:T(8,128)(2,1)S(1)}, bf16[16,64,128]{2,1,0:T(8,128)(2,1)S(1)}, u32[]{:S(2)}, u32[]{:S(2)}) collective-permute-start(bf16[16,64,128]{2,1,0:T(8,128)(2,1)S(1)} %shard_map.156.refs_6_), channel_id=1, source_target_pairs={{0,1},{1,0},{2,3},{3,2},{4,5},{5,4},{6,7},{7,6},{8,9},{9,8},{10,11... | collective-permute-start | bytes 786440 | tf_op jit(solution)/shard_map/ppermute | solution.py:415
  17.2 6.1 %collective-permute-start.10 = (bf16[12,56,128]{2,1,0:T(8,128)(2,1)S(1)}, bf16[12,56,128]{2,1,0:T(8,128)(2,1)S(1)}, u32[]{:S(2)}, u32[]{:S(2)}) collective-permute-start(bf16[12,56,128]{2,1,0:T(8,128)(2,1)S(1)} %shard_map.160), channel_id=1, source_target_pairs={{1,2},{2,1},{3,0},{0,3},{5,6},{6,5},{7,4},{4,7},{9,10},{10,9},{11,... | collective-permute-start | bytes 516104 | tf_op jit(solution)/shard_map/ppermute | solution.py:418
  18.4 4.1 %collective-permute-start.8 = (bf16[3,128,128]{2,1,0:T(8,128)(2,1)S(1)}, bf16[3,128,128]{2,1,0:T(8,128)(2,1)S(1)}, u32[]{:S(2)}, u32[]{:S(2)}) collective-permute-start(bf16[3,128,128]{2,1,0:T(8,128)(2,1)S(1)} %slice.46), channel_id=1, source_target_pairs={{0,16},{16,0},{1,17},{17,1},{2,18},{18,2},{3,19},{19,3},{4,20},{20... | collective-permute-start | bytes 294920 | tf_op jit(solution)/shard_map/ppermute | solution.py:457
  23.3 8.6 %copy-start.2 = (bf16[256,256]{1,0:T(8,128)(2,1)S(1)}, bf16[256,256]{1,0:T(8,128)(2,1)}, u32[]{:S(2)}) copy-start(bf16[256,256]{1,0:T(8,128)(2,1)} %constant.129.clone.refs_0_) | copy-start | bytes 393220
  23.3 8.6 %copy-start.6 = (bf16[160,160]{1,0:T(8,128)(2,1)S(1)}, bf16[160,160]{1,0:T(8,128)(2,1)}, u32[]{:S(2)}) copy-start(bf16[160,160]{1,0:T(8,128)(2,1)} %constant.130.clone.refs_8_) | copy-start | bytes 153604
  23.3 8.6 %copy-start.10 = (bf16[128,128]{1,0:T(8,128)(2,1)S(1)}, bf16[128,128]{1,0:T(8,128)(2,1)}, u32[]{:S(2)}) copy-start(bf16[128,128]{1,0:T(8,128)(2,1)} %constant.131.clone.refs_9_) | copy-start | bytes 98308
  25.8 6.1 %collective-permute-start.11 = (bf16[4,12,16,128]{3,2,1,0:T(8,128)(2,1)S(1)}, bf16[4,12,16,128]{3,2,1,0:T(8,128)(2,1)S(1)}, u32[]{:S(2)}, u32[]{:S(2)}) collective-permute-start(bf16[4,12,16,128]{3,2,1,0:T(8,128)(2,1)S(1)} %get-tuple-element.29.refs_10_), channel_id=1, source_target_pairs={{0,1},{1,0},{2,3},{3,2},{4,5},{5,4},{6,7},{7,6},{8,9},{9,8},{10,11... | collective-permute-start | bytes 589832 | tf_op jit(solution)/shard_map/ppermute | solution.py:415
  26.3 5.6 %collective-permute-start.12 = (bf16[36,16,128]{2,1,0:T(8,128)(2,1)S(1)}, bf16[36,16,128]{2,1,0:T(8,128)(2,1)S(1)}, u32[]{:S(2)}, u32[]{:S(2)}) collective-permute-start(bf16[36,16,128]{2,1,0:T(8,128)(2,1)S(1)} %get-tuple-element.30), channel_id=1, source_target_pairs={{1,2},{2,1},{3,0},{0,3},{5,6},{6,5},{7,4},{4,7},{9,10},{10,9},{11,... | collective-permute-start | bytes 442376 | tf_op jit(solution)/shard_map/ppermute | solution.py:418
  31.9 10.8 %copy-start.3 = (bf16[256,256]{1,0:T(8,128)(2,1)S(1)}, bf16[256,256]{1,0:T(8,128)(2,1)}, u32[]{:S(2)}) copy-start(bf16[256,256]{1,0:T(8,128)(2,1)} %constant.132.clone.refs_0_) | copy-start | bytes 393220
  33.9 1.3 %collective-permute-start.13 = (bf16[8,32,128]{2,1,0:T(8,128)(2,1)S(1)}, bf16[8,32,128]{2,1,0:T(8,128)(2,1)S(1)}, u32[]{:S(2)}, u32[]{:S(2)}) collective-permute-start(bf16[8,32,128]{2,1,0:T(8,128)(2,1)S(1)} %slice_bitcast_fusion), channel_id=1, source_target_pairs={{0,1},{1,0},{2,3},{3,2},{4,5},{5,4},{6,7},{7,6},{8,9},{9,8},{10,11... | collective-permute-start | bytes 196616 | tf_op jit(solution)/shard_map/ppermute | solution.py:415
  35.2 6.2 %collective-permute-start.14 = (bf16[2,4,32,128]{3,2,1,0:T(8,128)(2,1)S(1)}, bf16[2,4,32,128]{3,2,1,0:T(8,128)(2,1)S(1)}, u32[]{:S(2)}, u32[]{:S(2)}) collective-permute-start(bf16[2,4,32,128]{3,2,1,0:T(8,128)(2,1)S(1)} %pad_maximum_fusion.1), channel_id=1, source_target_pairs={{0,0},{1,4},{4,1},{5,5},{8,8},{9,12},{12,9},{13,13},{2,2},{3,6},{6... | collective-permute-start | bytes 196616 | tf_op jit(solution)/shard_map/ppermute | solution.py:581
  37.1 5.6 %collective-permute-start.15 = (bf16[2,4,32,128]{3,2,1,0:T(8,128)(2,1)S(1)}, bf16[2,4,32,128]{3,2,1,0:T(8,128)(2,1)S(1)}, u32[]{:S(2)}, u32[]{:S(2)}) collective-permute-start(bf16[2,4,32,128]{3,2,1,0:T(8,128)(2,1)S(1)} %pad_maximum_fusion.2), channel_id=1, source_target_pairs={{0,8},{1,12},{4,9},{5,13},{8,0},{9,4},{12,1},{13,5},{2,10},{3,14},... | collective-permute-start | bytes 196616 | tf_op jit(solution)/shard_map/ppermute | solution.py:581

commit v6 on v5

--- a/solution.py
+++ b/solution.py
@@ -172,11 +172,11 @@
         out[k * local : (k + 1) * local] = piece[:, 4 : rows - 4]
 
 
-def gather_kernel(*rest):
+def gather_kernel(places, *rest):
     parts, out = rest[:-1], rest[-1]
     local = parts[0].shape[0]
     mine = lax.axis_index("tm")
-    for k, part in enumerate(parts):
+    for k, part in zip(places, parts):
         out[pl.ds(lax.bitwise_xor(mine, k) * local, local)] = part[...]
 
 
@@ -289,8 +289,8 @@
     return outer[:each] + inner + outer[each:]
 
 
-def first_kernel(count, order, coef, diag, inverse, ready, near_across, near_along, picks, edge_one,
-                 edge_two, forward, backward, first, others, out, message, across, along, edge_tiles,
+def first_kernel(count, sent, order, coef, diag, inverse, ready, near_across, near_along, picks, edge_one,
+                 edge_two, forward, backward, early, second, others, out, message, across, along, edge_tiles,
                  arrived, values, packed, spec):
     core, mine, group = lax.axis_index("layer"), lax.axis_index("tm"), lax.axis_index("group")
     rest = 7 - edge_two.shape[0]
@@ -317,9 +317,10 @@
     local = steps // count
     arrived[:, :4] = jnp.zeros((steps, 4, width), jnp.bfloat16)
     arrived[:, rows - 4 :] = jnp.zeros((steps, 4, width), jnp.bfloat16)
-    for k in range(count):
-        part = first[...] if k == 0 else others[(k - 1) * local : k * local]
-        arrived[pl.ds(lax.bitwise_xor(mine, k) * local, local), 4 : rows - 4] = part
+    for parts, places in zip((early, second, others), sent):
+        for at, k in enumerate(places):
+            part = parts[at * local : (at + 1) * local]
+            arrived[pl.ds(lax.bitwise_xor(mine, k) * local, local), 4 : rows - 4] = part
     arrive(arrived, order, values, 8 * core)
 
     def write(element, state):
@@ -455,21 +456,29 @@
     )
     edge_one = over_circle(edge_one)
     edge_two = lax.ppermute(edge_one[rest : tiles.shape[1]], "group", swap)
+    turn = sorted(range(1, count), key=lambda k: (k < count // 2, -k))
+
     def trimmed(parts, later_than):
         return call(
             lambda *refs: trim_kernel(len(parts), *refs),
             held((local_steps * len(parts), (window - 2) * half, width)),
             [],
             [],
-            parts,
+            [chunks[k] for k in parts],
             later_than,
         )
 
-    across = [over_circle(trimmed(chunks[:1], []))]
-    across.append(over_circle(trimmed(chunks[1:], [across[0], edge_one])))
-
+    sent = [[0], turn[:1], turn[1:]]
+    across = [over_circle(trimmed(sent[0], [])), over_circle(trimmed(sent[1], []))]
+    across.append(over_circle(trimmed(sent[2], [across[0], edge_one])))
+
+    places = [0] + turn
     own = call(
-        gather_kernel, held((steps, window * half, width)), [], [], list(chunks)
+        lambda *refs: gather_kernel(places, *refs),
+        held((steps, window * half, width)),
+        [],
+        [],
+        [chunks[k] for k in places],
     )
 
     fields = call(
@@ -494,7 +503,7 @@
         [],
         [],
         [fields, over_core(fields), self_diag, slots],
-        [chunks[1]],
+        [chunks[turn[0]]],
     )
     bundle_edge = over_circle(bundle_edge)
     edge_slots = bundle_edge[3 * window + 1 :, :, :local_elems].reshape(4, local_elems)
@@ -547,7 +556,7 @@
         [constant(order), tiles, bundle, bundle_edge, self_diag, own, over_core(own)],
     )
     state, edge, *outer = call(
-        lambda *refs: first_kernel(count, *refs),
+        lambda *refs: first_kernel(count, sent, *refs),
         (
             held((4, window - 4, steps, width)),
             held((2 * (window - 6) + 2 * (window - 8), steps, width)),

time: 43.8 us -> 43.9 us (level)
  starting transfers between devices: 18.4 us -> 20.7 us
  waiting for transfers between devices: 15.6 us -> 13.3 us
    ppermute x3, waiting for transfers between devices: 3.77 us -> 2.13 us  [exchanged(): lax.ppermute(parts[k], 'tm', [(i, i ^ k) for i in range(count)])]
    ppermute x2, starting transfers between devices: 4.38 us -> 5.96 us  [shards(): lax.ppermute(jnp.stack([keep[cut], got[cut]]), ('tm', 'layer'), pairs)]
    ppermute x5, starting transfers between devices: 1.8 us -> 2.48 us  [over_core(): return lax.ppermute(array, 'layer', swap)]
    ppermute x2, waiting for transfers between devices: 3.1 us -> 2.63 us  [shards(): lax.ppermute(jnp.stack([keep[cut], got[cut]]), ('tm', 'layer'), pairs)]
    ppermute x5 -> x6, waiting for transfers between devices: 5.27 us -> 4.99 us  [over_circle(): return lax.ppermute(array, ('space', 'layer'), circle)]
    ppermute x5 -> x6, starting transfers between devices: 7.24 us -> 7.5 us  [over_circle(): return lax.ppermute(array, ('space', 'layer'), circle)]
    pallas_call x10 -> x11, Pallas kernels: 7.01 us -> 7.03 us  [call(): pl.pallas_call(kernel, out_shape=out_shape, in_specs=[pl.BlockSpec(memory...]
  transfers between devices with their start and end apart: 16 -> 17, of which waited for: 9 -> 9; matrix products, arithmetic and copies ran while one was open for 3% -> 3% of each run, Pallas kernels for 4% -> 4%
where the time goes in v6:
time: 43.9 us; the launch traced here: 43.7 us
  starting transfers between devices  20.7 us (47%)
  waiting for transfers between devices  13.3 us (30%)
  Pallas kernels  7.03 us (16%)
  local copies, waits for them, and re-layouts  1.28 us (3%)
  other arithmetic  1.13 us (3%)
    ppermute x6, starting transfers between devices, over_circle(): return lax.ppermute(array, ('space', 'layer'), circle)  7.5 us
    pallas_call x11, Pallas kernels, call(): pl.pallas_call(kernel, out_shape=out_shape, in_specs=[pl.BlockSpec(memory...  7.03 us
    ppermute x2, starting transfers between devices, shards(): lax.ppermute(jnp.stack([keep[cut], got[cut]]), ('tm', 'layer'), pairs)  5.96 us
    ppermute x6, waiting for transfers between devices, over_circle(): return lax.ppermute(array, ('space', 'layer'), circle)  4.99 us
    ppermute x3, starting transfers between devices, exchanged(): lax.ppermute(parts[k], 'tm', [(i, i ^ k) for i in range(count)])  3.42 us
    ppermute x2, waiting for transfers between devices, shards(): lax.ppermute(jnp.stack([keep[cut], got[cut]]), ('tm', 'layer'), pairs)  2.63 us
    ppermute x5, starting transfers between devices, over_core(): return lax.ppermute(array, 'layer', swap)  2.48 us
    ppermute x3, waiting for transfers between devices, exchanged(): lax.ppermute(parts[k], 'tm', [(i, i ^ k) for i in range(count)])  2.13 us
  transfers between devices with their start and end apart: 17, of which 9 were waited for; matrix products, arithmetic and copies ran while one was open for 3% of the time, Pallas kernels for 4%

profile of v6, /device:TPU:1, one launch (start us, length us, event | category | flops | bytes accessed | tf_op | source)
XLA Modules:
  0.0 43.7 jit_solution(7049193382414169322)
XLA Ops:
  0.0 1.0 %convert_element_type.15 = bf16[4,16,8,128]{3,2,1,0:T(8,128)(2,1)S(1)} convert(f32[4,16,8,128]{3,2,1,0:T(8,128)} %param.16) | non-fusion elementwise | flops 65536 | bytes 393216 | tf_op jit(solution)/shard_map/convert_element_type | solution.py:430
  1.0 0.0 copy-start.7
  1.0 0.0 copy-start.8
  1.0 0.0 copy-start.9
  1.0 0.1 constant_dynamic-slice_fusion.6
  1.1 0.1 collective-permute-start
  1.2 1.1 %constant_dynamic-slice_fusion.tiles = bf16[2,7,128,128]{3,2,1,0:T(8,128)(2,1)S(1)} fusion(bf16[8,7,128,128]{3,2,1,0:T(8,128)(2,1)} %refs_2_.3, s32[]{:T(128)S(6)} %select_n.90), kind=kLoop, calls=%fused_computation.15 | loop fusion | bytes 917508 | tf_op jit(solution)/shard_map/dynamic_slice | solution.py:455
  2.3 2.6 %collective-permute-start.7 = (bf16[11,128,128]{2,1,0:T(8,128)(2,1)S(1)}, bf16[11,128,128]{2,1,0:T(8,128)(2,1)S(1)}, u32[]{:S(2)}, u32[]{:S(2)}) collective-permute-start(bf16[11,128,128]{2,1,0:T(8,128)(2,1)S(1)} %shard_map.158), channel_id=1, source_target_pairs={{1,2},{2,1},{3,0},{0,3},{5,6},{6,5},{7,4},{4,7},{9,10},{10,9},{11,... | collective-permute-start | bytes 1081352 | tf_op jit(solution)/shard_map/ppermute | solution.py:419
  5.0 0.0 collective-permute-done
  5.0 0.0 copy-start
  5.0 0.0 copy-start.1
  5.1 3.4 %collective-permute-start.2 = (bf16[4,64,128]{2,1,0:T(8,128)(2,1)S(1)}, bf16[4,64,128]{2,1,0:T(8,128)(2,1)S(1)}, u32[]{:S(2)}, u32[]{:S(2)}) collective-permute-start(bf16[4,64,128]{2,1,0:T(8,128)(2,1)S(1)} %get-tuple-element.33), channel_id=1, source_target_pairs={{0,12},{4,8},{8,4},{12,0},{1,13},{5,9},{9,5},{13,1},{2,14},{6,10},... | collective-permute-start | bytes 196616 | tf_op jit(solution)/shard_map/ppermute | solution.py:423
  8.5 1.0 %collective-permute-start.9 = (bf16[4,56,128]{2,1,0:T(8,128)(2,1)S(1)}, bf16[4,56,128]{2,1,0:T(8,128)(2,1)S(1)}, u32[]{:S(2)}, u32[]{:S(2)}) collective-permute-start(bf16[4,56,128]{2,1,0:T(8,128)(2,1)S(1)} %shard_map.159), channel_id=1, source_target_pairs={{1,2},{2,1},{3,0},{0,3},{5,6},{6,5},{7,4},{4,7},{9,10},{10,9},{11,... | collective-permute-start | bytes 172040 | tf_op jit(solution)/shard_map/ppermute | solution.py:419
  9.5 0.0 collective-permute-start.5
  9.6 0.7 %collective-permute-done.2.refs_4_.refs_1_.refs_0_ = bf16[4,64,128]{2,1,0:T(8,128)(2,1)S(1)} collective-permute-done((bf16[4,64,128]{2,1,0:T(8,128)(2,1)S(1)}, bf16[4,64,128]{2,1,0:T(8,128)(2,1)S(1)}, u32[]{:S(2)}, u32[]{:S(2)}) %collective-permute-start.2) | collective-permute-done | bytes 65568 | tf_op jit(solution)/shard_map/ppermute | solution.py:423
  10.2 1.6 %collective-permute-start.1 = (f32[3,16,8,128]{3,2,1,0:T(8,128)S(1)}, f32[3,16,8,128]{3,2,1,0:T(8,128)S(1)}, u32[]{:S(2)}, u32[]{:S(2)}) collective-permute-start(f32[3,16,8,128]{3,2,1,0:T(8,128)S(1)} %shard_map.154.refs_0_), channel_id=1, source_target_pairs={{0,1},{1,0},{2,3},{3,2},{4,5},{5,4},{6,7},{7,6},{8,9},{9,8},{10,11... | collective-permute-start | bytes 589832 | tf_op jit(solution)/shard_map/ppermute | solution.py:416
  11.8 0.1 add_add_fusion.refs_3_
  11.9 1.0 %collective-permute-done.1.refs_1_ = f32[3,16,8,128]{3,2,1,0:T(8,128)S(1)} collective-permute-done((f32[3,16,8,128]{3,2,1,0:T(8,128)S(1)}, f32[3,16,8,128]{3,2,1,0:T(8,128)S(1)}, u32[]{:S(2)}, u32[]{:S(2)}) %collective-permute-start.1) | collective-permute-done | bytes 196640 | tf_op jit(solution)/shard_map/ppermute | solution.py:416
  12.9 0.1 shard_map.155
  13.0 0.5 %collective-permute-start.3 = (f32[51,2,128]{2,1,0:T(2,128)S(1)}, f32[51,2,128]{2,1,0:T(2,128)S(1)}, u32[]{:S(2)}, u32[]{:S(2)}) collective-permute-start(f32[51,2,128]{2,1,0:T(2,128)S(1)} %get-tuple-element.18), channel_id=1, source_target_pairs={{1,2},{2,1},{3,0},{0,3},{5,6},{6,5},{7,4},{4,7},{9,10},{10,9},{11,... | collective-permute-start | bytes 156680 | tf_op jit(solution)/shard_map/ppermute | solution.py:419
  13.4 1.5 %collective-permute-done.4.refs_2_.refs_0_ = bf16[4,64,128]{2,1,0:T(8,128)(2,1)S(1)} collective-permute-done((bf16[4,64,128]{2,1,0:T(8,128)(2,1)S(1)}, bf16[4,64,128]{2,1,0:T(8,128)(2,1)S(1)}, u32[]{:S(2)}, u32[]{:S(2)}) %collective-permute-start.4) | collective-permute-done | bytes 65568 | tf_op jit(solution)/shard_map/ppermute | solution.py:423
  14.9 1.6 %collective-permute-start.10 = (bf16[4,56,128]{2,1,0:T(8,128)(2,1)S(1)}, bf16[4,56,128]{2,1,0:T(8,128)(2,1)S(1)}, u32[]{:S(2)}, u32[]{:S(2)}) collective-permute-start(bf16[4,56,128]{2,1,0:T(8,128)(2,1)S(1)} %shard_map.160), channel_id=1, source_target_pairs={{1,2},{2,1},{3,0},{0,3},{5,6},{6,5},{7,4},{4,7},{9,10},{10,9},{11,... | collective-permute-start | bytes 172040 | tf_op jit(solution)/shard_map/ppermute | solution.py:419
  16.5 0.0 collective-permute-done.5.refs_3_.refs_1_
  16.5 0.0 copy-start.4
  16.5 0.0 copy-start.5
  16.6 0.1 collective-permute-start.6
  16.7 0.0 collective-permute-done.9.refs_2_.refs_12_
  16.7 0.0 collective-permute-done.7.refs_3_.refs_8_
  16.7 0.7 %collective-permute-start.11 = (bf16[8,56,128]{2,1,0:T(8,128)(2,1)S(1)}, bf16[8,56,128]{2,1,0:T(8,128)(2,1)S(1)}, u32[]{:S(2)}, u32[]{:S(2)}) collective-permute-start(bf16[8,56,128]{2,1,0:T(8,128)(2,1)S(1)} %shard_map.161), channel_id=1, source_target_pairs={{1,2},{2,1},{3,0},{0,3},{5,6},{6,5},{7,4},{4,7},{9,10},{10,9},{11,... | collective-permute-start | bytes 344072 | tf_op jit(solution)/shard_map/ppermute | solution.py:419
  17.4 0.0 collective-permute-done.3.refs_4_
  17.4 1.3 %collective-permute-start.8 = (bf16[3,128,128]{2,1,0:T(8,128)(2,1)S(1)}, bf16[3,128,128]{2,1,0:T(8,128)(2,1)S(1)}, u32[]{:S(2)}, u32[]{:S(2)}) collective-permute-start(bf16[3,128,128]{2,1,0:T(8,128)(2,1)S(1)} %slice.46), channel_id=1, source_target_pairs={{0,16},{16,0},{1,17},{17,1},{2,18},{18,2},{3,19},{19,3},{4,20},{20... | collective-permute-start | bytes 294920 | tf_op jit(solution)/shard_map/ppermute | solution.py:458
  18.7 1.4 %shard_map.157 = (f32[3,16,8,128]{3,2,1,0:T(8,128)S(1)}, f32[8,128]{1,0:T(8,128)S(1)}, f32[8,3,14,8,128]{4,3,2,1,0:T(8,128)S(1)}, bf16[12,16,16,128]{3,2,1,0:T(8...) custom-call(s32[8,8]{1,0:T(8,128)S(1)} %pad_add_fusion.refs_0_, ...), custom_call_target="tpu_custom_call" | custom-call | tf_op jit(solution)/shard_map/pallas_call | solution.py:386
  20.2 1.5 %collective-permute-done.8.refs_9_ = bf16[3,128,128]{2,1,0:T(8,128)(2,1)S(1)} collective-permute-done((bf16[3,128,128]{2,1,0:T(8,128)(2,1)S(1)}, bf16[3,128,128]{2,1,0:T(8,128)(2,1)S(1)}, u32[]{:S(2)}, u32[]{:S(2)}) %collective-permute-start.8) | collective-permute-done | bytes 98336 | tf_op jit(solution)/shard_map/ppermute | solution.py:458
  21.7 0.6 %collective-permute-done.11.refs_14_ = bf16[8,56,128]{2,1,0:T(8,128)(2,1)S(1)} collective-permute-done((bf16[8,56,128]{2,1,0:T(8,128)(2,1)S(1)}, bf16[8,56,128]{2,1,0:T(8,128)(2,1)S(1)}, u32[]{:S(2)}, u32[]{:S(2)}) %collective-permute-start.11) | collective-permute-done | bytes 114720 | tf_op jit(solution)/shard_map/ppermute | solution.py:419
  22.3 0.0 copy-start.10
  22.3 2.5 %shard_map.162 = (bf16[4,12,16,128]{3,2,1,0:T(8,128)(2,1)S(1)}, bf16[36,16,128]{2,1,0:T(8,128)(2,1)S(1)}, bf16[2,768,256]{2,1,0:T(8,128)(2,1)S(1)}, bf16[4,256,128]{2,1,0:T(8,128)(2,1)S(1)}) custom-call(bf16[256,256]{1,0:T(8,128)(2,1)S(1)} %copy-done.1, f32[3,16,8,128]{3,2,1,0:T(8,128)S(1)} %get-tuple-element.20.refs_1_, ...), custom_call_target="tpu_custom_call" | custom-call | tf_op jit(solution)/shard_map/pallas_call | solution.py:386
  24.8 0.5 %collective-permute-start.12 = (bf16[4,12,16,128]{3,2,1,0:T(8,128)(2,1)S(1)}, bf16[4,12,16,128]{3,2,1,0:T(8,128)(2,1)S(1)}, u32[]{:S(2)}, u32[]{:S(2)}) collective-permute-start(bf16[4,12,16,128]{3,2,1,0:T(8,128)(2,1)S(1)} %get-tuple-element.29.refs_10_), channel_id=1, source_target_pairs={{0,1},{1,0},{2,3},{3,2},{4,5},{5,4},{6,7},{7,6},{8,9},{9,8},{10,11... | collective-permute-start | bytes 589832 | tf_op jit(solution)/shard_map/ppermute | solution.py:416
  25.3 1.2 %collective-permute-start.13 = (bf16[36,16,128]{2,1,0:T(8,128)(2,1)S(1)}, bf16[36,16,128]{2,1,0:T(8,128)(2,1)S(1)}, u32[]{:S(2)}, u32[]{:S(2)}) collective-permute-start(bf16[36,16,128]{2,1,0:T(8,128)(2,1)S(1)} %get-tuple-element.30), channel_id=1, source_target_pairs={{1,2},{2,1},{3,0},{0,3},{5,6},{6,5},{7,4},{4,7},{9,10},{10,9},{11,... | collective-permute-start | bytes 442376 | tf_op jit(solution)/shard_map/ppermute | solution.py:419
  26.5 4.4 %collective-permute-done.13.refs_12_ = bf16[36,16,128]{2,1,0:T(8,128)(2,1)S(1)} collective-permute-done((bf16[36,16,128]{2,1,0:T(8,128)(2,1)S(1)}, bf16[36,16,128]{2,1,0:T(8,128)(2,1)S(1)}, u32[]{:S(2)}, u32[]{:S(2)}) %collective-permute-start.13) | collective-permute-done | bytes 147488 | tf_op jit(solution)/shard_map/ppermute | solution.py:419
  30.8 0.0 copy-start.3
  30.9 1.9 %shard_map.163 = bf16[2,8,32,128]{3,2,1,0:T(8,128)(2,1)S(1)} custom-call(bf16[256,256]{1,0:T(8,128)(2,1)S(1)} %copy-done.2, f32[3,16,8,128]{3,2,1,0:T(8,128)S(1)} %get-tuple-element.20.refs_1_, f32[8,128]{1,0:T(8,128)S(1)} %get-tuple-element.21.refs_2_, f32[8,3,14,8,128]{4,3,2,1,0:T(8,128)S(1)} %get-tuple-element.22.refs_3_, ...), custom_call_target="tpu_custom_call" | custom-call | tf_op jit(solution)/shard_map/pallas_call | solution.py:386
  32.8 0.2 collective-permute-start.14
  33.0 1.1 %collective-permute-done.14 = bf16[8,32,128]{2,1,0:T(8,128)(2,1)S(1)} collective-permute-done((bf16[8,32,128]{2,1,0:T(8,128)(2,1)S(1)}, bf16[8,32,128]{2,1,0:T(8,128)(2,1)S(1)}, u32[]{:S(2)}, u32[]{:S(2)}) %collective-permute-start.14) | collective-permute-done | bytes 65568 | tf_op jit(solution)/shard_map/ppermute | solution.py:416
  34.2 3.0 %collective-permute-start.15 = (bf16[2,4,32,128]{3,2,1,0:T(8,128)(2,1)S(1)}, bf16[2,4,32,128]{3,2,1,0:T(8,128)(2,1)S(1)}, u32[]{:S(2)}, u32[]{:S(2)}) collective-permute-start(bf16[2,4,32,128]{3,2,1,0:T(8,128)(2,1)S(1)} %pad_maximum_fusion.1), channel_id=1, source_target_pairs={{0,0},{1,4},{4,1},{5,5},{8,8},{9,12},{12,9},{13,13},{2,2},{3,6},{6... | collective-permute-start | bytes 196616 | tf_op jit(solution)/shard_map/ppermute | solution.py:590
  37.2 2.9 %collective-permute-start.16 = (bf16[2,4,32,128]{3,2,1,0:T(8,128)(2,1)S(1)}, bf16[2,4,32,128]{3,2,1,0:T(8,128)(2,1)S(1)}, u32[]{:S(2)}, u32[]{:S(2)}) collective-permute-start(bf16[2,4,32,128]{3,2,1,0:T(8,128)(2,1)S(1)} %pad_maximum_fusion.2), channel_id=1, source_target_pairs={{0,8},{1,12},{4,9},{5,13},{8,0},{9,4},{12,1},{13,5},{2,10},{3,14},... | collective-permute-start | bytes 196616 | tf_op jit(solution)/shard_map/ppermute | solution.py:590
  40.1 0.1 collective-permute-done.15.refs_1_
  40.3 2.5 %collective-permute-done.16.refs_2_ = bf16[2,4,32,128]{3,2,1,0:T(8,128)(2,1)S(1)} collective-permute-done((bf16[2,4,32,128]{3,2,1,0:T(8,128)(2,1)S(1)}, bf16[2,4,32,128]{3,2,1,0:T(8,128)(2,1)S(1)}, u32[]{:S(2)}, u32[]{:S(2)}) %collective-permute-start.16) | collective-permute-done | bytes 65568 | tf_op jit(solution)/shard_map/ppermute | solution.py:590
  42.8 0.9 %shard_map.164 = f32[4,16,8,128]{3,2,1,0:T(8,128)} custom-call(bf16[256,256]{1,0:T(8,128)(2,1)S(1)} %copy-done.3, bf16[2,4,32,128]{3,2,1,0:T(8,128)(2,1)S(1)} %collective-permute-done.15.refs_1_, bf16[2,4,32,128]{3,2,1,0:T(8,128)(2,1)S(1)} %collective-permute-done.16.refs_2_), custom_call_target="tpu_custom_call" | custom-call | tf_op jit(solution)/shard_map/pallas_call | solution.py:386
  (43 shorter events, 0.3 us)
Async XLA Ops:
  0.0 5.0 %copy-start.12 = (s32[8,4]{0,1:T(4,128)S(1)}, s32[8,4]{0,1:T(4,128)}, u32[]{:S(2)}) copy-start(s32[8,4]{0,1:T(4,128)} %param.22) | copy-start | bytes 388
  1.0 8.5 %copy-start.7 = (f32[16,8,128]{2,1,0:T(8,128)S(1)}, f32[16,8,128]{2,1,0:T(8,128)}, u32[]{:S(2)}) copy-start(f32[16,8,128]{2,1,0:T(8,128)} %start.1) | copy-start | bytes 196612
  1.0 8.5 %copy-start.8 = (f32[16,8,128]{2,1,0:T(8,128)S(1)}, f32[16,8,128]{2,1,0:T(8,128)}, u32[]{:S(2)}) copy-start(f32[16,8,128]{2,1,0:T(8,128)} %reaction.1) | copy-start | bytes 196612
  1.0 8.5 %copy-start.9 = (f32[16,8,128]{2,1,0:T(8,128)S(1)}, f32[16,8,128]{2,1,0:T(8,128)}, u32[]{:S(2)}) copy-start(f32[16,8,128]{2,1,0:T(8,128)} %source.1) | copy-start | bytes 196612
  1.1 3.9 %collective-permute-start = (bf16[4,64,128]{2,1,0:T(8,128)(2,1)S(1)}, bf16[4,64,128]{2,1,0:T(8,128)(2,1)S(1)}, u32[]{:S(2)}, u32[]{:S(2)}) collective-permute-start(bf16[4,64,128]{2,1,0:T(8,128)(2,1)S(1)} %bitcast.23), channel_id=1, source_target_pairs={{0,1},{1,0},{2,3},{3,2},{4,5},{5,4},{6,7},{7,6},{8,9},{9,8},{10,11... | collective-permute-start | bytes 196616 | tf_op jit(solution)/shard_map/ppermute | solution.py:416
  1.2 10.6 %copy-start.13 = (s32[4]{0:T(128)S(1)}, s32[4]{0:T(128)}, u32[]{:S(2)}) copy-start(s32[4]{0:T(128)} %constant.125.clone) | copy-start | bytes 52
  1.2 11.6 %copy-start.11 = (f32[8,128]{1,0:T(8,128)S(1)}, f32[8,128]{1,0:T(8,128)}, u32[]{:S(2)}) copy-start(f32[8,128]{1,0:T(8,128)} %refs_5_.1) | copy-start | bytes 12292
  2.3 14.3 %collective-permute-start.7 = (bf16[11,128,128]{2,1,0:T(8,128)(2,1)S(1)}, bf16[11,128,128]{2,1,0:T(8,128)(2,1)S(1)}, u32[]{:S(2)}, u32[]{:S(2)}) collective-permute-start(bf16[11,128,128]{2,1,0:T(8,128)(2,1)S(1)} %shard_map.158), channel_id=1, source_target_pairs={{1,2},{2,1},{3,0},{0,3},{5,6},{6,5},{7,4},{4,7},{9,10},{10,9},{11,... | collective-permute-start | bytes 1081352 | tf_op jit(solution)/shard_map/ppermute | solution.py:419
  5.0 13.7 %copy-start = (bf16[8,7,128,128]{3,2,1,0:T(8,128)(2,1)S(1)}, bf16[8,7,128,128]{3,2,1,0:T(8,128)(2,1)}, u32[]{:S(2)}) copy-start(bf16[8,7,128,128]{3,2,1,0:T(8,128)(2,1)} %refs_2_.3) | copy-start | bytes 5505028
  5.0 13.7 %copy-start.1 = (bf16[256,256]{1,0:T(8,128)(2,1)S(1)}, bf16[256,256]{1,0:T(8,128)(2,1)}, u32[]{:S(2)}) copy-start(bf16[256,256]{1,0:T(8,128)(2,1)} %constant.126.clone.refs_1_.refs_0_) | copy-start | bytes 393220
  5.1 5.1 %collective-permute-start.2 = (bf16[4,64,128]{2,1,0:T(8,128)(2,1)S(1)}, bf16[4,64,128]{2,1,0:T(8,128)(2,1)S(1)}, u32[]{:S(2)}, u32[]{:S(2)}) collective-permute-start(bf16[4,64,128]{2,1,0:T(8,128)(2,1)S(1)} %get-tuple-element.33), channel_id=1, source_target_pairs={{0,12},{4,8},{8,4},{12,0},{1,13},{5,9},{9,5},{13,1},{2,14},{6,10},... | collective-permute-start | bytes 196616 | tf_op jit(solution)/shard_map/ppermute | solution.py:423
  8.5 8.1 %collective-permute-start.9 = (bf16[4,56,128]{2,1,0:T(8,128)(2,1)S(1)}, bf16[4,56,128]{2,1,0:T(8,128)(2,1)S(1)}, u32[]{:S(2)}, u32[]{:S(2)}) collective-permute-start(bf16[4,56,128]{2,1,0:T(8,128)(2,1)S(1)} %shard_map.159), channel_id=1, source_target_pairs={{1,2},{2,1},{3,0},{0,3},{5,6},{6,5},{7,4},{4,7},{9,10},{10,9},{11,... | collective-permute-start | bytes 172040 | tf_op jit(solution)/shard_map/ppermute | solution.py:419
  9.5 5.4 %collective-permute-start.4 = (bf16[4,64,128]{2,1,0:T(8,128)(2,1)S(1)}, bf16[4,64,128]{2,1,0:T(8,128)(2,1)S(1)}, u32[]{:S(2)}, u32[]{:S(2)}) collective-permute-start(bf16[4,64,128]{2,1,0:T(8,128)(2,1)S(1)} %get-tuple-element.31), channel_id=1, source_target_pairs={{0,8},{4,12},{8,0},{12,4},{1,9},{5,13},{9,1},{13,5},{2,10},{6,14},... | collective-permute-start | bytes 196616 | tf_op jit(solution)/shard_map/ppermute | solution.py:423
  9.5 7.0 %collective-permute-start.5 = (bf16[4,64,128]{2,1,0:T(8,128)(2,1)S(1)}, bf16[4,64,128]{2,1,0:T(8,128)(2,1)S(1)}, u32[]{:S(2)}, u32[]{:S(2)}) collective-permute-start(bf16[4,64,128]{2,1,0:T(8,128)(2,1)S(1)} %get-tuple-element.34._), channel_id=1, source_target_pairs={{0,4},{4,0},{8,12},{12,8},{1,5},{5,1},{9,13},{13,9},{2,6},{6,2},{1... | collective-permute-start | bytes 196616 | tf_op jit(solution)/shard_map/ppermute | solution.py:423
  10.2 2.6 %collective-permute-start.1 = (f32[3,16,8,128]{3,2,1,0:T(8,128)S(1)}, f32[3,16,8,128]{3,2,1,0:T(8,128)S(1)}, u32[]{:S(2)}, u32[]{:S(2)}) collective-permute-start(f32[3,16,8,128]{3,2,1,0:T(8,128)S(1)} %shard_map.154.refs_0_), channel_id=1, source_target_pairs={{0,1},{1,0},{2,3},{3,2},{4,5},{5,4},{6,7},{7,6},{8,9},{9,8},{10,11... | collective-permute-start | bytes 589832 | tf_op jit(solution)/shard_map/ppermute | solution.py:416
  13.0 4.4 %collective-permute-start.3 = (f32[51,2,128]{2,1,0:T(2,128)S(1)}, f32[51,2,128]{2,1,0:T(2,128)S(1)}, u32[]{:S(2)}, u32[]{:S(2)}) collective-permute-start(f32[51,2,128]{2,1,0:T(2,128)S(1)} %get-tuple-element.18), channel_id=1, source_target_pairs={{1,2},{2,1},{3,0},{0,3},{5,6},{6,5},{7,4},{4,7},{9,10},{10,9},{11,... | collective-permute-start | bytes 156680 | tf_op jit(solution)/shard_map/ppermute | solution.py:419
  14.9 5.3 %collective-permute-start.10 = (bf16[4,56,128]{2,1,0:T(8,128)(2,1)S(1)}, bf16[4,56,128]{2,1,0:T(8,128)(2,1)S(1)}, u32[]{:S(2)}, u32[]{:S(2)}) collective-permute-start(bf16[4,56,128]{2,1,0:T(8,128)(2,1)S(1)} %shard_map.160), channel_id=1, source_target_pairs={{1,2},{2,1},{3,0},{0,3},{5,6},{6,5},{7,4},{4,7},{9,10},{10,9},{11,... | collective-permute-start | bytes 172040 | tf_op jit(solution)/shard_map/ppermute | solution.py:419
  16.5 5.8 %copy-start.4 = (bf16[224,224]{1,0:T(8,128)(2,1)S(1)}, bf16[224,224]{1,0:T(8,128)(2,1)}, u32[]{:S(2)}) copy-start(bf16[224,224]{1,0:T(8,128)(2,1)} %constant.127.clone.refs_10_) | copy-start | bytes 301060
  16.5 5.7 %copy-start.5 = (bf16[192,192]{1,0:T(8,128)(2,1)S(1)}, bf16[192,192]{1,0:T(8,128)(2,1)}, u32[]{:S(2)}) copy-start(bf16[192,192]{1,0:T(8,128)(2,1)} %constant.128.clone.refs_11_) | copy-start | bytes 221188
  16.6 2.2 %collective-permute-start.6 = (bf16[16,64,128]{2,1,0:T(8,128)(2,1)S(1)}, bf16[16,64,128]{2,1,0:T(8,128)(2,1)S(1)}, u32[]{:S(2)}, u32[]{:S(2)}) collective-permute-start(bf16[16,64,128]{2,1,0:T(8,128)(2,1)S(1)} %shard_map.156.refs_6_), channel_id=1, source_target_pairs={{0,1},{1,0},{2,3},{3,2},{4,5},{5,4},{6,7},{7,6},{8,9},{9,8},{10,11... | collective-permute-start | bytes 786440 | tf_op jit(solution)/shard_map/ppermute | solution.py:416
  16.7 5.6 %collective-permute-start.11 = (bf16[8,56,128]{2,1,0:T(8,128)(2,1)S(1)}, bf16[8,56,128]{2,1,0:T(8,128)(2,1)S(1)}, u32[]{:S(2)}, u32[]{:S(2)}) collective-permute-start(bf16[8,56,128]{2,1,0:T(8,128)(2,1)S(1)} %shard_map.161), channel_id=1, source_target_pairs={{1,2},{2,1},{3,0},{0,3},{5,6},{6,5},{7,4},{4,7},{9,10},{10,9},{11,... | collective-permute-start | bytes 344072 | tf_op jit(solution)/shard_map/ppermute | solution.py:419
  17.4 4.3 %collective-permute-start.8 = (bf16[3,128,128]{2,1,0:T(8,128)(2,1)S(1)}, bf16[3,128,128]{2,1,0:T(8,128)(2,1)S(1)}, u32[]{:S(2)}, u32[]{:S(2)}) collective-permute-start(bf16[3,128,128]{2,1,0:T(8,128)(2,1)S(1)} %slice.46), channel_id=1, source_target_pairs={{0,16},{16,0},{1,17},{17,1},{2,18},{18,2},{3,19},{19,3},{4,20},{20... | collective-permute-start | bytes 294920 | tf_op jit(solution)/shard_map/ppermute | solution.py:458
  22.3 8.5 %copy-start.2 = (bf16[256,256]{1,0:T(8,128)(2,1)S(1)}, bf16[256,256]{1,0:T(8,128)(2,1)}, u32[]{:S(2)}) copy-start(bf16[256,256]{1,0:T(8,128)(2,1)} %constant.129.clone.refs_0_) | copy-start | bytes 393220
  22.3 8.5 %copy-start.6 = (bf16[160,160]{1,0:T(8,128)(2,1)S(1)}, bf16[160,160]{1,0:T(8,128)(2,1)}, u32[]{:S(2)}) copy-start(bf16[160,160]{1,0:T(8,128)(2,1)} %constant.130.clone.refs_8_) | copy-start | bytes 153604
  22.3 8.5 %copy-start.10 = (bf16[128,128]{1,0:T(8,128)(2,1)S(1)}, bf16[128,128]{1,0:T(8,128)(2,1)}, u32[]{:S(2)}) copy-start(bf16[128,128]{1,0:T(8,128)(2,1)} %constant.131.clone.refs_9_) | copy-start | bytes 98308
  24.8 6.0 %collective-permute-start.12 = (bf16[4,12,16,128]{3,2,1,0:T(8,128)(2,1)S(1)}, bf16[4,12,16,128]{3,2,1,0:T(8,128)(2,1)S(1)}, u32[]{:S(2)}, u32[]{:S(2)}) collective-permute-start(bf16[4,12,16,128]{3,2,1,0:T(8,128)(2,1)S(1)} %get-tuple-element.29.refs_10_), channel_id=1, source_target_pairs={{0,1},{1,0},{2,3},{3,2},{4,5},{5,4},{6,7},{7,6},{8,9},{9,8},{10,11... | collective-permute-start | bytes 589832 | tf_op jit(solution)/shard_map/ppermute | solution.py:416
  25.3 5.5 %collective-permute-start.13 = (bf16[36,16,128]{2,1,0:T(8,128)(2,1)S(1)}, bf16[36,16,128]{2,1,0:T(8,128)(2,1)S(1)}, u32[]{:S(2)}, u32[]{:S(2)}) collective-permute-start(bf16[36,16,128]{2,1,0:T(8,128)(2,1)S(1)} %get-tuple-element.30), channel_id=1, source_target_pairs={{1,2},{2,1},{3,0},{0,3},{5,6},{6,5},{7,4},{4,7},{9,10},{10,9},{11,... | collective-permute-start | bytes 442376 | tf_op jit(solution)/shard_map/ppermute | solution.py:419
  30.8 11.9 %copy-start.3 = (bf16[256,256]{1,0:T(8,128)(2,1)S(1)}, bf16[256,256]{1,0:T(8,128)(2,1)}, u32[]{:S(2)}) copy-start(bf16[256,256]{1,0:T(8,128)(2,1)} %constant.132.clone.refs_0_) | copy-start | bytes 393220
  32.8 1.3 %collective-permute-start.14 = (bf16[8,32,128]{2,1,0:T(8,128)(2,1)S(1)}, bf16[8,32,128]{2,1,0:T(8,128)(2,1)S(1)}, u32[]{:S(2)}, u32[]{:S(2)}) collective-permute-start(bf16[8,32,128]{2,1,0:T(8,128)(2,1)S(1)} %slice_bitcast_fusion), channel_id=1, source_target_pairs={{0,1},{1,0},{2,3},{3,2},{4,5},{5,4},{6,7},{7,6},{8,9},{9,8},{10,11... | collective-permute-start | bytes 196616 | tf_op jit(solution)/shard_map/ppermute | solution.py:416
  34.2 6.1 %collective-permute-start.15 = (bf16[2,4,32,128]{3,2,1,0:T(8,128)(2,1)S(1)}, bf16[2,4,32,128]{3,2,1,0:T(8,128)(2,1)S(1)}, u32[]{:S(2)}, u32[]{:S(2)}) collective-permute-start(bf16[2,4,32,128]{3,2,1,0:T(8,128)(2,1)S(1)} %pad_maximum_fusion.1), channel_id=1, source_target_pairs={{0,0},{1,4},{4,1},{5,5},{8,8},{9,12},{12,9},{13,13},{2,2},{3,6},{6... | collective-permute-start | bytes 196616 | tf_op jit(solution)/shard_map/ppermute | solution.py:590
  37.2 5.6 %collective-permute-start.16 = (bf16[2,4,32,128]{3,2,1,0:T(8,128)(2,1)S(1)}, bf16[2,4,32,128]{3,2,1,0:T(8,128)(2,1)S(1)}, u32[]{:S(2)}, u32[]{:S(2)}) collective-permute-start(bf16[2,4,32,128]{3,2,1,0:T(8,128)(2,1)S(1)} %pad_maximum_fusion.2), channel_id=1, source_target_pairs={{0,8},{1,12},{4,9},{5,13},{8,0},{9,4},{12,1},{13,5},{2,10},{3,14},... | collective-permute-start | bytes 196616 | tf_op jit(solution)/shard_map/ppermute | solution.py:590
